TPU v7x, 256 devices: a whole 4x4x8 slice. The times are simulated.
256 devices in a mesh: row: 64 (over x, y, z_hi, core), rep: 4 (over z_lo).
Axes of the slice: x: 4, y: 4, z: 8 (z_hi: 2, z_lo: 4; z = z_hi * 4 + z_lo), core: 2. Of those that a mesh axis runs over, the one named last changes fastest.
Arguments:
- features: float32 [32768, 128], P(('row', 'rep')), may hold values from -6 to 6
- tiles: float32 [256, 4, 8, 128, 128], P('row', 'rep'), may hold values from -0.15625 to 0.15625
- columns: int32 [256, 4, 8], P('row', 'rep'), may hold values from 0 to 63, as said below
- counts: int32 [256, 4], P('row', 'rep'), may hold values from 1 to 8, as said below
- self_one: float32 [128, 256], replicated, may hold values from -0.5 to 0.5
- neigh_one: float32 [128, 256], replicated, may hold values from -0.5 to 0.5
- bias_one: float32 [256], replicated, may hold values from -3 to 3
- self_two: float32 [256, 172], replicated, may hold values from -0.375 to 0.375
- neigh_two: float32 [256, 172], replicated, may hold values from -0.375 to 0.375
- bias_two: float32 [172], replicated, may hold values from -3 to 3
- cotangent: float32 [32768, 172], P(('row', 'rep')), may hold values from -0.03314563 to 0.03314563
Outputs:
- logits: float32 [32768, 172], P(('row', 'rep'))
- grad_self_one: float32 [128, 256], replicated
- grad_neigh_one: float32 [128, 256], replicated
- grad_bias_one: float32 [256], replicated
- grad_self_two: float32 [256, 172], replicated
- grad_neigh_two: float32 [256, 172], replicated
- grad_bias_two: float32 [172], replicated
Inputs may be any that keep to these rules, and one draw needn't show every extreme that they name: `columns`: in each list the first 8 entries are distinct, and entry 0 of the lists of row block b is b // 4; only the first counts[b, j] entries are live. `counts`: A few groups of 4 consecutive row blocks hold far more live tiles than the others; 8 is reached in every draw.
All inputs are finite; a program needn't handle non-finite values.
Results may differ from a plain program's by a relative error of at most 0.0003.
Values sent between devices are 32-bit elements; how exact they have to be, the bound alone decides.
No kernel may reach another device: no remote copies, remote signals or barrier semaphores. Data moves between devices by JAX's collectives and lax.ppermute only.
A program may use at most 64 MiB of HBM per device.

v0:
```python
import functools

import jax
import jax.numpy as jnp
from jax import lax
from jax.experimental import pallas as pl
from jax.experimental.pallas import tpu as pltpu
from jax.sharding import PartitionSpec as P

NX, NY, NZ, NC, NR = 4, 4, 2, 2, 4
SIDE = 128
CLS = 172
CP = 176
GROWS = 1280
F32 = jnp.float32
VMEM = pl.BlockSpec(memory_space=pltpu.VMEM)
SMEM = pl.BlockSpec(memory_space=pltpu.SMEM)
ANY = pl.BlockSpec(memory_space=pl.ANY)
MIB = 1024 * 1024
COUNTS, ME, REP = 32, 36, 37


def row_perm(shift):
    pairs = []
    for x in range(NX):
        for y in range(NY):
            for z in range(NZ):
                for c in range(NC):
                    dx, dy, dz, dc = shift(c)
                    src = ((x * NY + y) * NZ + z) * NC + c
                    dst = (((x + dx) % NX * NY + (y + dy) % NY) * NZ + (z ^ dz)) * NC + (c ^ dc)
                    pairs.append((src, dst))
    return pairs


def send_core(a):
    return lax.ppermute(a, "row", row_perm(lambda c: (0, 0, 0, 1)))


def send_z(a):
    return lax.ppermute(a, "row", row_perm(lambda c: (0, 0, 1, 0)))


def send_plane(a, stage, d):
    return lax.ppermute(
        a, "row", row_perm(lambda c: (d, 0, 0, 0) if c == stage else (0, d, 0, 0))
    )


def send_rep(a, d):
    return lax.ppermute(a, "rep", [(j, (j + d) % NR) for j in range(NR)])


def swap_rep(a, bit):
    return lax.ppermute(a, "rep", [(j, j ^ bit) for j in range(NR)])


def split(a):
    hi = a.astype(jnp.bfloat16)
    lo = (a - hi.astype(F32)).astype(jnp.bfloat16)
    return hi, lo


def dot3(a, b, dims=((1,), (0,))):
    dn = (dims, ((), ()))
    ah, al = split(a)
    bh, bl = split(b)
    mm = lambda p, q: lax.dot_general(p, q, dn, preferred_element_type=F32)
    return mm(ah, bh) + (mm(ah, bl) + mm(al, bh))


def wide(a):
    return jnp.concatenate(split(a), axis=1)


def twice(a):
    w = wide(a)
    return jnp.concatenate([w, w], axis=0)


def twice_t(a):
    h, l = split(a)
    return jnp.concatenate(
        [jnp.concatenate([h, h], axis=1), jnp.concatenate([l, l], axis=1)], axis=0
    )


def fold(a):
    return a[:, :SIDE] + a[:, SIDE:]


def relative(c, me):
    diff = c ^ me
    dx = ((c >> 4) - (me >> 4)) & 3
    dy = ((c >> 2) - (me >> 2)) & 3
    core = c & 1
    d1 = jnp.where(core == 0, dx, dy)
    d2 = jnp.where(core == 0, dy, dx)
    return d1, d2, (diff >> 1) & 1, diff & 1


def live_tile(tile_buf, meta, block, s):
    t = tile_buf[block, 0, s]
    return jnp.where(s < meta[COUNTS + block], t, jnp.zeros_like(t))


def start_loads(refs, buf, tiles, tile_buf, sems):
    copies = [pltpu.make_async_copy(tiles, tile_buf, sems.at[len(refs)])]
    start = 0
    for k, ref in enumerate(refs):
        size = ref.shape[0]
        copies.append(pltpu.make_async_copy(ref, buf.at[pl.ds(start, size)], sems.at[k]))
        start += size
    for c in copies:
        c.start()
    for c in copies:
        c.wait()


def agg_kernel(second, meta, tiles, *rest):
    refs, outs, (buf, tile_buf, sems) = rest[:6], rest[6:10], rest[10:]
    me, rep = meta[ME], meta[REP]
    start_loads(refs, buf, tiles, tile_buf, sems)
    rows = buf.shape[1]
    for d in range(NR):
        block = (rep + d) & 3

        def step(i, acc, block=block):
            for u in range(2):
                s = 2 * i + u
                d1, d2, dz, dc = relative(meta[block * 8 + s], me)
                piece = buf[((dc * 4 + d2) * 4 + d1) * 2 + dz]
                tile = live_tile(tile_buf, meta, block, s)
                if second:
                    dn = (((1,), (1,)), ((), ()))
                    acc += lax.dot_general(
                        wide(piece), twice_t(tile), dn, preferred_element_type=F32
                    )
                else:
                    acc += jnp.dot(wide(tile), twice(piece), preferred_element_type=F32)
            return acc

        pairs = (meta[COUNTS + block] + 1) >> 1
        outs[d][...] = fold(lax.fori_loop(0, pairs, step, jnp.zeros((rows, 256), F32)))


def transposed_kernel(meta, tiles, ct0, ct1, ct2, ct3, own, oth, tile_buf, ct_buf, sem):
    me, rep = meta[ME], meta[REP]
    copy = pltpu.make_async_copy(tiles, tile_buf, sem)
    copy.start()
    for o in (own, oth):
        o[...] = jnp.zeros(o.shape, F32)
    copy.wait()
    for d, ct in enumerate((ct0, ct1, ct2, ct3)):
        block = (rep + d) & 3
        ct_buf[...] = jnp.concatenate(
            [wide(ct[...]), jnp.zeros((CP - CLS, 256), jnp.bfloat16)], axis=0
        )

        def step(i, _, block=block):
            done = []
            for u in range(2):
                s = 2 * i + u
                tile = live_tile(tile_buf, meta, block, s)
                done.append(
                    (s, fold(jnp.dot(ct_buf[...], twice(tile), preferred_element_type=F32)))
                )
            for s, r in done:
                d1, d2, dz, dc = relative(meta[block * 8 + s], me)
                at = (d1 * 4 + d2) * 2 + dz

                @pl.when(dc == 0)
                def _():
                    own[at] += r

                @pl.when(dc != 0)
                def _():
                    oth[at] += r

            return 0

        lax.fori_loop(0, (meta[COUNTS + block] + 1) >> 1, step, 0)


def hidden_kernel(a0, a1, a2, a3, feat, self_one, neigh_one, bias, nt, agg, pre, yt):
    total = (a0[...] + a1[...]) + (a2[...] + a3[...])
    agg[...] = total
    p = dot3(feat[...], self_one[...]) + dot3(total, neigh_one[...]) + bias[...]
    pre[...] = p
    h = p * jax.nn.sigmoid(p)
    yt[pl.ds(CP - 8, 8)] = jnp.zeros((8, SIDE), F32)
    yt[pl.ds(0, CLS)] = dot3(nt[...], h, ((1,), (1,)))


def grad_kernel(meta, g, gz, pre, agg, feat, ct, st, nt, bias_two, base, same, other, packed):
    p = pre[...]
    s = jax.nn.sigmoid(p)
    h = p * s
    base[...] = dot3(st[...], h, ((1,), (1,))) + jnp.broadcast_to(bias_two[...], (SIDE, CLS)).T
    gt = g[pl.ds(0, CLS)] + gz[pl.ds(0, CLS)]
    cot = ct[...].T
    gh = dot3(cot, st[...]) + dot3(gt.T, nt[...])
    gp = gh * s * (1.0 + p * (1.0 - s))
    bias_one_grad = jnp.sum(gp, axis=0, keepdims=True)
    bias_two_grad = jnp.sum(cot, axis=0, keepdims=True)

    def put(start, value):
        rows = value.shape[0]
        packed[pl.ds(start, rows)] = value[:, :SIDE]
        packed[pl.ds(608 + start, rows)] = value[:, SIDE:]

    for start in (424, 600, 1032, 1208):
        packed[pl.ds(start, 8)] = jnp.zeros((8, SIDE), F32)
    packed[pl.ds(1216, 64)] = jnp.zeros((64, SIDE), F32)
    put(0, dot3(feat[...].T, gp))
    put(128, dot3(agg[...].T, gp))
    put(256, dot3(ct[...], h))
    put(432, dot3(gt, h))
    packed[pl.ds(256 + CLS, 1)] = bias_one_grad[:, :SIDE]
    packed[pl.ds(608 + 256 + CLS, 1)] = bias_one_grad[:, SIDE:]
    packed[pl.ds(432 + CLS, 1)] = bias_two_grad[:, :SIDE]
    packed[pl.ds(608 + 432 + CLS, 1), : CLS - SIDE] = bias_two_grad[:, SIDE:]
    for slot, d, start in piece_order(meta):
        (same, other)[slot][d] = packed[pl.ds(start, 160)]


def piece_order(meta):
    for slot in range(2):
        for d in range(NR):
            start = (((meta[ME] & 1) ^ slot) * NR + (meta[REP] ^ d)) * 160
            yield slot, d, pl.multiple_of(start, 8)


def finish_kernel(meta, q, qo, gs1, gn1, gb1, gs2, gn2, gb2, packed):
    for slot, d, start in piece_order(meta):
        packed[pl.ds(start, 160)] = (q, qo)[slot][(0, 2, 1, 3)[d]]

    def take(start, rows):
        return jnp.concatenate(
            [packed[pl.ds(start, rows)], packed[pl.ds(608 + start, rows)]], axis=1
        )

    gs1[...] = take(0, 128)
    gn1[...] = take(128, 128)
    gs2[...] = take(256, CLS)
    gn2[...] = take(432, CLS)
    gb1[...] = take(256 + CLS, 1)
    gb2[...] = take(432 + CLS, 1)[:, :CLS]


def logits_kernel(z0, z1, z2, z3, base, out):
    total = (z0[...] + z1[...]) + (z2[...] + z3[...])
    out[...] = base[...] + total[:CLS]


def call(kernel, outs, ins, scratch=(), smem=0, in_any=(), mib=8, cost=6):
    specs = [SMEM] * smem + [VMEM] * (len(ins) - smem)
    for k in in_any:
        specs[k] = ANY
    return pl.pallas_call(
        kernel,
        out_shape=[jax.ShapeDtypeStruct(s, F32) for s in outs],
        in_specs=specs,
        out_specs=[VMEM] * len(outs),
        scratch_shapes=list(scratch),
        cost_estimate=pl.CostEstimate(flops=0, bytes_accessed=cost * MIB, transcendentals=0),
        compiler_params=pltpu.CompilerParams(vmem_limit_bytes=mib * MIB),
    )(*ins)


def after(a, *others):
    return lax.optimization_barrier((a, *others))[0]


def add4(a, b, c, d):
    return (a + b) + (c + d)


def gather_lane(block, swapped, *held):
    pair = after(jnp.stack([block, swapped]), *held)
    return jnp.concatenate([pair] + [send_plane(pair, 0, -d) for d in (1, 2, 3)])


def gather_plane(lane):
    return [lane] + [send_plane(lane, 1, -d) for d in (1, 2, 3)]


def gather_core(plane, *held):
    rest = jnp.concatenate([after(plane[1], *held)] + plane[2:])
    return plane + [send_core(plane[0]), send_core(rest)]


def scatter_core(own, oth):
    got = send_core(oth)
    return [own[8 * d : 8 * d + 8] + got[8 * d : 8 * d + 8] for d in range(4)]


def scatter_lane(parts, *held):
    return [parts[0]] + [send_plane(after(parts[d], *held), 0, d) for d in (1, 2, 3)]


def scatter_plane(q):
    q = add4(q[:2], *(send_plane(q[2 * d : 2 * d + 2], 1, d) for d in (1, 2, 3)))
    return q[0], send_z(q[1])


def reduce_reps(same, other):
    got = send_core(other)
    kept = jnp.stack([same[0] + got[0], same[2] + got[2]])
    kept = kept + swap_rep(jnp.stack([same[1] + got[1], same[3] + got[3]]), 1)
    q = kept[0] + swap_rep(kept[1], 2)
    return q + send_z(q)


def all_reduce(q, products, held):
    q = add4(after(q, products[0]), *(send_plane(q, 1, d) for d in (1, 2, 3)))
    q = after(q, held[1])
    q = after(jnp.stack([q, swap_rep(q, 2)]), *held[2:])
    q = jnp.concatenate([q, swap_rep(q, 1)])
    return q, send_core(q)


def agg(second, head, pieces):
    rows = pieces[0].shape[1]
    shape = (rows, SIDE)
    return call(
        functools.partial(agg_kernel, second), [shape] * 4, head + tuple(pieces),
        scratch=(
            pltpu.VMEM((64, rows, SIDE), F32),
            pltpu.VMEM((4, 1, 8, SIDE, SIDE), F32),
            pltpu.SemaphoreType.DMA((7,)),
        ),
        smem=1, in_any=range(1, 8), mib=16, cost=12,
    )


def sum_reps(parts, *held):
    return [parts[0]] + [send_rep(after(parts[d], *held), d) for d in (1, 2, 3)]


def shards(
    features,
    tiles,
    columns,
    counts,
    self_one,
    neigh_one,
    bias_one,
    self_two,
    neigh_two,
    bias_two,
    cotangent,
):
    place = jnp.stack([lax.axis_index("row"), lax.axis_index("rep")]).astype(jnp.int32)
    meta = jnp.concatenate([columns.reshape(-1), counts.reshape(-1), place])
    head = (meta, tiles)
    block = (SIDE, SIDE)
    tall, padded = (CLS, SIDE), (CP, SIDE)
    ct, st, nt = cotangent.T, self_two.T, neigh_two.T

    swapped = send_z(features)
    cts = [ct] + [after(send_rep(ct, -d), swapped) for d in (1, 2, 3)]
    lane = gather_lane(features, swapped)
    own, oth = call(
        transposed_kernel, [(32,) + padded] * 2, head + tuple(after(c, lane) for c in cts),
        scratch=(
            pltpu.VMEM((4, 1, 8, SIDE, SIDE), F32),
            pltpu.VMEM((CP, 256), jnp.bfloat16),
            pltpu.SemaphoreType.DMA(()),
        ),
        smem=1, in_any=(1,), mib=16, cost=12,
    )
    plane = gather_plane(lane)
    parts = scatter_core(own, oth)
    laned = scatter_lane(parts, *plane[1:])
    products = agg(False, head, gather_core(plane, *parts))
    q = add4(after(laned[0], products[0]), *laned[1:])

    sums, pre, yt = call(
        hidden_kernel, [block, (SIDE, 256), padded],
        (*sum_reps(products, q), features, self_one, neigh_one, bias_one.reshape(1, -1), nt),
    )
    g, gz = scatter_plane(q)
    plane = gather_plane(gather_lane(yt, send_z(yt), gz))
    base, same, other = call(
        grad_kernel, [tall, (4, 160, SIDE), (4, 160, SIDE)],
        (meta, g, gz, pre, sums, features, ct, st, nt, bias_two.reshape(1, -1)),
        scratch=(pltpu.VMEM((GROWS, SIDE), F32),), smem=1,
    )
    kept = reduce_reps(same, other)
    pieces = gather_core(plane, kept)
    kept = add4(kept, *(send_plane(kept, 0, d) for d in (1, 2, 3)))
    pieces[-1] = after(pieces[-1], kept)
    products = agg(True, head, pieces)
    parts = sum_reps(products)
    (logits,) = call(logits_kernel, [tall], (*parts, base))
    q, qo = all_reduce(kept, products, parts)
    gs1, gn1, gb1, gs2, gn2, gb2 = call(
        finish_kernel,
        [(128, 256), (128, 256), (1, 256), (CLS, 256), (CLS, 256), (1, CLS)],
        (meta, q, qo), scratch=(pltpu.VMEM((GROWS, SIDE), F32),), smem=1,
    )
    return logits.T, gs1, gn1, gb1.reshape(-1), gs2.T, gn2.T, gb2.reshape(-1)


def solution(mesh):
    return jax.shard_map(
        shards,
        mesh=mesh,
        in_specs=(
            P(("row", "rep"), None),
            P("row", "rep", None, None, None),
            P("row", "rep", None),
            P("row", "rep"),
            P(),
            P(),
            P(),
            P(),
            P(),
            P(),
            P(("row", "rep"), None),
        ),
        out_specs=(P(("row", "rep"), None), P(), P(), P(), P(), P(), P()),
        check_vma=False,
    )
```

profile of v0, /device:TPU:1, one launch (start us, length us, event | category | flops | bytes accessed | tf_op | source)
XLA Modules:
  0.0 178.0 jit_solution(6819629959686339619)
XLA Ops:
  0.6 7.8 %collective-permute-start = (f32[128,128]{1,0:T(8,128)}, f32[128,128]{1,0:T(8,128)S(1)}, u32[]{:S(2)}, u32[]{:S(2)}) collective-permute-start(f32[128,128]{1,0:T(8,128)} %feat.3), channel_id=1, source_target_pairs={{0,8},{4,12},{8,0},{12,4},{16,24},{20,28},{24,16},{28,20},{32,40},... | collective-permute-start | bytes 196616 | tf_op jit(solution)/shard_map/ppermute | solution.py:41
  8.5 1.6 collective-permute-start.8
  10.4 0.8 pad_maximum_fusion.6
  11.3 2.8 %collective-permute-start.1 = (f32[2,128,128]{2,1,0:T(8,128)S(1)}, f32[2,128,128]{2,1,0:T(8,128)S(1)}, u32[]{:S(2)}, u32[]{:S(2)}) collective-permute-start(f32[2,128,128]{2,1,0:T(8,128)S(1)} %pad_maximum_fusion.6), channel_id=1, source_target_pairs={{0,192},{4,52},{8,200},{12,60},{16,208},{20,4},{24,216},{28,12},{3... | collective-permute-start | bytes 393224 | tf_op jit(solution)/shard_map/ppermute | solution.py:45
  15.1 1.4 collective-permute-start.9
  17.0 1.3 reduce.3
  18.4 1.7 collective-permute-start.10
  20.2 0.7 pad_add_fusion.meta
  20.9 3.5 %collective-permute-done.10.ct3 = f32[172,128]{1,0:T(8,128)S(1)} collective-permute-done((f32[172,128]{1,0:T(8,128)}, f32[172,128]{1,0:T(8,128)S(1)}, u32[]{:S(2)}, u32[]{:S(2)}) %collective-permute-start.10) | collective-permute-done | bytes 88096 | tf_op jit(solution)/shard_map/ppermute | solution.py:51
  24.5 1.6 copy-done
  26.1 0.9 copy-done.4
  27.0 2.6 %shard_map.162 = (f32[32,176,128]{2,1,0:T(8,128)S(1)}, f32[32,176,128]{2,1,0:T(8,128)S(1)}) custom-call(s32[38]{0:T(128)S(1)} %pad_add_fusion.meta, f32[4,1,8,128,128]{4,3,2,1,0:T(8,128)S(1)} %copy-done, f32[172,128]{1,0:T(8,128)S(1)} %bitcast.35, f32[172,128]{1,0:T(8,128)S(1)} %collective-permute-done.8.ct1, f32[172,128]{1,0:T(8,128)S(1)} %collective-permute-done.9.ct2, ...), custom_call_target="tpu_custom_call" | custom-call | bytes 12582912 | tf_op jit(solution)/shard_map/pallas_call | solution.py:260
  29.6 6.5 %collective-permute-start.11 = (f32[32,176,128]{2,1,0:T(8,128)S(1)}, f32[32,176,128]{2,1,0:T(8,128)S(1)}, u32[]{:S(2)}, u32[]{:S(2)}) collective-permute-start(f32[32,176,128]{2,1,0:T(8,128)S(1)} %get-tuple-element.58), channel_id=1, source_target_pairs={{0,4},{4,0},{8,12},{12,8},{16,20},{20,16},{24,28},{28,24},{32,36},... | collective-permute-start | bytes 8650760 | tf_op jit(solution)/shard_map/ppermute | solution.py:37
  36.1 1.7 collective-permute-start.5
  37.9 0.9 collective-permute-start.6
  38.7 2.3 %collective-permute-done.11 = f32[32,176,128]{2,1,0:T(8,128)S(1)} collective-permute-done((f32[32,176,128]{2,1,0:T(8,128)S(1)}, f32[32,176,128]{2,1,0:T(8,128)S(1)}, u32[]{:S(2)}, u32[]{:S(2)}) %collective-permute-start.11) | collective-permute-done | bytes 2883616 | tf_op jit(solution)/shard_map/ppermute | solution.py:37
  41.4 3.0 %collective-permute-done.4.rest_1_ = f32[8,128,128]{2,1,0:T(8,128)S(1)} collective-permute-done((f32[8,128,128]{2,1,0:T(8,128)S(1)}, f32[8,128,128]{2,1,0:T(8,128)S(1)}, u32[]{:S(2)}, u32[]{:S(2)}) %collective-permute-start.4) | collective-permute-done | bytes 524320 | tf_op jit(solution)/shard_map/ppermute | solution.py:45
  44.4 1.6 collective-permute-done.5.rest_2_
  46.0 5.6 %collective-permute-done.6.rest_3_ = f32[8,128,128]{2,1,0:T(8,128)S(1)} collective-permute-done((f32[8,128,128]{2,1,0:T(8,128)S(1)}, f32[8,128,128]{2,1,0:T(8,128)S(1)}, u32[]{:S(2)}, u32[]{:S(2)}) %collective-permute-start.6) | collective-permute-done | bytes 524320 | tf_op jit(solution)/shard_map/ppermute | solution.py:45
  51.7 1.7 collective-permute-start.12
  53.5 0.9 collective-permute-start.13
  54.4 1.8 collective-permute-start.15
  56.1 1.6 collective-permute-start.14
  57.8 1.9 %collective-permute-done.7.rest_4_ = f32[8,128,128]{2,1,0:T(8,128)S(1)} collective-permute-done((f32[8,128,128]{2,1,0:T(8,128)S(1)}, f32[8,128,128]{2,1,0:T(8,128)S(1)}, u32[]{:S(2)}, u32[]{:S(2)}) %collective-permute-start.7) | collective-permute-done | bytes 524320 | tf_op jit(solution)/shard_map/ppermute | solution.py:37
  59.6 2.4 %shard_map.163 = (f32[128,128]{1,0:T(8,128)S(1)}, f32[128,128]{1,0:T(8,128)S(1)}, f32[128,128]{1,0:T(8,128)S(1)}, f32[128,128]{1,0:T(8,128)S(1)}) custom-call(s32[38]{0:T(128)S(1)} %pad_add_fusion.meta, f32[4,1,8,128,128]{4,3,2,1,0:T(8,128)S(1)} %copy-done.1, f32[8,128,128]{2,1,0:T(8,128)S(1)} %pad_maximum_fusion.2.rest_0_, ...), custom_call_target="tpu_custom_call" | custom-call | bytes 12582912 | tf_op jit(solution)/shard_map/pallas_call | solution.py:260
  62.0 3.1 %collective-permute-done.13 = f32[8,176,128]{2,1,0:T(8,128)S(1)} collective-permute-done((f32[8,176,128]{2,1,0:T(8,128)S(1)}, f32[8,176,128]{2,1,0:T(8,128)S(1)}, u32[]{:S(2)}, u32[]{:S(2)}) %collective-permute-start.13) | collective-permute-done | bytes 720928 | tf_op jit(solution)/shard_map/ppermute | solution.py:45
  65.1 7.0 %collective-permute-done.15 = f32[8,176,128]{2,1,0:T(8,128)S(1)} collective-permute-done((f32[8,176,128]{2,1,0:T(8,128)S(1)}, f32[8,176,128]{2,1,0:T(8,128)S(1)}, u32[]{:S(2)}, u32[]{:S(2)}) %collective-permute-start.15) | collective-permute-done | bytes 720928 | tf_op jit(solution)/shard_map/ppermute | solution.py:45
  72.1 0.8 collective-permute-done.14
  73.2 1.6 collective-permute-start.20
  74.8 1.6 collective-permute-start.21
  76.5 0.8 collective-permute-start.22
  77.3 0.7 collective-permute-start.17
  78.1 1.1 collective-permute-done.20
  79.1 2.4 %collective-permute-done.21 = f32[2,176,128]{2,1,0:T(8,128)S(1)} collective-permute-done((f32[2,176,128]{2,1,0:T(8,128)S(1)}, f32[2,176,128]{2,1,0:T(8,128)S(1)}, u32[]{:S(2)}, u32[]{:S(2)}) %collective-permute-start.21) | collective-permute-done | bytes 180256 | tf_op jit(solution)/shard_map/ppermute | solution.py:45
  81.7 5.9 %collective-permute-start.23 = (f32[176,128]{1,0:T(8,128)S(1)}, f32[176,128]{1,0:T(8,128)S(1)}, u32[]{:S(2)}, u32[]{:S(2)}) collective-permute-start(f32[176,128]{1,0:T(8,128)S(1)} %get-tuple-element.105), channel_id=1, source_target_pairs={{0,8},{4,12},{8,0},{12,4},{16,24},{20,28},{24,16},{28,20},{32,40},... | collective-permute-start | bytes 270344 | tf_op jit(solution)/shard_map/ppermute | solution.py:41
  88.2 5.6 %collective-permute-start.19 = (f32[176,128]{1,0:T(8,128)S(1)}, f32[176,128]{1,0:T(8,128)S(1)}, u32[]{:S(2)}, u32[]{:S(2)}) collective-permute-start(f32[176,128]{1,0:T(8,128)S(1)} %get-tuple-element.71), channel_id=1, source_target_pairs={{0,8},{4,12},{8,0},{12,4},{16,24},{20,28},{24,16},{28,20},{32,40},... | collective-permute-start | bytes 270344 | tf_op jit(solution)/shard_map/ppermute | solution.py:41
  93.9 1.5 shard_map.165
  95.4 1.5 collective-permute-start.31
  96.9 2.1 %collective-permute-start.24 = (f32[2,176,128]{2,1,0:T(8,128)S(1)}, f32[2,176,128]{2,1,0:T(8,128)S(1)}, u32[]{:S(2)}, u32[]{:S(2)}) collective-permute-start(f32[2,176,128]{2,1,0:T(8,128)S(1)} %pad_maximum_fusion.3), channel_id=1, source_target_pairs={{0,192},{4,52},{8,200},{12,60},{16,208},{20,4},{24,216},{28,12},{3... | collective-permute-start | bytes 540680 | tf_op jit(solution)/shard_map/ppermute | solution.py:45
  99.0 2.6 %collective-permute-start.25 = (f32[2,176,128]{2,1,0:T(8,128)S(1)}, f32[2,176,128]{2,1,0:T(8,128)S(1)}, u32[]{:S(2)}, u32[]{:S(2)}) collective-permute-start(f32[2,176,128]{2,1,0:T(8,128)S(1)} %pad_maximum_fusion.3), channel_id=1, source_target_pairs={{0,128},{4,36},{8,136},{12,44},{16,144},{20,52},{24,152},{28,60},{... | collective-permute-start | bytes 540680 | tf_op jit(solution)/shard_map/ppermute | solution.py:45
  101.6 1.4 collective-permute-done.24
  103.1 1.6 collective-permute-start.32
  104.9 2.3 %collective-permute-done.26 = f32[2,176,128]{2,1,0:T(8,128)S(1)} collective-permute-done((f32[2,176,128]{2,1,0:T(8,128)S(1)}, f32[2,176,128]{2,1,0:T(8,128)S(1)}, u32[]{:S(2)}, u32[]{:S(2)}) %collective-permute-start.26) | collective-permute-done | bytes 180256 | tf_op jit(solution)/shard_map/ppermute | solution.py:45
  107.2 3.5 %collective-permute-start.27 = (f32[8,176,128]{2,1,0:T(8,128)S(1)}, f32[8,176,128]{2,1,0:T(8,128)S(1)}, u32[]{:S(2)}, u32[]{:S(2)}) collective-permute-start(f32[8,176,128]{2,1,0:T(8,128)S(1)} %constant_dynamic-update-slice_fusion.rest_0_), channel_id=1, source_target_pairs={{0,48},{4,196},{8,56},{12,204},{16,0},{20,212},{24,8},{28,220},{32... | collective-permute-start | bytes 2162696 | tf_op jit(solution)/shard_map/ppermute | solution.py:45
  111.6 4.9 %collective-permute-done.33 = f32[160,128]{1,0:T(8,128)S(1)} collective-permute-done((f32[160,128]{1,0:T(8,128)S(1)}, f32[160,128]{1,0:T(8,128)S(1)}, u32[]{:S(2)}, u32[]{:S(2)}) %collective-permute-start.33) | collective-permute-done | bytes 81952 | tf_op jit(solution)/shard_map/ppermute | solution.py:55
  116.6 4.9 %collective-permute-start.34 = (f32[160,128]{1,0:T(8,128)S(1)}, f32[160,128]{1,0:T(8,128)S(1)}, u32[]{:S(2)}, u32[]{:S(2)}) collective-permute-start(f32[160,128]{1,0:T(8,128)S(1)} %fusion.1), channel_id=1, source_target_pairs={{0,8},{4,12},{8,0},{12,4},{16,24},{20,28},{24,16},{28,20},{32,40},... | collective-permute-start | bytes 245768 | tf_op jit(solution)/shard_map/ppermute | solution.py:41
  121.5 3.1 %collective-permute-done.34 = f32[160,128]{1,0:T(8,128)S(1)} collective-permute-done((f32[160,128]{1,0:T(8,128)S(1)}, f32[160,128]{1,0:T(8,128)S(1)}, u32[]{:S(2)}, u32[]{:S(2)}) %collective-permute-start.34) | collective-permute-done | bytes 81952 | tf_op jit(solution)/shard_map/ppermute | solution.py:41
  124.6 2.0 %collective-permute-done.27.rest_1_ = f32[8,176,128]{2,1,0:T(8,128)S(1)} collective-permute-done((f32[8,176,128]{2,1,0:T(8,128)S(1)}, f32[8,176,128]{2,1,0:T(8,128)S(1)}, u32[]{:S(2)}, u32[]{:S(2)}) %collective-permute-start.27) | collective-permute-done | bytes 720928 | tf_op jit(solution)/shard_map/ppermute | solution.py:45
  126.7 3.4 %collective-permute-done.29.rest_3_ = f32[8,176,128]{2,1,0:T(8,128)S(1)} collective-permute-done((f32[8,176,128]{2,1,0:T(8,128)S(1)}, f32[8,176,128]{2,1,0:T(8,128)S(1)}, u32[]{:S(2)}, u32[]{:S(2)}) %collective-permute-start.29) | collective-permute-done | bytes 720928 | tf_op jit(solution)/shard_map/ppermute | solution.py:45
  130.2 5.7 %collective-permute-start.35 = (f32[24,176,128]{2,1,0:T(8,128)S(1)}, f32[24,176,128]{2,1,0:T(8,128)S(1)}, u32[]{:S(2)}, u32[]{:S(2)}) collective-permute-start(f32[24,176,128]{2,1,0:T(8,128)S(1)} %pad_maximum_fusion), channel_id=1, source_target_pairs={{0,4},{4,0},{8,12},{12,8},{16,20},{20,16},{24,28},{28,24},{32,36},... | collective-permute-start | bytes 6488072 | tf_op jit(solution)/shard_map/ppermute | solution.py:37
  136.0 1.6 collective-permute-start.37
  137.6 1.0 collective-permute-start.38
  138.7 3.0 %collective-permute-done.36 = f32[160,128]{1,0:T(8,128)S(1)} collective-permute-done((f32[160,128]{1,0:T(8,128)S(1)}, f32[160,128]{1,0:T(8,128)S(1)}, u32[]{:S(2)}, u32[]{:S(2)}) %collective-permute-start.36) | collective-permute-done | bytes 81952 | tf_op jit(solution)/shard_map/ppermute | solution.py:45
  142.3 1.3 collective-permute-start.43
  143.6 1.4 collective-permute-start.44
  145.0 4.0 %shard_map.166 = (f32[176,128]{1,0:T(8,128)S(1)}, f32[176,128]{1,0:T(8,128)S(1)}, f32[176,128]{1,0:T(8,128)S(1)}, f32[176,128]{1,0:T(8,128)S(1)}) custom-call(s32[38]{0:T(128)S(1)} %pad_add_fusion.meta, f32[4,1,8,128,128]{4,3,2,1,0:T(8,128)S(1)} %copy-done.1, f32[8,176,128]{2,1,0:T(8,128)S(1)} %constant_dynamic-update-slice_fusion.rest_0_, ...), custom_call_target="tpu_custom_call" | custom-call | bytes 12582912 | tf_op jit(solution)/shard_map/pallas_call | solution.py:260
  149.2 5.1 %collective-permute-done.39.z1 = f32[176,128]{1,0:T(8,128)S(1)} collective-permute-done((f32[176,128]{1,0:T(8,128)S(1)}, f32[176,128]{1,0:T(8,128)S(1)}, u32[]{:S(2)}, u32[]{:S(2)}) %collective-permute-start.39) | collective-permute-done | bytes 90144 | tf_op jit(solution)/shard_map/ppermute | solution.py:51
  154.3 2.4 %collective-permute-start.40 = (f32[176,128]{1,0:T(8,128)S(1)}, f32[176,128]{1,0:T(8,128)S(1)}, u32[]{:S(2)}, u32[]{:S(2)}) collective-permute-start(f32[176,128]{1,0:T(8,128)S(1)} %get-tuple-element.81), channel_id=1, source_target_pairs={{0,2},{1,3},{2,0},{3,1},{4,6},{5,7},{6,4},{7,5},{8,10},{9,11},{10,... | collective-permute-start | bytes 270344 | tf_op jit(solution)/shard_map/ppermute | solution.py:51
  156.7 3.8 %collective-permute-done.45 = f32[160,128]{1,0:T(8,128)S(1)} collective-permute-done((f32[160,128]{1,0:T(8,128)S(1)}, f32[160,128]{1,0:T(8,128)S(1)}, u32[]{:S(2)}, u32[]{:S(2)}) %collective-permute-start.45) | collective-permute-done | bytes 81952 | tf_op jit(solution)/shard_map/ppermute | solution.py:55
  160.5 1.0 collective-permute-done.40.z2
  161.5 0.8 collective-permute-done.41.z3
  162.7 6.4 %collective-permute-done.46 = f32[2,160,128]{2,1,0:T(8,128)S(1)} collective-permute-done((f32[2,160,128]{2,1,0:T(8,128)S(1)}, f32[2,160,128]{2,1,0:T(8,128)S(1)}, u32[]{:S(2)}, u32[]{:S(2)}) %collective-permute-start.46) | collective-permute-done | bytes 163872 | tf_op jit(solution)/shard_map/ppermute | solution.py:55
  169.1 6.2 %collective-permute-start.47 = (f32[4,160,128]{2,1,0:T(8,128)S(1)}, f32[4,160,128]{2,1,0:T(8,128)S(1)}, u32[]{:S(2)}, u32[]{:S(2)}) collective-permute-start(f32[4,160,128]{2,1,0:T(8,128)S(1)} %constant_dynamic-update-slice_fusion.4.q), channel_id=1, source_target_pairs={{0,4},{4,0},{8,12},{12,8},{16,20},{20,16},{24,28},{28,24},{32,36},... | collective-permute-start | bytes 983048 | tf_op jit(solution)/shard_map/ppermute | solution.py:37
  176.5 1.4 shard_map.168
  (90 shorter events, 7.6 us)
Async XLA Ops:
  0.6 9.8 %collective-permute-start = (f32[128,128]{1,0:T(8,128)}, f32[128,128]{1,0:T(8,128)S(1)}, u32[]{:S(2)}, u32[]{:S(2)}) collective-permute-start(f32[128,128]{1,0:T(8,128)} %feat.3), channel_id=1, source_target_pairs={{0,8},{4,12},{8,0},{12,4},{16,24},{20,28},{24,16},{28,20},{32,40},... | collective-permute-start | bytes 196616 | tf_op jit(solution)/shard_map/ppermute | solution.py:41
  8.5 10.0 %collective-permute-start.8 = (f32[172,128]{1,0:T(8,128)}, f32[172,128]{1,0:T(8,128)S(1)}, u32[]{:S(2)}, u32[]{:S(2)}) collective-permute-start(f32[172,128]{1,0:T(8,128)} %bitcast.32), channel_id=1, source_target_pairs={{0,3},{1,0},{2,1},{3,2},{4,7},{5,4},{6,5},{7,6},{8,11},{9,8},{10,9... | collective-permute-start | bytes 264200 | tf_op jit(solution)/shard_map/ppermute | solution.py:51
  11.3 13.2 %collective-permute-start.1 = (f32[2,128,128]{2,1,0:T(8,128)S(1)}, f32[2,128,128]{2,1,0:T(8,128)S(1)}, u32[]{:S(2)}, u32[]{:S(2)}) collective-permute-start(f32[2,128,128]{2,1,0:T(8,128)S(1)} %pad_maximum_fusion.6), channel_id=1, source_target_pairs={{0,192},{4,52},{8,200},{12,60},{16,208},{20,4},{24,216},{28,12},{3... | collective-permute-start | bytes 393224 | tf_op jit(solution)/shard_map/ppermute | solution.py:45
  14.1 10.4 %collective-permute-start.2 = (f32[2,128,128]{2,1,0:T(8,128)S(1)}, f32[2,128,128]{2,1,0:T(8,128)S(1)}, u32[]{:S(2)}, u32[]{:S(2)}) collective-permute-start(f32[2,128,128]{2,1,0:T(8,128)S(1)} %pad_maximum_fusion.6), channel_id=1, source_target_pairs={{0,128},{4,36},{8,136},{12,44},{16,144},{20,52},{24,152},{28,60},{... | collective-permute-start | bytes 393224 | tf_op jit(solution)/shard_map/ppermute | solution.py:45
  14.4 10.0 %collective-permute-start.3 = (f32[2,128,128]{2,1,0:T(8,128)S(1)}, f32[2,128,128]{2,1,0:T(8,128)S(1)}, u32[]{:S(2)}, u32[]{:S(2)}) collective-permute-start(f32[2,128,128]{2,1,0:T(8,128)S(1)} %pad_maximum_fusion.6), channel_id=1, source_target_pairs={{0,64},{4,20},{8,72},{12,28},{16,80},{20,36},{24,88},{28,44},{32,9... | collective-permute-start | bytes 393224 | tf_op jit(solution)/shard_map/ppermute | solution.py:45
  15.1 5.8 %collective-permute-start.9 = (f32[172,128]{1,0:T(8,128)}, f32[172,128]{1,0:T(8,128)S(1)}, u32[]{:S(2)}, u32[]{:S(2)}) collective-permute-start(f32[172,128]{1,0:T(8,128)} %bitcast.33), channel_id=1, source_target_pairs={{0,2},{1,3},{2,0},{3,1},{4,6},{5,7},{6,4},{7,5},{8,10},{9,11},{10,... | collective-permute-start | bytes 264200 | tf_op jit(solution)/shard_map/ppermute | solution.py:51
  18.4 6.0 %collective-permute-start.10 = (f32[172,128]{1,0:T(8,128)}, f32[172,128]{1,0:T(8,128)S(1)}, u32[]{:S(2)}, u32[]{:S(2)}) collective-permute-start(f32[172,128]{1,0:T(8,128)} %bitcast.34), channel_id=1, source_target_pairs={{0,1},{1,2},{2,3},{3,0},{4,5},{5,6},{6,7},{7,4},{8,9},{9,10},{10,1... | collective-permute-start | bytes 264200 | tf_op jit(solution)/shard_map/ppermute | solution.py:51
  24.5 1.6 copy-start
  26.1 0.9 copy-start.4
  29.6 11.4 %collective-permute-start.11 = (f32[32,176,128]{2,1,0:T(8,128)S(1)}, f32[32,176,128]{2,1,0:T(8,128)S(1)}, u32[]{:S(2)}, u32[]{:S(2)}) collective-permute-start(f32[32,176,128]{2,1,0:T(8,128)S(1)} %get-tuple-element.58), channel_id=1, source_target_pairs={{0,4},{4,0},{8,12},{12,8},{16,20},{20,16},{24,28},{28,24},{32,36},... | collective-permute-start | bytes 8650760 | tf_op jit(solution)/shard_map/ppermute | solution.py:37
  36.1 8.3 %collective-permute-start.4 = (f32[8,128,128]{2,1,0:T(8,128)S(1)}, f32[8,128,128]{2,1,0:T(8,128)S(1)}, u32[]{:S(2)}, u32[]{:S(2)}) collective-permute-start(f32[8,128,128]{2,1,0:T(8,128)S(1)} %pad_maximum_fusion.2.rest_0_), channel_id=1, source_target_pairs={{0,48},{4,196},{8,56},{12,204},{16,0},{20,212},{24,8},{28,220},{32... | collective-permute-start | bytes 1572872 | tf_op jit(solution)/shard_map/ppermute | solution.py:45
  36.1 9.9 %collective-permute-start.5 = (f32[8,128,128]{2,1,0:T(8,128)S(1)}, f32[8,128,128]{2,1,0:T(8,128)S(1)}, u32[]{:S(2)}, u32[]{:S(2)}) collective-permute-start(f32[8,128,128]{2,1,0:T(8,128)S(1)} %pad_maximum_fusion.2.rest_0_), channel_id=1, source_target_pairs={{0,32},{4,132},{8,40},{12,140},{16,48},{20,148},{24,56},{28,156},{... | collective-permute-start | bytes 1572872 | tf_op jit(solution)/shard_map/ppermute | solution.py:45
  37.9 13.7 %collective-permute-start.6 = (f32[8,128,128]{2,1,0:T(8,128)S(1)}, f32[8,128,128]{2,1,0:T(8,128)S(1)}, u32[]{:S(2)}, u32[]{:S(2)}) collective-permute-start(f32[8,128,128]{2,1,0:T(8,128)S(1)} %pad_maximum_fusion.2.rest_0_), channel_id=1, source_target_pairs={{0,16},{4,68},{8,24},{12,76},{16,32},{20,84},{24,40},{28,92},{32,4... | collective-permute-start | bytes 1572872 | tf_op jit(solution)/shard_map/ppermute | solution.py:45
  41.4 18.2 %copy-start.1 = (f32[4,1,8,128,128]{4,3,2,1,0:T(8,128)S(1)}, f32[4,1,8,128,128]{4,3,2,1,0:T(8,128)}, u32[]{:S(2)}) copy-start(f32[4,1,8,128,128]{4,3,2,1,0:T(8,128)} %tiles.5) | copy-start | bytes 6291460
  51.7 7.9 %collective-permute-start.12 = (f32[24,128,128]{2,1,0:T(8,128)S(1)}, f32[24,128,128]{2,1,0:T(8,128)S(1)}, u32[]{:S(2)}, u32[]{:S(2)}) collective-permute-start(f32[24,128,128]{2,1,0:T(8,128)S(1)} %pad_maximum_fusion.1), channel_id=1, source_target_pairs={{0,4},{4,0},{8,12},{12,8},{16,20},{20,16},{24,28},{28,24},{32,36},... | collective-permute-start | bytes 4718600 | tf_op jit(solution)/shard_map/ppermute | solution.py:37
  53.5 11.6 %collective-permute-start.13 = (f32[8,176,128]{2,1,0:T(8,128)S(1)}, f32[8,176,128]{2,1,0:T(8,128)S(1)}, u32[]{:S(2)}, u32[]{:S(2)}) collective-permute-start(f32[8,176,128]{2,1,0:T(8,128)S(1)} %get-tuple-element.63), channel_id=1, source_target_pairs={{0,64},{4,20},{8,72},{12,28},{16,80},{20,36},{24,88},{28,44},{32,9... | collective-permute-start | bytes 2162696 | tf_op jit(solution)/shard_map/ppermute | solution.py:45
  54.4 17.7 %collective-permute-start.15 = (f32[8,176,128]{2,1,0:T(8,128)S(1)}, f32[8,176,128]{2,1,0:T(8,128)S(1)}, u32[]{:S(2)}, u32[]{:S(2)}) collective-permute-start(f32[8,176,128]{2,1,0:T(8,128)S(1)} %get-tuple-element.65), channel_id=1, source_target_pairs={{0,192},{4,52},{8,200},{12,60},{16,208},{20,4},{24,216},{28,12},{3... | collective-permute-start | bytes 2162696 | tf_op jit(solution)/shard_map/ppermute | solution.py:45
  56.1 16.8 %collective-permute-start.14 = (f32[8,176,128]{2,1,0:T(8,128)S(1)}, f32[8,176,128]{2,1,0:T(8,128)S(1)}, u32[]{:S(2)}, u32[]{:S(2)}) collective-permute-start(f32[8,176,128]{2,1,0:T(8,128)S(1)} %get-tuple-element.64), channel_id=1, source_target_pairs={{0,128},{4,36},{8,136},{12,44},{16,144},{20,52},{24,152},{28,60},{... | collective-permute-start | bytes 2162696 | tf_op jit(solution)/shard_map/ppermute | solution.py:45
  57.7 1.9 %collective-permute-start.7 = (f32[8,128,128]{2,1,0:T(8,128)S(1)}, f32[8,128,128]{2,1,0:T(8,128)S(1)}, u32[]{:S(2)}, u32[]{:S(2)}) collective-permute-start(f32[8,128,128]{2,1,0:T(8,128)S(1)} %pad_maximum_fusion.2.rest_0_), channel_id=1, source_target_pairs={{0,4},{4,0},{8,12},{12,8},{16,20},{20,16},{24,28},{28,24},{32,36},... | collective-permute-start | bytes 1572872 | tf_op jit(solution)/shard_map/ppermute | solution.py:37
  62.0 25.6 %copy-start.2 = (f32[256,172]{0,1:T(8,128)S(1)}, f32[256,172]{0,1:T(8,128)}, u32[]{:S(2)}) copy-start(f32[256,172]{0,1:T(8,128)} %param.19) | copy-start | bytes 528388
  62.0 25.6 %copy-start.3 = (f32[128,128]{1,0:T(8,128)S(1)}, f32[128,128]{1,0:T(8,128)}, u32[]{:S(2)}) copy-start(f32[128,128]{1,0:T(8,128)} %feat.3) | copy-start | bytes 196612
  62.0 25.6 %copy-start.7 = (f32[128,256]{1,0:T(8,128)S(1)}, f32[128,256]{1,0:T(8,128)}, u32[]{:S(2)}) copy-start(f32[128,256]{1,0:T(8,128)} %self_one.1) | copy-start | bytes 393220
  62.0 25.6 %copy-start.8 = (f32[128,256]{1,0:T(8,128)S(1)}, f32[128,256]{1,0:T(8,128)}, u32[]{:S(2)}) copy-start(f32[128,256]{1,0:T(8,128)} %neigh_one.1) | copy-start | bytes 393220
  62.0 25.6 %copy-start.9 = (f32[256]{0:T(256)S(1)}, f32[256]{0:T(256)}, u32[]{:S(2)}) copy-start(f32[256]{0:T(256)} %param.17) | copy-start | bytes 3076
  73.1 20.7 %copy-start.5 = (f32[128,172]{0,1:T(8,128)S(1)}, f32[128,172]{0,1:T(8,128)}, u32[]{:S(2)}) copy-start(f32[128,172]{0,1:T(8,128)} %param.21) | copy-start | bytes 264196
  73.1 20.7 %copy-start.6 = (f32[256,172]{0,1:T(8,128)S(1)}, f32[256,172]{0,1:T(8,128)}, u32[]{:S(2)}) copy-start(f32[256,172]{0,1:T(8,128)} %param.18) | copy-start | bytes 528388
  73.2 20.7 %copy-start.10 = (f32[172]{0:T(256)S(1)}, f32[172]{0:T(256)}, u32[]{:S(2)}) copy-start(f32[172]{0:T(256)} %param.20) | copy-start | bytes 2068
  73.2 5.9 %collective-permute-start.20 = (f32[2,176,128]{2,1,0:T(8,128)S(1)}, f32[2,176,128]{2,1,0:T(8,128)S(1)}, u32[]{:S(2)}, u32[]{:S(2)}) collective-permute-start(f32[2,176,128]{2,1,0:T(8,128)S(1)} %get-tuple-element.99), channel_id=1, source_target_pairs={{0,16},{4,68},{8,24},{12,76},{16,32},{20,84},{24,40},{28,92},{32,4... | collective-permute-start | bytes 540680 | tf_op jit(solution)/shard_map/ppermute | solution.py:45
  74.8 6.8 %collective-permute-start.21 = (f32[2,176,128]{2,1,0:T(8,128)S(1)}, f32[2,176,128]{2,1,0:T(8,128)S(1)}, u32[]{:S(2)}, u32[]{:S(2)}) collective-permute-start(f32[2,176,128]{2,1,0:T(8,128)S(1)} %get-tuple-element.98), channel_id=1, source_target_pairs={{0,32},{4,132},{8,40},{12,140},{16,48},{20,148},{24,56},{28,156},{... | collective-permute-start | bytes 540680 | tf_op jit(solution)/shard_map/ppermute | solution.py:45
  76.5 5.2 %collective-permute-start.22 = (f32[2,176,128]{2,1,0:T(8,128)S(1)}, f32[2,176,128]{2,1,0:T(8,128)S(1)}, u32[]{:S(2)}, u32[]{:S(2)}) collective-permute-start(f32[2,176,128]{2,1,0:T(8,128)S(1)} %get-tuple-element.97), channel_id=1, source_target_pairs={{0,48},{4,196},{8,56},{12,204},{16,0},{20,212},{24,8},{28,220},{32... | collective-permute-start | bytes 540680 | tf_op jit(solution)/shard_map/ppermute | solution.py:45
  77.3 10.3 %collective-permute-start.18 = (f32[128,128]{1,0:T(8,128)S(1)}, f32[128,128]{1,0:T(8,128)S(1)}, u32[]{:S(2)}, u32[]{:S(2)}) collective-permute-start(f32[128,128]{1,0:T(8,128)S(1)} %get-tuple-element.70), channel_id=1, source_target_pairs={{0,3},{1,0},{2,1},{3,2},{4,7},{5,4},{6,5},{7,6},{8,11},{9,8},{10,9... | collective-permute-start | bytes 196616 | tf_op jit(solution)/shard_map/ppermute | solution.py:51
  77.3 10.3 %collective-permute-start.17 = (f32[128,128]{1,0:T(8,128)S(1)}, f32[128,128]{1,0:T(8,128)S(1)}, u32[]{:S(2)}, u32[]{:S(2)}) collective-permute-start(f32[128,128]{1,0:T(8,128)S(1)} %get-tuple-element.68), channel_id=1, source_target_pairs={{0,2},{1,3},{2,0},{3,1},{4,6},{5,7},{6,4},{7,5},{8,10},{9,11},{10,... | collective-permute-start | bytes 196616 | tf_op jit(solution)/shard_map/ppermute | solution.py:51
  79.1 8.5 %collective-permute-start.16 = (f32[128,128]{1,0:T(8,128)S(1)}, f32[128,128]{1,0:T(8,128)S(1)}, u32[]{:S(2)}, u32[]{:S(2)}) collective-permute-start(f32[128,128]{1,0:T(8,128)S(1)} %get-tuple-element.66), channel_id=1, source_target_pairs={{0,1},{1,2},{2,3},{3,0},{4,5},{5,6},{6,7},{7,4},{8,9},{9,10},{10,1... | collective-permute-start | bytes 196616 | tf_op jit(solution)/shard_map/ppermute | solution.py:51
  81.7 12.1 %collective-permute-start.23 = (f32[176,128]{1,0:T(8,128)S(1)}, f32[176,128]{1,0:T(8,128)S(1)}, u32[]{:S(2)}, u32[]{:S(2)}) collective-permute-start(f32[176,128]{1,0:T(8,128)S(1)} %get-tuple-element.105), channel_id=1, source_target_pairs={{0,8},{4,12},{8,0},{12,4},{16,24},{20,28},{24,16},{28,20},{32,40},... | collective-permute-start | bytes 270344 | tf_op jit(solution)/shard_map/ppermute | solution.py:41
  88.2 8.6 %collective-permute-start.19 = (f32[176,128]{1,0:T(8,128)S(1)}, f32[176,128]{1,0:T(8,128)S(1)}, u32[]{:S(2)}, u32[]{:S(2)}) collective-permute-start(f32[176,128]{1,0:T(8,128)S(1)} %get-tuple-element.71), channel_id=1, source_target_pairs={{0,8},{4,12},{8,0},{12,4},{16,24},{20,28},{24,16},{28,20},{32,40},... | collective-permute-start | bytes 270344 | tf_op jit(solution)/shard_map/ppermute | solution.py:41
  95.4 7.6 %collective-permute-start.31 = (f32[4,160,128]{2,1,0:T(8,128)S(1)}, f32[4,160,128]{2,1,0:T(8,128)S(1)}, u32[]{:S(2)}, u32[]{:S(2)}) collective-permute-start(f32[4,160,128]{2,1,0:T(8,128)S(1)} %get-tuple-element.76), channel_id=1, source_target_pairs={{0,4},{4,0},{8,12},{12,8},{16,20},{20,16},{24,28},{28,24},{32,36},... | collective-permute-start | bytes 983048 | tf_op jit(solution)/shard_map/ppermute | solution.py:37
  96.9 6.1 %collective-permute-start.24 = (f32[2,176,128]{2,1,0:T(8,128)S(1)}, f32[2,176,128]{2,1,0:T(8,128)S(1)}, u32[]{:S(2)}, u32[]{:S(2)}) collective-permute-start(f32[2,176,128]{2,1,0:T(8,128)S(1)} %pad_maximum_fusion.3), channel_id=1, source_target_pairs={{0,192},{4,52},{8,200},{12,60},{16,208},{20,4},{24,216},{28,12},{3... | collective-permute-start | bytes 540680 | tf_op jit(solution)/shard_map/ppermute | solution.py:45
  99.0 5.8 %collective-permute-start.25 = (f32[2,176,128]{2,1,0:T(8,128)S(1)}, f32[2,176,128]{2,1,0:T(8,128)S(1)}, u32[]{:S(2)}, u32[]{:S(2)}) collective-permute-start(f32[2,176,128]{2,1,0:T(8,128)S(1)} %pad_maximum_fusion.3), channel_id=1, source_target_pairs={{0,128},{4,36},{8,136},{12,44},{16,144},{20,52},{24,152},{28,60},{... | collective-permute-start | bytes 540680 | tf_op jit(solution)/shard_map/ppermute | solution.py:45
  101.6 5.6 %collective-permute-start.26 = (f32[2,176,128]{2,1,0:T(8,128)S(1)}, f32[2,176,128]{2,1,0:T(8,128)S(1)}, u32[]{:S(2)}, u32[]{:S(2)}) collective-permute-start(f32[2,176,128]{2,1,0:T(8,128)S(1)} %pad_maximum_fusion.3), channel_id=1, source_target_pairs={{0,64},{4,20},{8,72},{12,28},{16,80},{20,36},{24,88},{28,44},{32,9... | collective-permute-start | bytes 540680 | tf_op jit(solution)/shard_map/ppermute | solution.py:45
  103.1 8.3 %collective-permute-start.32 = (f32[2,160,128]{2,1,0:T(8,128)S(1)}, f32[2,160,128]{2,1,0:T(8,128)S(1)}, u32[]{:S(2)}, u32[]{:S(2)}) collective-permute-start(f32[2,160,128]{2,1,0:T(8,128)S(1)} %pad_maximum_fusion.4), channel_id=1, source_target_pairs={{0,1},{1,0},{2,3},{3,2},{4,5},{5,4},{6,7},{7,6},{8,9},{9,8},{10,11... | collective-permute-start | bytes 491528 | tf_op jit(solution)/shard_map/ppermute | solution.py:55
  107.2 19.5 %collective-permute-start.27 = (f32[8,176,128]{2,1,0:T(8,128)S(1)}, f32[8,176,128]{2,1,0:T(8,128)S(1)}, u32[]{:S(2)}, u32[]{:S(2)}) collective-permute-start(f32[8,176,128]{2,1,0:T(8,128)S(1)} %constant_dynamic-update-slice_fusion.rest_0_), channel_id=1, source_target_pairs={{0,48},{4,196},{8,56},{12,204},{16,0},{20,212},{24,8},{28,220},{32... | collective-permute-start | bytes 2162696 | tf_op jit(solution)/shard_map/ppermute | solution.py:45
  110.7 16.0 %collective-permute-start.28 = (f32[8,176,128]{2,1,0:T(8,128)S(1)}, f32[8,176,128]{2,1,0:T(8,128)S(1)}, u32[]{:S(2)}, u32[]{:S(2)}) collective-permute-start(f32[8,176,128]{2,1,0:T(8,128)S(1)} %constant_dynamic-update-slice_fusion.rest_0_), channel_id=1, source_target_pairs={{0,32},{4,132},{8,40},{12,140},{16,48},{20,148},{24,56},{28,156},{... | collective-permute-start | bytes 2162696 | tf_op jit(solution)/shard_map/ppermute | solution.py:45
  110.7 19.4 %collective-permute-start.29 = (f32[8,176,128]{2,1,0:T(8,128)S(1)}, f32[8,176,128]{2,1,0:T(8,128)S(1)}, u32[]{:S(2)}, u32[]{:S(2)}) collective-permute-start(f32[8,176,128]{2,1,0:T(8,128)S(1)} %constant_dynamic-update-slice_fusion.rest_0_), channel_id=1, source_target_pairs={{0,16},{4,68},{8,24},{12,76},{16,32},{20,84},{24,40},{28,92},{32,4... | collective-permute-start | bytes 2162696 | tf_op jit(solution)/shard_map/ppermute | solution.py:45
  111.4 5.2 %collective-permute-start.33 = (f32[160,128]{1,0:T(8,128)S(1)}, f32[160,128]{1,0:T(8,128)S(1)}, u32[]{:S(2)}, u32[]{:S(2)}) collective-permute-start(f32[160,128]{1,0:T(8,128)S(1)} %slice_bitcast_fusion.2), channel_id=1, source_target_pairs={{0,2},{1,3},{2,0},{3,1},{4,6},{5,7},{6,4},{7,5},{8,10},{9,11},{10,... | collective-permute-start | bytes 245768 | tf_op jit(solution)/shard_map/ppermute | solution.py:55
  116.6 8.0 %collective-permute-start.34 = (f32[160,128]{1,0:T(8,128)S(1)}, f32[160,128]{1,0:T(8,128)S(1)}, u32[]{:S(2)}, u32[]{:S(2)}) collective-permute-start(f32[160,128]{1,0:T(8,128)S(1)} %fusion.1), channel_id=1, source_target_pairs={{0,8},{4,12},{8,0},{12,4},{16,24},{20,28},{24,16},{28,20},{32,40},... | collective-permute-start | bytes 245768 | tf_op jit(solution)/shard_map/ppermute | solution.py:41
  130.2 14.8 %collective-permute-start.35 = (f32[24,176,128]{2,1,0:T(8,128)S(1)}, f32[24,176,128]{2,1,0:T(8,128)S(1)}, u32[]{:S(2)}, u32[]{:S(2)}) collective-permute-start(f32[24,176,128]{2,1,0:T(8,128)S(1)} %pad_maximum_fusion), channel_id=1, source_target_pairs={{0,4},{4,0},{8,12},{12,8},{16,20},{20,16},{24,28},{28,24},{32,36},... | collective-permute-start | bytes 6488072 | tf_op jit(solution)/shard_map/ppermute | solution.py:37
  135.9 9.1 %collective-permute-start.30 = (f32[8,176,128]{2,1,0:T(8,128)S(1)}, f32[8,176,128]{2,1,0:T(8,128)S(1)}, u32[]{:S(2)}, u32[]{:S(2)}) collective-permute-start(f32[8,176,128]{2,1,0:T(8,128)S(1)} %constant_dynamic-update-slice_fusion.rest_0_), channel_id=1, source_target_pairs={{0,4},{4,0},{8,12},{12,8},{16,20},{20,16},{24,28},{28,24},{32,36},... | collective-permute-start | bytes 2162696 | tf_op jit(solution)/shard_map/ppermute | solution.py:37
  136.0 5.7 %collective-permute-start.36 = (f32[160,128]{1,0:T(8,128)S(1)}, f32[160,128]{1,0:T(8,128)S(1)}, u32[]{:S(2)}, u32[]{:S(2)}) collective-permute-start(f32[160,128]{1,0:T(8,128)S(1)} %add.89), channel_id=1, source_target_pairs={{0,64},{4,20},{8,72},{12,28},{16,80},{20,36},{24,88},{28,44},{32,9... | collective-permute-start | bytes 245768 | tf_op jit(solution)/shard_map/ppermute | solution.py:45
  136.0 5.7 %collective-permute-start.37 = (f32[160,128]{1,0:T(8,128)S(1)}, f32[160,128]{1,0:T(8,128)S(1)}, u32[]{:S(2)}, u32[]{:S(2)}) collective-permute-start(f32[160,128]{1,0:T(8,128)S(1)} %add.89), channel_id=1, source_target_pairs={{0,128},{4,36},{8,136},{12,44},{16,144},{20,52},{24,152},{28,60},{... | collective-permute-start | bytes 245768 | tf_op jit(solution)/shard_map/ppermute | solution.py:45
  137.6 4.6 %collective-permute-start.38 = (f32[160,128]{1,0:T(8,128)S(1)}, f32[160,128]{1,0:T(8,128)S(1)}, u32[]{:S(2)}, u32[]{:S(2)}) collective-permute-start(f32[160,128]{1,0:T(8,128)S(1)} %add.89), channel_id=1, source_target_pairs={{0,192},{4,52},{8,200},{12,60},{16,208},{20,4},{24,216},{28,12},{3... | collective-permute-start | bytes 245768 | tf_op jit(solution)/shard_map/ppermute | solution.py:45
  142.3 6.9 %collective-permute-start.42 = (f32[160,128]{1,0:T(8,128)S(1)}, f32[160,128]{1,0:T(8,128)S(1)}, u32[]{:S(2)}, u32[]{:S(2)}) collective-permute-start(f32[160,128]{1,0:T(8,128)S(1)} %add_add_fusion.2), channel_id=1, source_target_pairs={{0,16},{4,68},{8,24},{12,76},{16,32},{20,84},{24,40},{28,92},{32,4... | collective-permute-start | bytes 245768 | tf_op jit(solution)/shard_map/ppermute | solution.py:45
  142.3 6.8 %collective-permute-start.43 = (f32[160,128]{1,0:T(8,128)S(1)}, f32[160,128]{1,0:T(8,128)S(1)}, u32[]{:S(2)}, u32[]{:S(2)}) collective-permute-start(f32[160,128]{1,0:T(8,128)S(1)} %add_add_fusion.2), channel_id=1, source_target_pairs={{0,32},{4,132},{8,40},{12,140},{16,48},{20,148},{24,56},{28,156},{... | collective-permute-start | bytes 245768 | tf_op jit(solution)/shard_map/ppermute | solution.py:45
  143.6 5.5 %collective-permute-start.44 = (f32[160,128]{1,0:T(8,128)S(1)}, f32[160,128]{1,0:T(8,128)S(1)}, u32[]{:S(2)}, u32[]{:S(2)}) collective-permute-start(f32[160,128]{1,0:T(8,128)S(1)} %add_add_fusion.2), channel_id=1, source_target_pairs={{0,48},{4,196},{8,56},{12,204},{16,0},{20,212},{24,8},{28,220},{32... | collective-permute-start | bytes 245768 | tf_op jit(solution)/shard_map/ppermute | solution.py:45
  149.0 5.3 %collective-permute-start.39 = (f32[176,128]{1,0:T(8,128)S(1)}, f32[176,128]{1,0:T(8,128)S(1)}, u32[]{:S(2)}, u32[]{:S(2)}) collective-permute-start(f32[176,128]{1,0:T(8,128)S(1)} %get-tuple-element.80), channel_id=1, source_target_pairs={{0,1},{1,2},{2,3},{3,0},{4,5},{5,6},{6,7},{7,4},{8,9},{9,10},{10,1... | collective-permute-start | bytes 270344 | tf_op jit(solution)/shard_map/ppermute | solution.py:51
  154.3 6.2 %collective-permute-start.45 = (f32[160,128]{1,0:T(8,128)S(1)}, f32[160,128]{1,0:T(8,128)S(1)}, u32[]{:S(2)}, u32[]{:S(2)}) collective-permute-start(f32[160,128]{1,0:T(8,128)S(1)} %add_add_fusion.1), channel_id=1, source_target_pairs={{0,2},{1,3},{2,0},{3,1},{4,6},{5,7},{6,4},{7,5},{8,10},{9,11},{10,... | collective-permute-start | bytes 245768 | tf_op jit(solution)/shard_map/ppermute | solution.py:55
  154.3 7.2 %collective-permute-start.40 = (f32[176,128]{1,0:T(8,128)S(1)}, f32[176,128]{1,0:T(8,128)S(1)}, u32[]{:S(2)}, u32[]{:S(2)}) collective-permute-start(f32[176,128]{1,0:T(8,128)S(1)} %get-tuple-element.81), channel_id=1, source_target_pairs={{0,2},{1,3},{2,0},{3,1},{4,6},{5,7},{6,4},{7,5},{8,10},{9,11},{10,... | collective-permute-start | bytes 270344 | tf_op jit(solution)/shard_map/ppermute | solution.py:51
  156.7 5.7 %collective-permute-start.41 = (f32[176,128]{1,0:T(8,128)S(1)}, f32[176,128]{1,0:T(8,128)S(1)}, u32[]{:S(2)}, u32[]{:S(2)}) collective-permute-start(f32[176,128]{1,0:T(8,128)S(1)} %get-tuple-element.82), channel_id=1, source_target_pairs={{0,3},{1,0},{2,1},{3,2},{4,7},{5,4},{6,5},{7,6},{8,11},{9,8},{10,9... | collective-permute-start | bytes 270344 | tf_op jit(solution)/shard_map/ppermute | solution.py:51
  162.3 6.7 %collective-permute-start.46 = (f32[2,160,128]{2,1,0:T(8,128)S(1)}, f32[2,160,128]{2,1,0:T(8,128)S(1)}, u32[]{:S(2)}, u32[]{:S(2)}) collective-permute-start(f32[2,160,128]{2,1,0:T(8,128)S(1)} %pad_maximum_fusion.5), channel_id=1, source_target_pairs={{0,1},{1,0},{2,3},{3,2},{4,5},{5,4},{6,7},{7,6},{8,9},{9,8},{10,11... | collective-permute-start | bytes 491528 | tf_op jit(solution)/shard_map/ppermute | solution.py:55
  169.1 7.5 %collective-permute-start.47 = (f32[4,160,128]{2,1,0:T(8,128)S(1)}, f32[4,160,128]{2,1,0:T(8,128)S(1)}, u32[]{:S(2)}, u32[]{:S(2)}) collective-permute-start(f32[4,160,128]{2,1,0:T(8,128)S(1)} %constant_dynamic-update-slice_fusion.4.q), channel_id=1, source_target_pairs={{0,4},{4,0},{8,12},{12,8},{16,20},{20,16},{24,28},{28,24},{32,36},... | collective-permute-start | bytes 983048 | tf_op jit(solution)/shard_map/ppermute | solution.py:37
where the time goes:
time: 179 us; the launch traced here: 178 us
  starting transfers between devices  85.2 us (48%)
  waiting for transfers between devices  71.3 us (40%)
  Pallas kernels  13.1 us (7%)
  other arithmetic  4.03 us (2%)
  local copies, waits for them, and re-layouts  3.26 us (2%)
    ppermute x24, waiting for transfers between devices, send_plane(): lax.ppermute(a, 'row', row_perm(lambda c: (d, 0, 0, 0) if c == stage else...  37.6 us
    ppermute x24, starting transfers between devices, send_plane(): lax.ppermute(a, 'row', row_perm(lambda c: (d, 0, 0, 0) if c == stage else...  29.2 us
    ppermute x4, starting transfers between devices, send_z(): return lax.ppermute(a, 'row', row_perm(lambda c: (0, 0, 1, 0)))  24.2 us
    ppermute x7, starting transfers between devices, send_core(): return lax.ppermute(a, 'row', row_perm(lambda c: (0, 0, 0, 1)))  21.7 us
    ppermute x4, waiting for transfers between devices, swap_rep(): return lax.ppermute(a, 'rep', [(j, j ^ bit) for j in range(NR)])  15.2 us
    pallas_call x7, Pallas kernels, call(): pl.pallas_call(kernel, out_shape=[jax.ShapeDtypeStruct(s, F32) for s in o...  13.1 us
    ppermute x9, waiting for transfers between devices, send_rep(): return lax.ppermute(a, 'rep', [(j, (j + d) % NR) for j in range(NR)])  10.4 us
    ppermute x9, starting transfers between devices, send_rep(): return lax.ppermute(a, 'rep', [(j, (j + d) % NR) for j in range(NR)])  7.95 us
  transfers between devices with their start and end apart: 48, of which 28 were waited for; matrix products, arithmetic and copies ran while one was open for 2% of the time, Pallas kernels for 5%

commit v1 on v0

--- a/solution.py
+++ b/solution.py
@@ -16,6 +16,7 @@
 VMEM = pl.BlockSpec(memory_space=pltpu.VMEM)
 SMEM = pl.BlockSpec(memory_space=pltpu.SMEM)
 ANY = pl.BlockSpec(memory_space=pl.ANY)
+HBM = pl.BlockSpec(memory_space=pltpu.HBM)
 MIB = 1024 * 1024
 COUNTS, ME, REP = 32, 36, 37
 
@@ -118,12 +119,12 @@
 
 
 def agg_kernel(second, meta, tiles, *rest):
-    refs, outs, (buf, tile_buf, sems) = rest[:6], rest[6:10], rest[10:]
+    refs, outs, (buf, tile_buf, sems) = rest[:6], rest[6:8], rest[8:]
     me, rep = meta[ME], meta[REP]
     start_loads(refs, buf, tiles, tile_buf, sems)
     rows = buf.shape[1]
     for d in range(NR):
-        block = (rep + d) & 3
+        block = rep ^ d
 
         def step(i, acc, block=block):
             for u in range(2):
@@ -141,20 +142,20 @@
             return acc
 
         pairs = (meta[COUNTS + block] + 1) >> 1
-        outs[d][...] = fold(lax.fori_loop(0, pairs, step, jnp.zeros((rows, 256), F32)))
-
-
-def transposed_kernel(meta, tiles, ct0, ct1, ct2, ct3, own, oth, tile_buf, ct_buf, sem):
+        outs[d & 1][d >> 1] = fold(lax.fori_loop(0, pairs, step, jnp.zeros((rows, 256), F32)))
+
+
+def transposed_kernel(meta, tiles, near, far, own, oth, tile_buf, ct_buf, sem):
     me, rep = meta[ME], meta[REP]
     copy = pltpu.make_async_copy(tiles, tile_buf, sem)
     copy.start()
     for o in (own, oth):
         o[...] = jnp.zeros(o.shape, F32)
     copy.wait()
-    for d, ct in enumerate((ct0, ct1, ct2, ct3)):
-        block = (rep + d) & 3
+    for d in range(NR):
+        block = rep ^ d
         ct_buf[...] = jnp.concatenate(
-            [wide(ct[...]), jnp.zeros((CP - CLS, 256), jnp.bfloat16)], axis=0
+            [wide((near, far)[d & 1][d >> 1]), jnp.zeros((CP - CLS, 256), jnp.bfloat16)], axis=0
         )
 
         def step(i, _, block=block):
@@ -182,8 +183,8 @@
         lax.fori_loop(0, (meta[COUNTS + block] + 1) >> 1, step, 0)
 
 
-def hidden_kernel(a0, a1, a2, a3, feat, self_one, neigh_one, bias, nt, agg, pre, yt):
-    total = (a0[...] + a1[...]) + (a2[...] + a3[...])
+def hidden_kernel(kept, got, last, feat, self_one, neigh_one, bias, nt, agg, pre, yt):
+    total = (kept[0] + got[0]) + last[...]
     agg[...] = total
     p = dot3(feat[...], self_one[...]) + dot3(total, neigh_one[...]) + bias[...]
     pre[...] = p
@@ -225,15 +226,18 @@
 
 
 def piece_order(meta):
+    me = meta[ME]
     for slot in range(2):
-        for d in range(NR):
-            start = (((meta[ME] & 1) ^ slot) * NR + (meta[REP] ^ d)) * 160
+        core = (me & 1) ^ slot
+        at = jnp.where(core == 0, me >> 4, me >> 2)
+        for d in range(4):
+            start = (core * 4 + ((at + d) & 3)) * 160
             yield slot, d, pl.multiple_of(start, 8)
 
 
 def finish_kernel(meta, q, qo, gs1, gn1, gb1, gs2, gn2, gb2, packed):
     for slot, d, start in piece_order(meta):
-        packed[pl.ds(start, 160)] = (q, qo)[slot][(0, 2, 1, 3)[d]]
+        packed[pl.ds(start, 160)] = (q, qo)[slot][d]
 
     def take(start, rows):
         return jnp.concatenate(
@@ -248,15 +252,17 @@
     gb2[...] = take(432 + CLS, 1)[:, :CLS]
 
 
-def logits_kernel(z0, z1, z2, z3, base, out):
-    total = (z0[...] + z1[...]) + (z2[...] + z3[...])
-    out[...] = base[...] + total[:CLS]
-
-
-def call(kernel, outs, ins, scratch=(), smem=0, in_any=(), mib=8, cost=6):
+def logits_kernel(kept, got, last, base, out):
+    part = pl.ds(0, CLS)
+    out[...] = base[...] + ((kept[0, part] + got[0, part]) + last[part])
+
+
+def call(kernel, outs, ins, scratch=(), smem=0, in_hbm=(), in_any=(), mib=8, cost=6):
     specs = [SMEM] * smem + [VMEM] * (len(ins) - smem)
     for k in in_any:
         specs[k] = ANY
+    for k in in_hbm:
+        specs[k] = HBM
     return pl.pallas_call(
         kernel,
         out_shape=[jax.ShapeDtypeStruct(s, F32) for s in outs],
@@ -285,6 +291,12 @@
     return [lane] + [send_plane(lane, 1, -d) for d in (1, 2, 3)]
 
 
+def gather_ring(lane):
+    one, three = send_plane(lane, 1, 3), send_plane(lane, 1, 1)
+    two = jnp.concatenate([send_plane(one[:4], 1, 3), send_plane(three[4:], 1, 1)])
+    return [lane, one, two, three]
+
+
 def gather_core(plane, *held):
     rest = jnp.concatenate([after(plane[1], *held)] + plane[2:])
     return plane + [send_core(plane[0]), send_core(rest)]
@@ -296,7 +308,8 @@
 
 
 def scatter_lane(parts, *held):
-    return [parts[0]] + [send_plane(after(parts[d], *held), 0, d) for d in (1, 2, 3)]
+    one, three = send_plane(parts[1], 0, 1), send_plane(parts[3], 0, 3)
+    return [parts[0], one, send_plane(after(parts[2], *held), 0, 2), three]
 
 
 def scatter_plane(q):
@@ -304,38 +317,36 @@
     return q[0], send_z(q[1])
 
 
-def reduce_reps(same, other):
+def reduce_lane(same, other):
     got = send_core(other)
-    kept = jnp.stack([same[0] + got[0], same[2] + got[2]])
-    kept = kept + swap_rep(jnp.stack([same[1] + got[1], same[3] + got[3]]), 1)
-    q = kept[0] + swap_rep(kept[1], 2)
-    return q + send_z(q)
-
-
-def all_reduce(q, products, held):
-    q = add4(after(q, products[0]), *(send_plane(q, 1, d) for d in (1, 2, 3)))
-    q = after(q, held[1])
-    q = after(jnp.stack([q, swap_rep(q, 2)]), *held[2:])
-    q = jnp.concatenate([q, swap_rep(q, 1)])
-    return q, send_core(q)
+    parts = [same[d] + got[d] for d in range(4)]
+    return add4(parts[0], *(send_plane(parts[d], 0, d) for d in (1, 2, 3)))
+
+
+def last_sums(q, products):
+    kept, given = products
+    got = swap_rep(given, 1)
+    last = swap_rep(kept[1] + got[1], 2)
+    q = after(q, kept) + send_z(q)
+    q = add4(q, *(send_plane(q, 1, d) for d in (1, 2, 3)))
+    q = after(q, got)
+    q = jnp.stack([q] + [send_plane(q, 0, -d) for d in (1, 2, 3)])
+    q = after(q, last)
+    return kept, got, last, q, send_core(q)
 
 
 def agg(second, head, pieces):
     rows = pieces[0].shape[1]
     shape = (rows, SIDE)
     return call(
-        functools.partial(agg_kernel, second), [shape] * 4, head + tuple(pieces),
+        functools.partial(agg_kernel, second), [(2,) + shape] * 2, head + tuple(pieces),
         scratch=(
             pltpu.VMEM((64, rows, SIDE), F32),
             pltpu.VMEM((4, 1, 8, SIDE, SIDE), F32),
             pltpu.SemaphoreType.DMA((7,)),
         ),
-        smem=1, in_any=range(1, 8), mib=16, cost=12,
-    )
-
-
-def sum_reps(parts, *held):
-    return [parts[0]] + [send_rep(after(parts[d], *held), d) for d in (1, 2, 3)]
+        smem=1, in_hbm=(1,), in_any=range(2, 8), mib=16, cost=12,
+    )
 
 
 def shards(
@@ -359,42 +370,48 @@
     ct, st, nt = cotangent.T, self_two.T, neigh_two.T
 
     swapped = send_z(features)
-    cts = [ct] + [after(send_rep(ct, -d), swapped) for d in (1, 2, 3)]
+    pair = jnp.stack([ct, swap_rep(ct, 2)])
+    far = swap_rep(pair, 1)
     lane = gather_lane(features, swapped)
     own, oth = call(
-        transposed_kernel, [(32,) + padded] * 2, head + tuple(after(c, lane) for c in cts),
+        transposed_kernel, [(32,) + padded] * 2, head + (after(pair, lane), far),
         scratch=(
             pltpu.VMEM((4, 1, 8, SIDE, SIDE), F32),
             pltpu.VMEM((CP, 256), jnp.bfloat16),
             pltpu.SemaphoreType.DMA(()),
         ),
-        smem=1, in_any=(1,), mib=16, cost=12,
+        smem=1, in_hbm=(1,), mib=16, cost=12,
     )
     plane = gather_plane(lane)
     parts = scatter_core(own, oth)
     laned = scatter_lane(parts, *plane[1:])
-    products = agg(False, head, gather_core(plane, *parts))
-    q = add4(after(laned[0], products[0]), *laned[1:])
-
+    pieces = gather_core(plane, *parts)
+    products = agg(False, head, pieces)
+
+    kept, given = products
+    got = swap_rep(given, 1)
+    last = swap_rep(kept[1] + got[1], 2)
+    q = add4(after(laned[0], got), *laned[1:])
     sums, pre, yt = call(
         hidden_kernel, [block, (SIDE, 256), padded],
-        (*sum_reps(products, q), features, self_one, neigh_one, bias_one.reshape(1, -1), nt),
+        (kept, got, last, features, self_one, neigh_one, bias_one.reshape(1, -1), nt),
     )
     g, gz = scatter_plane(q)
-    plane = gather_plane(gather_lane(yt, send_z(yt), gz))
+    lane = gather_lane(yt, send_z(yt))
     base, same, other = call(
         grad_kernel, [tall, (4, 160, SIDE), (4, 160, SIDE)],
-        (meta, g, gz, pre, sums, features, ct, st, nt, bias_two.reshape(1, -1)),
+        (meta, g, gz, after(pre, lane), sums, features, ct, st, nt, bias_two.reshape(1, -1)),
         scratch=(pltpu.VMEM((GROWS, SIDE), F32),), smem=1,
     )
-    kept = reduce_reps(same, other)
+    plane = gather_plane(after(lane, same))
+    kept = reduce_lane(same, other)
+    kept = kept + swap_rep(kept, 1)
     pieces = gather_core(plane, kept)
-    kept = add4(kept, *(send_plane(kept, 0, d) for d in (1, 2, 3)))
+    kept = kept + swap_rep(kept, 2)
     pieces[-1] = after(pieces[-1], kept)
     products = agg(True, head, pieces)
-    parts = sum_reps(products)
+    *parts, q, qo = last_sums(kept, products)
     (logits,) = call(logits_kernel, [tall], (*parts, base))
-    q, qo = all_reduce(kept, products, parts)
     gs1, gn1, gb1, gs2, gn2, gb2 = call(
         finish_kernel,
         [(128, 256), (128, 256), (1, 256), (CLS, 256), (CLS, 256), (1, CLS)],

time: 179 us -> 165 us (0.922)
  starting transfers between devices: 85.2 us -> 71 us
    ppermute x24 -> x27, waiting for transfers between devices: 37.6 us -> 49.9 us  [send_plane(): lax.ppermute(a, 'row', row_perm(lambda c: (d, 0, 0, 0) if c == stage else...]
    ppermute x9 -> x0, waiting for transfers between devices: 10.4 us -> none  [send_rep(): return lax.ppermute(a, 'rep', [(j, (j + d) % NR) for j in range(NR)])]
    ppermute x4, starting transfers between devices: 24.2 us -> 15.5 us  [send_z(): return lax.ppermute(a, 'row', row_perm(lambda c: (0, 0, 1, 0)))]
    ppermute x9 -> x0, starting transfers between devices: 7.95 us -> none  [send_rep(): return lax.ppermute(a, 'rep', [(j, (j + d) % NR) for j in range(NR)])]
    ppermute x7, starting transfers between devices: 21.7 us -> 16.1 us  [send_core(): return lax.ppermute(a, 'row', row_perm(lambda c: (0, 0, 0, 1)))]
    ppermute x4 -> x8, starting transfers between devices: 2.14 us -> 6.52 us  [swap_rep(): return lax.ppermute(a, 'rep', [(j, j ^ bit) for j in range(NR)])]
    ppermute x24 -> x27, starting transfers between devices: 29.2 us -> 32.8 us  [send_plane(): lax.ppermute(a, 'row', row_perm(lambda c: (d, 0, 0, 0) if c == stage else...]
    ppermute x7, waiting for transfers between devices: 4.71 us -> 1.74 us  [send_core(): return lax.ppermute(a, 'row', row_perm(lambda c: (0, 0, 0, 1)))]
  transfers between devices with their start and end apart: 48 -> 46, of which waited for: 28 -> 27; matrix products, arithmetic and copies ran while one was open for 2% -> 3% of each run, Pallas kernels for 5% -> 4%
where the time goes in v1:
time: 165 us; the launch traced here: 164 us
  waiting for transfers between devices  72.7 us (44%)
  starting transfers between devices  71 us (43%)
  Pallas kernels  12.4 us (8%)
  other arithmetic  5.01 us (3%)
  local copies, waits for them, and re-layouts  2.29 us (1%)
    ppermute x27, waiting for transfers between devices, send_plane(): lax.ppermute(a, 'row', row_perm(lambda c: (d, 0, 0, 0) if c == stage else...  49.9 us
    ppermute x27, starting transfers between devices, send_plane(): lax.ppermute(a, 'row', row_perm(lambda c: (d, 0, 0, 0) if c == stage else...  32.8 us
    ppermute x7, starting transfers between devices, send_core(): return lax.ppermute(a, 'row', row_perm(lambda c: (0, 0, 0, 1)))  16.1 us
    ppermute x4, starting transfers between devices, send_z(): return lax.ppermute(a, 'row', row_perm(lambda c: (0, 0, 1, 0)))  15.5 us
    ppermute x8, waiting for transfers between devices, swap_rep(): return lax.ppermute(a, 'rep', [(j, j ^ bit) for j in range(NR)])  14.8 us
    pallas_call x7, Pallas kernels, call(): pl.pallas_call(kernel, out_shape=[jax.ShapeDtypeStruct(s, F32) for s in o...  12.4 us
    ppermute x8, starting transfers between devices, swap_rep(): return lax.ppermute(a, 'rep', [(j, j ^ bit) for j in range(NR)])  6.52 us
    ppermute x4, waiting for transfers between devices, send_z(): return lax.ppermute(a, 'row', row_perm(lambda c: (0, 0, 1, 0)))  6.33 us
  transfers between devices with their start and end apart: 46, of which 27 were waited for; matrix products, arithmetic and copies ran while one was open for 3% of the time, Pallas kernels for 4%

profile of v1, /device:TPU:1, one launch (start us, length us, event | category | flops | bytes accessed | tf_op | source)
XLA Modules:
  0.0 164.5 jit_solution(13676826474103496088)
XLA Ops:
  0.6 7.8 %collective-permute-start = (f32[128,128]{1,0:T(8,128)}, f32[128,128]{1,0:T(8,128)S(1)}, u32[]{:S(2)}, u32[]{:S(2)}) collective-permute-start(f32[128,128]{1,0:T(8,128)} %feat.3), channel_id=1, source_target_pairs={{0,8},{4,12},{8,0},{12,4},{16,24},{20,28},{24,16},{28,20},{32,40},... | collective-permute-start | bytes 196616 | tf_op jit(solution)/shard_map/ppermute | solution.py:42
  8.5 1.2 collective-permute-start.8
  10.2 1.3 reduce.3
  11.6 0.9 pad_maximum_fusion.7
  12.4 2.8 %collective-permute-start.1 = (f32[2,128,128]{2,1,0:T(8,128)S(1)}, f32[2,128,128]{2,1,0:T(8,128)S(1)}, u32[]{:S(2)}, u32[]{:S(2)}) collective-permute-start(f32[2,128,128]{2,1,0:T(8,128)S(1)} %pad_maximum_fusion.7), channel_id=1, source_target_pairs={{0,192},{4,52},{8,200},{12,60},{16,208},{20,4},{24,216},{28,12},{3... | collective-permute-start | bytes 393224 | tf_op jit(solution)/shard_map/ppermute | solution.py:46
  15.6 0.7 collective-permute-start.3
  16.3 0.8 collective-permute-done.8
  17.1 0.9 pad_maximum_fusion.5.near
  18.1 0.7 pad_add_fusion.meta
  18.8 1.8 %collective-permute-done.2 = f32[2,128,128]{2,1,0:T(8,128)S(1)} collective-permute-done((f32[2,128,128]{2,1,0:T(8,128)S(1)}, f32[2,128,128]{2,1,0:T(8,128)S(1)}, u32[]{:S(2)}, u32[]{:S(2)}) %collective-permute-start.2) | collective-permute-done | bytes 131104 | tf_op jit(solution)/shard_map/ppermute | solution.py:46
  20.7 1.6 collective-permute-done.3
  22.3 0.7 collective-permute-done.9.far
  23.0 1.6 copy-done
  24.6 2.4 %shard_map.162 = (f32[32,176,128]{2,1,0:T(8,128)S(1)}, f32[32,176,128]{2,1,0:T(8,128)S(1)}) custom-call(s32[38]{0:T(128)S(1)} %pad_add_fusion.meta, f32[4,1,8,128,128]{4,3,2,1,0:T(8,128)S(1)} %copy-done, f32[2,172,128]{2,1,0:T(8,128)S(1)} %pad_maximum_fusion.5.near, f32[2,172,128]{2,1,0:T(8,128)S(1)} %collective-permute-done.9.far), custom_call_target="tpu_custom_call" | custom-call | bytes 12582912 | tf_op jit(solution)/shard_map/pallas_call | solution.py:266
  27.0 1.9 %collective-permute-start.10 = (f32[32,176,128]{2,1,0:T(8,128)S(1)}, f32[32,176,128]{2,1,0:T(8,128)S(1)}, u32[]{:S(2)}, u32[]{:S(2)}) collective-permute-start(f32[32,176,128]{2,1,0:T(8,128)S(1)} %get-tuple-element.38), channel_id=1, source_target_pairs={{0,4},{4,0},{8,12},{12,8},{16,20},{20,16},{24,28},{28,24},{32,36},... | collective-permute-start | bytes 8650760 | tf_op jit(solution)/shard_map/ppermute | solution.py:38
  28.9 2.7 %collective-permute-start.4 = (f32[8,128,128]{2,1,0:T(8,128)S(1)}, f32[8,128,128]{2,1,0:T(8,128)S(1)}, u32[]{:S(2)}, u32[]{:S(2)}) collective-permute-start(f32[8,128,128]{2,1,0:T(8,128)S(1)} %pad_maximum_fusion.3.rest_0_), channel_id=1, source_target_pairs={{0,48},{4,196},{8,56},{12,204},{16,0},{20,212},{24,8},{28,220},{32... | collective-permute-start | bytes 1572872 | tf_op jit(solution)/shard_map/ppermute | solution.py:46
  32.1 0.6 collective-permute-start.6
  32.7 1.0 collective-permute-done.10
  34.2 9.2 %collective-permute-done.4.rest_1_ = f32[8,128,128]{2,1,0:T(8,128)S(1)} collective-permute-done((f32[8,128,128]{2,1,0:T(8,128)S(1)}, f32[8,128,128]{2,1,0:T(8,128)S(1)}, u32[]{:S(2)}, u32[]{:S(2)}) %collective-permute-start.4) | collective-permute-done | bytes 524320 | tf_op jit(solution)/shard_map/ppermute | solution.py:46
  43.3 3.7 %collective-permute-done.6.rest_3_ = f32[8,128,128]{2,1,0:T(8,128)S(1)} collective-permute-done((f32[8,128,128]{2,1,0:T(8,128)S(1)}, f32[8,128,128]{2,1,0:T(8,128)S(1)}, u32[]{:S(2)}, u32[]{:S(2)}) %collective-permute-start.6) | collective-permute-done | bytes 524320 | tf_op jit(solution)/shard_map/ppermute | solution.py:46
  47.2 1.8 %collective-permute-start.11 = (f32[24,128,128]{2,1,0:T(8,128)S(1)}, f32[24,128,128]{2,1,0:T(8,128)S(1)}, u32[]{:S(2)}, u32[]{:S(2)}) collective-permute-start(f32[24,128,128]{2,1,0:T(8,128)S(1)} %pad_maximum_fusion.1), channel_id=1, source_target_pairs={{0,4},{4,0},{8,12},{12,8},{16,20},{20,16},{24,28},{28,24},{32,36},... | collective-permute-start | bytes 4718600 | tf_op jit(solution)/shard_map/ppermute | solution.py:38
  49.1 1.8 %collective-permute-start.19 = (f32[8,176,128]{2,1,0:T(8,128)S(1)}, f32[8,176,128]{2,1,0:T(8,128)S(1)}, u32[]{:S(2)}, u32[]{:S(2)}) collective-permute-start(f32[8,176,128]{2,1,0:T(8,128)S(1)} %get-tuple-element.44), channel_id=1, source_target_pairs={{0,128},{4,36},{8,136},{12,44},{16,144},{20,52},{24,152},{28,60},{... | collective-permute-start | bytes 2162696 | tf_op jit(solution)/shard_map/ppermute | solution.py:46
  50.9 2.7 %collective-permute-start.20 = (f32[8,176,128]{2,1,0:T(8,128)S(1)}, f32[8,176,128]{2,1,0:T(8,128)S(1)}, u32[]{:S(2)}, u32[]{:S(2)}) collective-permute-start(f32[8,176,128]{2,1,0:T(8,128)S(1)} %get-tuple-element.65), channel_id=1, source_target_pairs={{0,192},{4,52},{8,200},{12,60},{16,208},{20,4},{24,216},{28,12},{3... | collective-permute-start | bytes 2162696 | tf_op jit(solution)/shard_map/ppermute | solution.py:46
  53.6 2.1 %shard_map.163 = (f32[2,128,128]{2,1,0:T(8,128)S(1)}, f32[2,128,128]{2,1,0:T(8,128)S(1)}) custom-call(s32[38]{0:T(128)S(1)} %pad_add_fusion.meta, f32[4,1,8,128,128]{4,3,2,1,0:T(8,128)S(1)} %copy-done.1, f32[8,128,128]{2,1,0:T(8,128)S(1)} %pad_maximum_fusion.3.rest_0_, f32[8,128,128]{2,1,0:T(8,128)S(1)} %collective-permute-done.4.rest_1_, ...), custom_call_target="tpu_custom_call" | custom-call | bytes 12582912 | tf_op jit(solution)/shard_map/pallas_call | solution.py:266
  56.1 4.1 %collective-permute-done.12.got = f32[2,128,128]{2,1,0:T(8,128)S(1)} collective-permute-done((f32[2,128,128]{2,1,0:T(8,128)S(1)}, f32[2,128,128]{2,1,0:T(8,128)S(1)}, u32[]{:S(2)}, u32[]{:S(2)}) %collective-permute-start.12) | collective-permute-done | bytes 131104 | tf_op jit(solution)/shard_map/ppermute | solution.py:56
  60.2 0.7 collective-permute-start.13
  61.1 7.7 %collective-permute-done.18 = f32[8,176,128]{2,1,0:T(8,128)S(1)} collective-permute-done((f32[8,176,128]{2,1,0:T(8,128)S(1)}, f32[8,176,128]{2,1,0:T(8,128)S(1)}, u32[]{:S(2)}, u32[]{:S(2)}) %collective-permute-start.18) | collective-permute-done | bytes 720928 | tf_op jit(solution)/shard_map/ppermute | solution.py:46
  69.1 0.6 shard_map.164
  69.7 5.7 %collective-permute-start.14 = (f32[176,128]{1,0:T(8,128)S(1)}, f32[176,128]{1,0:T(8,128)S(1)}, u32[]{:S(2)}, u32[]{:S(2)}) collective-permute-start(f32[176,128]{1,0:T(8,128)S(1)} %get-tuple-element.42), channel_id=1, source_target_pairs={{0,8},{4,12},{8,0},{12,4},{16,24},{20,28},{24,16},{28,20},{32,40},... | collective-permute-start | bytes 270344 | tf_op jit(solution)/shard_map/ppermute | solution.py:42
  75.4 1.0 collective-permute-start.21
  76.4 2.0 %collective-permute-start.22 = (f32[2,176,128]{2,1,0:T(8,128)S(1)}, f32[2,176,128]{2,1,0:T(8,128)S(1)}, u32[]{:S(2)}, u32[]{:S(2)}) collective-permute-start(f32[2,176,128]{2,1,0:T(8,128)S(1)} %get-tuple-element.70), channel_id=1, source_target_pairs={{0,32},{4,132},{8,40},{12,140},{16,48},{20,148},{24,56},{28,156},{... | collective-permute-start | bytes 540680 | tf_op jit(solution)/shard_map/ppermute | solution.py:46
  78.9 0.7 collective-permute-start.15
  79.6 0.6 collective-permute-start.16
  80.2 0.8 collective-permute-done.21
  81.0 1.7 %collective-permute-start.17 = (f32[2,176,128]{2,1,0:T(8,128)S(1)}, f32[2,176,128]{2,1,0:T(8,128)S(1)}, u32[]{:S(2)}, u32[]{:S(2)}) collective-permute-start(f32[2,176,128]{2,1,0:T(8,128)S(1)} %pad_maximum_fusion.6), channel_id=1, source_target_pairs={{0,64},{4,20},{8,72},{12,28},{16,80},{20,36},{24,88},{28,44},{32,9... | collective-permute-start | bytes 540680 | tf_op jit(solution)/shard_map/ppermute | solution.py:46
  82.8 0.8 collective-permute-done.22
  83.9 1.8 %collective-permute-start.24 = (f32[176,128]{1,0:T(8,128)S(1)}, f32[176,128]{1,0:T(8,128)S(1)}, u32[]{:S(2)}, u32[]{:S(2)}) collective-permute-start(f32[176,128]{1,0:T(8,128)S(1)} %get-tuple-element.75), channel_id=1, source_target_pairs={{0,8},{4,12},{8,0},{12,4},{16,24},{20,28},{24,16},{28,20},{32,40},... | collective-permute-start | bytes 270344 | tf_op jit(solution)/shard_map/ppermute | solution.py:42
  85.9 3.2 %collective-permute-done.17 = f32[2,176,128]{2,1,0:T(8,128)S(1)} collective-permute-done((f32[2,176,128]{2,1,0:T(8,128)S(1)}, f32[2,176,128]{2,1,0:T(8,128)S(1)}, u32[]{:S(2)}, u32[]{:S(2)}) %collective-permute-start.17) | collective-permute-done | bytes 180256 | tf_op jit(solution)/shard_map/ppermute | solution.py:46
  89.2 3.1 %collective-permute-done.24.gz = f32[176,128]{1,0:T(8,128)S(1)} collective-permute-done((f32[176,128]{1,0:T(8,128)S(1)}, f32[176,128]{1,0:T(8,128)S(1)}, u32[]{:S(2)}, u32[]{:S(2)}) %collective-permute-start.24) | collective-permute-done | bytes 90144 | tf_op jit(solution)/shard_map/ppermute | solution.py:42
  92.3 1.5 shard_map.165
  93.8 6.6 %collective-permute-start.29 = (f32[4,160,128]{2,1,0:T(8,128)S(1)}, f32[4,160,128]{2,1,0:T(8,128)S(1)}, u32[]{:S(2)}, u32[]{:S(2)}) collective-permute-start(f32[4,160,128]{2,1,0:T(8,128)S(1)} %get-tuple-element.50), channel_id=1, source_target_pairs={{0,4},{4,0},{8,12},{12,8},{16,20},{20,16},{24,28},{28,24},{32,36},... | collective-permute-start | bytes 983048 | tf_op jit(solution)/shard_map/ppermute | solution.py:38
  100.3 1.4 collective-permute-start.25
  101.7 2.1 %collective-permute-start.26 = (f32[8,176,128]{2,1,0:T(8,128)S(1)}, f32[8,176,128]{2,1,0:T(8,128)S(1)}, u32[]{:S(2)}, u32[]{:S(2)}) collective-permute-start(f32[8,176,128]{2,1,0:T(8,128)S(1)} %pad_maximum_fusion.2.rest_0_), channel_id=1, source_target_pairs={{0,32},{4,132},{8,40},{12,140},{16,48},{20,148},{24,56},{28,156},{... | collective-permute-start | bytes 2162696 | tf_op jit(solution)/shard_map/ppermute | solution.py:46
  103.9 1.9 %collective-permute-start.31 = (f32[160,128]{1,0:T(8,128)S(1)}, f32[160,128]{1,0:T(8,128)S(1)}, u32[]{:S(2)}, u32[]{:S(2)}) collective-permute-start(f32[160,128]{1,0:T(8,128)S(1)} %get-tuple-element.73), channel_id=1, source_target_pairs={{0,128},{4,36},{8,136},{12,44},{16,144},{20,52},{24,152},{28,60},{... | collective-permute-start | bytes 245768 | tf_op jit(solution)/shard_map/ppermute | solution.py:46
  105.8 11.8 %collective-permute-done.30 = f32[160,128]{1,0:T(8,128)S(1)} collective-permute-done((f32[160,128]{1,0:T(8,128)S(1)}, f32[160,128]{1,0:T(8,128)S(1)}, u32[]{:S(2)}, u32[]{:S(2)}) %collective-permute-start.30) | collective-permute-done | bytes 81952 | tf_op jit(solution)/shard_map/ppermute | solution.py:46
  117.6 3.6 %collective-permute-done.32 = f32[160,128]{1,0:T(8,128)S(1)} collective-permute-done((f32[160,128]{1,0:T(8,128)S(1)}, f32[160,128]{1,0:T(8,128)S(1)}, u32[]{:S(2)}, u32[]{:S(2)}) %collective-permute-start.32) | collective-permute-done | bytes 81952 | tf_op jit(solution)/shard_map/ppermute | solution.py:46
  121.2 1.8 %collective-permute-start.33 = (f32[160,128]{1,0:T(8,128)S(1)}, f32[160,128]{1,0:T(8,128)S(1)}, u32[]{:S(2)}, u32[]{:S(2)}) collective-permute-start(f32[160,128]{1,0:T(8,128)S(1)} %fusion.7), channel_id=1, source_target_pairs={{0,1},{1,0},{2,3},{3,2},{4,5},{5,4},{6,7},{7,6},{8,9},{9,8},{10,11... | collective-permute-start | bytes 245768 | tf_op jit(solution)/shard_map/ppermute | solution.py:56
  123.0 2.7 %collective-permute-done.33 = f32[160,128]{1,0:T(8,128)S(1)} collective-permute-done((f32[160,128]{1,0:T(8,128)S(1)}, f32[160,128]{1,0:T(8,128)S(1)}, u32[]{:S(2)}, u32[]{:S(2)}) %collective-permute-start.33) | collective-permute-done | bytes 81952 | tf_op jit(solution)/shard_map/ppermute | solution.py:56
  125.9 0.8 collective-permute-start.34
  127.3 4.0 %collective-permute-done.35 = f32[160,128]{1,0:T(8,128)S(1)} collective-permute-done((f32[160,128]{1,0:T(8,128)S(1)}, f32[160,128]{1,0:T(8,128)S(1)}, u32[]{:S(2)}, u32[]{:S(2)}) %collective-permute-start.35) | collective-permute-done | bytes 81952 | tf_op jit(solution)/shard_map/ppermute | solution.py:56
  131.6 3.8 %shard_map.166 = (f32[2,176,128]{2,1,0:T(8,128)S(1)}, f32[2,176,128]{2,1,0:T(8,128)S(1)}) custom-call(s32[38]{0:T(128)S(1)} %pad_add_fusion.meta, f32[4,1,8,128,128]{4,3,2,1,0:T(8,128)S(1)} %copy-done.1, f32[8,176,128]{2,1,0:T(8,128)S(1)} %pad_maximum_fusion.2.rest_0_, f32[8,176,128]{2,1,0:T(8,128)S(1)} %collective-permute-done.25.rest_1_, ...), custom_call_target="tpu_custom_call" | custom-call | bytes 12582912 | tf_op jit(solution)/shard_map/pallas_call | solution.py:266
  135.4 3.2 %collective-permute-done.38 = f32[160,128]{1,0:T(8,128)S(1)} collective-permute-done((f32[160,128]{1,0:T(8,128)S(1)}, f32[160,128]{1,0:T(8,128)S(1)}, u32[]{:S(2)}, u32[]{:S(2)}) %collective-permute-start.38) | collective-permute-done | bytes 81952 | tf_op jit(solution)/shard_map/ppermute | solution.py:42
  138.6 3.8 %collective-permute-start.39 = (f32[160,128]{1,0:T(8,128)S(1)}, f32[160,128]{1,0:T(8,128)S(1)}, u32[]{:S(2)}, u32[]{:S(2)}) collective-permute-start(f32[160,128]{1,0:T(8,128)S(1)} %add.120), channel_id=1, source_target_pairs={{0,16},{4,68},{8,24},{12,76},{16,32},{20,84},{24,40},{28,92},{32,4... | collective-permute-start | bytes 245768 | tf_op jit(solution)/shard_map/ppermute | solution.py:46
  142.4 2.5 %collective-permute-start.41 = (f32[160,128]{1,0:T(8,128)S(1)}, f32[160,128]{1,0:T(8,128)S(1)}, u32[]{:S(2)}, u32[]{:S(2)}) collective-permute-start(f32[160,128]{1,0:T(8,128)S(1)} %add.120), channel_id=1, source_target_pairs={{0,48},{4,196},{8,56},{12,204},{16,0},{20,212},{24,8},{28,220},{32... | collective-permute-start | bytes 245768 | tf_op jit(solution)/shard_map/ppermute | solution.py:46
  144.9 2.3 %collective-permute-done.40 = f32[160,128]{1,0:T(8,128)S(1)} collective-permute-done((f32[160,128]{1,0:T(8,128)S(1)}, f32[160,128]{1,0:T(8,128)S(1)}, u32[]{:S(2)}, u32[]{:S(2)}) %collective-permute-start.40) | collective-permute-done | bytes 81952 | tf_op jit(solution)/shard_map/ppermute | solution.py:46
  147.3 2.4 %collective-permute-done.36.got = f32[2,176,128]{2,1,0:T(8,128)S(1)} collective-permute-done((f32[2,176,128]{2,1,0:T(8,128)S(1)}, f32[2,176,128]{2,1,0:T(8,128)S(1)}, u32[]{:S(2)}, u32[]{:S(2)}) %collective-permute-start.36) | collective-permute-done | bytes 180256 | tf_op jit(solution)/shard_map/ppermute | solution.py:56
  149.7 1.8 %collective-permute-start.42 = (f32[160,128]{1,0:T(8,128)S(1)}, f32[160,128]{1,0:T(8,128)S(1)}, u32[]{:S(2)}, u32[]{:S(2)}) collective-permute-start(f32[160,128]{1,0:T(8,128)S(1)} %add_add_fusion.1), channel_id=1, source_target_pairs={{0,192},{4,52},{8,200},{12,60},{16,208},{20,4},{24,216},{28,12},{3... | collective-permute-start | bytes 245768 | tf_op jit(solution)/shard_map/ppermute | solution.py:46
  151.5 0.6 collective-permute-start.44
  152.1 2.1 %collective-permute-start.37 = (f32[176,128]{1,0:T(8,128)S(1)}, f32[176,128]{1,0:T(8,128)S(1)}, u32[]{:S(2)}, u32[]{:S(2)}) collective-permute-start(f32[176,128]{1,0:T(8,128)S(1)} %fusion.1), channel_id=1, source_target_pairs={{0,2},{1,3},{2,0},{3,1},{4,6},{5,7},{6,4},{7,5},{8,10},{9,11},{10,... | collective-permute-start | bytes 270344 | tf_op jit(solution)/shard_map/ppermute | solution.py:56
  154.2 2.2 %collective-permute-done.43 = f32[160,128]{1,0:T(8,128)S(1)} collective-permute-done((f32[160,128]{1,0:T(8,128)S(1)}, f32[160,128]{1,0:T(8,128)S(1)}, u32[]{:S(2)}, u32[]{:S(2)}) %collective-permute-start.43) | collective-permute-done | bytes 81952 | tf_op jit(solution)/shard_map/ppermute | solution.py:46
  156.9 4.9 %collective-permute-start.45 = (f32[4,160,128]{2,1,0:T(8,128)S(1)}, f32[4,160,128]{2,1,0:T(8,128)S(1)}, u32[]{:S(2)}, u32[]{:S(2)}) collective-permute-start(f32[4,160,128]{2,1,0:T(8,128)S(1)} %pad_maximum_fusion.4.q), channel_id=1, source_target_pairs={{0,4},{4,0},{8,12},{12,8},{16,20},{20,16},{24,28},{28,24},{32,36},... | collective-permute-start | bytes 983048 | tf_op jit(solution)/shard_map/ppermute | solution.py:38
  161.8 0.7 shard_map.167
  162.4 0.6 collective-permute-done.45.qo
  163.0 1.4 shard_map.168
  (80 shorter events, 5.9 us)
Async XLA Ops:
  0.6 11.0 %collective-permute-start = (f32[128,128]{1,0:T(8,128)}, f32[128,128]{1,0:T(8,128)S(1)}, u32[]{:S(2)}, u32[]{:S(2)}) collective-permute-start(f32[128,128]{1,0:T(8,128)} %feat.3), channel_id=1, source_target_pairs={{0,8},{4,12},{8,0},{12,4},{16,24},{20,28},{24,16},{28,20},{32,40},... | collective-permute-start | bytes 196616 | tf_op jit(solution)/shard_map/ppermute | solution.py:42
  8.5 8.6 %collective-permute-start.8 = (f32[172,128]{1,0:T(8,128)}, f32[172,128]{1,0:T(8,128)S(1)}, u32[]{:S(2)}, u32[]{:S(2)}) collective-permute-start(f32[172,128]{1,0:T(8,128)} %bitcast.47), channel_id=1, source_target_pairs={{0,2},{1,3},{2,0},{3,1},{4,6},{5,7},{6,4},{7,5},{8,10},{9,11},{10,... | collective-permute-start | bytes 264200 | tf_op jit(solution)/shard_map/ppermute | solution.py:56
  12.4 6.4 %collective-permute-start.1 = (f32[2,128,128]{2,1,0:T(8,128)S(1)}, f32[2,128,128]{2,1,0:T(8,128)S(1)}, u32[]{:S(2)}, u32[]{:S(2)}) collective-permute-start(f32[2,128,128]{2,1,0:T(8,128)S(1)} %pad_maximum_fusion.7), channel_id=1, source_target_pairs={{0,192},{4,52},{8,200},{12,60},{16,208},{20,4},{24,216},{28,12},{3... | collective-permute-start | bytes 393224 | tf_op jit(solution)/shard_map/ppermute | solution.py:46
  15.3 5.4 %collective-permute-start.2 = (f32[2,128,128]{2,1,0:T(8,128)S(1)}, f32[2,128,128]{2,1,0:T(8,128)S(1)}, u32[]{:S(2)}, u32[]{:S(2)}) collective-permute-start(f32[2,128,128]{2,1,0:T(8,128)S(1)} %pad_maximum_fusion.7), channel_id=1, source_target_pairs={{0,128},{4,36},{8,136},{12,44},{16,144},{20,52},{24,152},{28,60},{... | collective-permute-start | bytes 393224 | tf_op jit(solution)/shard_map/ppermute | solution.py:46
  15.6 6.7 %collective-permute-start.3 = (f32[2,128,128]{2,1,0:T(8,128)S(1)}, f32[2,128,128]{2,1,0:T(8,128)S(1)}, u32[]{:S(2)}, u32[]{:S(2)}) collective-permute-start(f32[2,128,128]{2,1,0:T(8,128)S(1)} %pad_maximum_fusion.7), channel_id=1, source_target_pairs={{0,64},{4,20},{8,72},{12,28},{16,80},{20,36},{24,88},{28,44},{32,9... | collective-permute-start | bytes 393224 | tf_op jit(solution)/shard_map/ppermute | solution.py:46
  18.0 5.0 %collective-permute-start.9 = (f32[2,172,128]{2,1,0:T(8,128)S(1)}, f32[2,172,128]{2,1,0:T(8,128)S(1)}, u32[]{:S(2)}, u32[]{:S(2)}) collective-permute-start(f32[2,172,128]{2,1,0:T(8,128)S(1)} %pad_maximum_fusion.5.near), channel_id=1, source_target_pairs={{0,1},{1,0},{2,3},{3,2},{4,5},{5,4},{6,7},{7,6},{8,9},{9,8},{10,11... | collective-permute-start | bytes 528392 | tf_op jit(solution)/shard_map/ppermute | solution.py:56
  23.0 1.6 copy-start
  27.0 6.8 %collective-permute-start.10 = (f32[32,176,128]{2,1,0:T(8,128)S(1)}, f32[32,176,128]{2,1,0:T(8,128)S(1)}, u32[]{:S(2)}, u32[]{:S(2)}) collective-permute-start(f32[32,176,128]{2,1,0:T(8,128)S(1)} %get-tuple-element.38), channel_id=1, source_target_pairs={{0,4},{4,0},{8,12},{12,8},{16,20},{20,16},{24,28},{28,24},{32,36},... | collective-permute-start | bytes 8650760 | tf_op jit(solution)/shard_map/ppermute | solution.py:38
  28.9 14.5 %collective-permute-start.4 = (f32[8,128,128]{2,1,0:T(8,128)S(1)}, f32[8,128,128]{2,1,0:T(8,128)S(1)}, u32[]{:S(2)}, u32[]{:S(2)}) collective-permute-start(f32[8,128,128]{2,1,0:T(8,128)S(1)} %pad_maximum_fusion.3.rest_0_), channel_id=1, source_target_pairs={{0,48},{4,196},{8,56},{12,204},{16,0},{20,212},{24,8},{28,220},{32... | collective-permute-start | bytes 1572872 | tf_op jit(solution)/shard_map/ppermute | solution.py:46
  31.6 11.7 %collective-permute-start.5 = (f32[8,128,128]{2,1,0:T(8,128)S(1)}, f32[8,128,128]{2,1,0:T(8,128)S(1)}, u32[]{:S(2)}, u32[]{:S(2)}) collective-permute-start(f32[8,128,128]{2,1,0:T(8,128)S(1)} %pad_maximum_fusion.3.rest_0_), channel_id=1, source_target_pairs={{0,32},{4,132},{8,40},{12,140},{16,48},{20,148},{24,56},{28,156},{... | collective-permute-start | bytes 1572872 | tf_op jit(solution)/shard_map/ppermute | solution.py:46
  32.1 14.9 %collective-permute-start.6 = (f32[8,128,128]{2,1,0:T(8,128)S(1)}, f32[8,128,128]{2,1,0:T(8,128)S(1)}, u32[]{:S(2)}, u32[]{:S(2)}) collective-permute-start(f32[8,128,128]{2,1,0:T(8,128)S(1)} %pad_maximum_fusion.3.rest_0_), channel_id=1, source_target_pairs={{0,16},{4,68},{8,24},{12,76},{16,32},{20,84},{24,40},{28,92},{32,4... | collective-permute-start | bytes 1572872 | tf_op jit(solution)/shard_map/ppermute | solution.py:46
  34.2 19.4 %copy-start.1 = (f32[4,1,8,128,128]{4,3,2,1,0:T(8,128)S(1)}, f32[4,1,8,128,128]{4,3,2,1,0:T(8,128)}, u32[]{:S(2)}) copy-start(f32[4,1,8,128,128]{4,3,2,1,0:T(8,128)} %tiles.5) | copy-start | bytes 6291460
  47.2 6.4 %collective-permute-start.11 = (f32[24,128,128]{2,1,0:T(8,128)S(1)}, f32[24,128,128]{2,1,0:T(8,128)S(1)}, u32[]{:S(2)}, u32[]{:S(2)}) collective-permute-start(f32[24,128,128]{2,1,0:T(8,128)S(1)} %pad_maximum_fusion.1), channel_id=1, source_target_pairs={{0,4},{4,0},{8,12},{12,8},{16,20},{20,16},{24,28},{28,24},{32,36},... | collective-permute-start | bytes 4718600 | tf_op jit(solution)/shard_map/ppermute | solution.py:38
  49.0 4.5 %collective-permute-start.7 = (f32[8,128,128]{2,1,0:T(8,128)S(1)}, f32[8,128,128]{2,1,0:T(8,128)S(1)}, u32[]{:S(2)}, u32[]{:S(2)}) collective-permute-start(f32[8,128,128]{2,1,0:T(8,128)S(1)} %pad_maximum_fusion.3.rest_0_), channel_id=1, source_target_pairs={{0,4},{4,0},{8,12},{12,8},{16,20},{20,16},{24,28},{28,24},{32,36},... | collective-permute-start | bytes 1572872 | tf_op jit(solution)/shard_map/ppermute | solution.py:38
  49.1 12.0 %collective-permute-start.19 = (f32[8,176,128]{2,1,0:T(8,128)S(1)}, f32[8,176,128]{2,1,0:T(8,128)S(1)}, u32[]{:S(2)}, u32[]{:S(2)}) collective-permute-start(f32[8,176,128]{2,1,0:T(8,128)S(1)} %get-tuple-element.44), channel_id=1, source_target_pairs={{0,128},{4,36},{8,136},{12,44},{16,144},{20,52},{24,152},{28,60},{... | collective-permute-start | bytes 2162696 | tf_op jit(solution)/shard_map/ppermute | solution.py:46
  50.9 17.9 %collective-permute-start.18 = (f32[8,176,128]{2,1,0:T(8,128)S(1)}, f32[8,176,128]{2,1,0:T(8,128)S(1)}, u32[]{:S(2)}, u32[]{:S(2)}) collective-permute-start(f32[8,176,128]{2,1,0:T(8,128)S(1)} %get-tuple-element.67), channel_id=1, source_target_pairs={{0,64},{4,20},{8,72},{12,28},{16,80},{20,36},{24,88},{28,44},{32,9... | collective-permute-start | bytes 2162696 | tf_op jit(solution)/shard_map/ppermute | solution.py:46
  50.9 17.9 %collective-permute-start.20 = (f32[8,176,128]{2,1,0:T(8,128)S(1)}, f32[8,176,128]{2,1,0:T(8,128)S(1)}, u32[]{:S(2)}, u32[]{:S(2)}) collective-permute-start(f32[8,176,128]{2,1,0:T(8,128)S(1)} %get-tuple-element.65), channel_id=1, source_target_pairs={{0,192},{4,52},{8,200},{12,60},{16,208},{20,4},{24,216},{28,12},{3... | collective-permute-start | bytes 2162696 | tf_op jit(solution)/shard_map/ppermute | solution.py:46
  55.7 13.3 %copy-start.2 = (f32[256,172]{0,1:T(8,128)S(1)}, f32[256,172]{0,1:T(8,128)}, u32[]{:S(2)}) copy-start(f32[256,172]{0,1:T(8,128)} %param.19) | copy-start | bytes 528388
  55.7 13.3 %copy-start.3 = (f32[128,128]{1,0:T(8,128)S(1)}, f32[128,128]{1,0:T(8,128)}, u32[]{:S(2)}) copy-start(f32[128,128]{1,0:T(8,128)} %feat.3) | copy-start | bytes 196612
  55.7 13.3 %copy-start.6 = (f32[128,256]{1,0:T(8,128)S(1)}, f32[128,256]{1,0:T(8,128)}, u32[]{:S(2)}) copy-start(f32[128,256]{1,0:T(8,128)} %self_one.1) | copy-start | bytes 393220
  55.8 13.3 %copy-start.7 = (f32[128,256]{1,0:T(8,128)S(1)}, f32[128,256]{1,0:T(8,128)}, u32[]{:S(2)}) copy-start(f32[128,256]{1,0:T(8,128)} %neigh_one.1) | copy-start | bytes 393220
  55.8 13.3 %copy-start.8 = (f32[256]{0:T(256)S(1)}, f32[256]{0:T(256)}, u32[]{:S(2)}) copy-start(f32[256]{0:T(256)} %param.17) | copy-start | bytes 3076
  55.8 4.4 %collective-permute-start.12 = (f32[2,128,128]{2,1,0:T(8,128)S(1)}, f32[2,128,128]{2,1,0:T(8,128)S(1)}, u32[]{:S(2)}, u32[]{:S(2)}) collective-permute-start(f32[2,128,128]{2,1,0:T(8,128)S(1)} %get-tuple-element.41), channel_id=1, source_target_pairs={{0,1},{1,0},{2,3},{3,2},{4,5},{5,4},{6,7},{7,6},{8,9},{9,8},{10,11... | collective-permute-start | bytes 393224 | tf_op jit(solution)/shard_map/ppermute | solution.py:56
  60.2 8.8 %collective-permute-start.13 = (f32[128,128]{1,0:T(8,128)S(1)}, f32[128,128]{1,0:T(8,128)S(1)}, u32[]{:S(2)}, u32[]{:S(2)}) collective-permute-start(f32[128,128]{1,0:T(8,128)S(1)} %fusion.8), channel_id=1, source_target_pairs={{0,2},{1,3},{2,0},{3,1},{4,6},{5,7},{6,4},{7,5},{8,10},{9,11},{10,... | collective-permute-start | bytes 196616 | tf_op jit(solution)/shard_map/ppermute | solution.py:56
  69.6 22.6 %copy-start.4 = (f32[128,172]{0,1:T(8,128)S(1)}, f32[128,172]{0,1:T(8,128)}, u32[]{:S(2)}) copy-start(f32[128,172]{0,1:T(8,128)} %param.21) | copy-start | bytes 264196
  69.6 22.6 %copy-start.5 = (f32[256,172]{0,1:T(8,128)S(1)}, f32[256,172]{0,1:T(8,128)}, u32[]{:S(2)}) copy-start(f32[256,172]{0,1:T(8,128)} %param.18) | copy-start | bytes 528388
  69.7 22.6 %copy-start.9 = (f32[172]{0:T(256)S(1)}, f32[172]{0:T(256)}, u32[]{:S(2)}) copy-start(f32[172]{0:T(256)} %param.20) | copy-start | bytes 2068
  69.7 9.3 %collective-permute-start.14 = (f32[176,128]{1,0:T(8,128)S(1)}, f32[176,128]{1,0:T(8,128)S(1)}, u32[]{:S(2)}, u32[]{:S(2)}) collective-permute-start(f32[176,128]{1,0:T(8,128)S(1)} %get-tuple-element.42), channel_id=1, source_target_pairs={{0,8},{4,12},{8,0},{12,4},{16,24},{20,28},{24,16},{28,20},{32,40},... | collective-permute-start | bytes 270344 | tf_op jit(solution)/shard_map/ppermute | solution.py:42
  75.4 5.6 %collective-permute-start.21 = (f32[2,176,128]{2,1,0:T(8,128)S(1)}, f32[2,176,128]{2,1,0:T(8,128)S(1)}, u32[]{:S(2)}, u32[]{:S(2)}) collective-permute-start(f32[2,176,128]{2,1,0:T(8,128)S(1)} %get-tuple-element.71), channel_id=1, source_target_pairs={{0,16},{4,68},{8,24},{12,76},{16,32},{20,84},{24,40},{28,92},{32,4... | collective-permute-start | bytes 540680 | tf_op jit(solution)/shard_map/ppermute | solution.py:46
  76.4 7.1 %collective-permute-start.22 = (f32[2,176,128]{2,1,0:T(8,128)S(1)}, f32[2,176,128]{2,1,0:T(8,128)S(1)}, u32[]{:S(2)}, u32[]{:S(2)}) collective-permute-start(f32[2,176,128]{2,1,0:T(8,128)S(1)} %get-tuple-element.70), channel_id=1, source_target_pairs={{0,32},{4,132},{8,40},{12,140},{16,48},{20,148},{24,56},{28,156},{... | collective-permute-start | bytes 540680 | tf_op jit(solution)/shard_map/ppermute | solution.py:46
  78.5 5.4 %collective-permute-start.23 = (f32[2,176,128]{2,1,0:T(8,128)S(1)}, f32[2,176,128]{2,1,0:T(8,128)S(1)}, u32[]{:S(2)}, u32[]{:S(2)}) collective-permute-start(f32[2,176,128]{2,1,0:T(8,128)S(1)} %get-tuple-element.69), channel_id=1, source_target_pairs={{0,48},{4,196},{8,56},{12,204},{16,0},{20,212},{24,8},{28,220},{32... | collective-permute-start | bytes 540680 | tf_op jit(solution)/shard_map/ppermute | solution.py:46
  78.9 6.8 %collective-permute-start.15 = (f32[2,176,128]{2,1,0:T(8,128)S(1)}, f32[2,176,128]{2,1,0:T(8,128)S(1)}, u32[]{:S(2)}, u32[]{:S(2)}) collective-permute-start(f32[2,176,128]{2,1,0:T(8,128)S(1)} %pad_maximum_fusion.6), channel_id=1, source_target_pairs={{0,192},{4,52},{8,200},{12,60},{16,208},{20,4},{24,216},{28,12},{3... | collective-permute-start | bytes 540680 | tf_op jit(solution)/shard_map/ppermute | solution.py:46
  79.6 6.3 %collective-permute-start.16 = (f32[2,176,128]{2,1,0:T(8,128)S(1)}, f32[2,176,128]{2,1,0:T(8,128)S(1)}, u32[]{:S(2)}, u32[]{:S(2)}) collective-permute-start(f32[2,176,128]{2,1,0:T(8,128)S(1)} %pad_maximum_fusion.6), channel_id=1, source_target_pairs={{0,128},{4,36},{8,136},{12,44},{16,144},{20,52},{24,152},{28,60},{... | collective-permute-start | bytes 540680 | tf_op jit(solution)/shard_map/ppermute | solution.py:46
  81.0 8.1 %collective-permute-start.17 = (f32[2,176,128]{2,1,0:T(8,128)S(1)}, f32[2,176,128]{2,1,0:T(8,128)S(1)}, u32[]{:S(2)}, u32[]{:S(2)}) collective-permute-start(f32[2,176,128]{2,1,0:T(8,128)S(1)} %pad_maximum_fusion.6), channel_id=1, source_target_pairs={{0,64},{4,20},{8,72},{12,28},{16,80},{20,36},{24,88},{28,44},{32,9... | collective-permute-start | bytes 540680 | tf_op jit(solution)/shard_map/ppermute | solution.py:46
  83.9 8.3 %collective-permute-start.24 = (f32[176,128]{1,0:T(8,128)S(1)}, f32[176,128]{1,0:T(8,128)S(1)}, u32[]{:S(2)}, u32[]{:S(2)}) collective-permute-start(f32[176,128]{1,0:T(8,128)S(1)} %get-tuple-element.75), channel_id=1, source_target_pairs={{0,8},{4,12},{8,0},{12,4},{16,24},{20,28},{24,16},{28,20},{32,40},... | collective-permute-start | bytes 270344 | tf_op jit(solution)/shard_map/ppermute | solution.py:42
  93.8 10.0 %collective-permute-start.29 = (f32[4,160,128]{2,1,0:T(8,128)S(1)}, f32[4,160,128]{2,1,0:T(8,128)S(1)}, u32[]{:S(2)}, u32[]{:S(2)}) collective-permute-start(f32[4,160,128]{2,1,0:T(8,128)S(1)} %get-tuple-element.50), channel_id=1, source_target_pairs={{0,4},{4,0},{8,12},{12,8},{16,20},{20,16},{24,28},{28,24},{32,36},... | collective-permute-start | bytes 983048 | tf_op jit(solution)/shard_map/ppermute | solution.py:38
  100.3 25.3 %collective-permute-start.25 = (f32[8,176,128]{2,1,0:T(8,128)S(1)}, f32[8,176,128]{2,1,0:T(8,128)S(1)}, u32[]{:S(2)}, u32[]{:S(2)}) collective-permute-start(f32[8,176,128]{2,1,0:T(8,128)S(1)} %pad_maximum_fusion.2.rest_0_), channel_id=1, source_target_pairs={{0,48},{4,196},{8,56},{12,204},{16,0},{20,212},{24,8},{28,220},{32... | collective-permute-start | bytes 2162696 | tf_op jit(solution)/shard_map/ppermute | solution.py:46
  101.7 24.0 %collective-permute-start.26 = (f32[8,176,128]{2,1,0:T(8,128)S(1)}, f32[8,176,128]{2,1,0:T(8,128)S(1)}, u32[]{:S(2)}, u32[]{:S(2)}) collective-permute-start(f32[8,176,128]{2,1,0:T(8,128)S(1)} %pad_maximum_fusion.2.rest_0_), channel_id=1, source_target_pairs={{0,32},{4,132},{8,40},{12,140},{16,48},{20,148},{24,56},{28,156},{... | collective-permute-start | bytes 2162696 | tf_op jit(solution)/shard_map/ppermute | solution.py:46
  103.8 21.9 %collective-permute-start.27 = (f32[8,176,128]{2,1,0:T(8,128)S(1)}, f32[8,176,128]{2,1,0:T(8,128)S(1)}, u32[]{:S(2)}, u32[]{:S(2)}) collective-permute-start(f32[8,176,128]{2,1,0:T(8,128)S(1)} %pad_maximum_fusion.2.rest_0_), channel_id=1, source_target_pairs={{0,16},{4,68},{8,24},{12,76},{16,32},{20,84},{24,40},{28,92},{32,4... | collective-permute-start | bytes 2162696 | tf_op jit(solution)/shard_map/ppermute | solution.py:46
  103.9 13.8 %collective-permute-start.30 = (f32[160,128]{1,0:T(8,128)S(1)}, f32[160,128]{1,0:T(8,128)S(1)}, u32[]{:S(2)}, u32[]{:S(2)}) collective-permute-start(f32[160,128]{1,0:T(8,128)S(1)} %get-tuple-element.74), channel_id=1, source_target_pairs={{0,64},{4,20},{8,72},{12,28},{16,80},{20,36},{24,88},{28,44},{32,9... | collective-permute-start | bytes 245768 | tf_op jit(solution)/shard_map/ppermute | solution.py:46
  103.9 13.7 %collective-permute-start.31 = (f32[160,128]{1,0:T(8,128)S(1)}, f32[160,128]{1,0:T(8,128)S(1)}, u32[]{:S(2)}, u32[]{:S(2)}) collective-permute-start(f32[160,128]{1,0:T(8,128)S(1)} %get-tuple-element.73), channel_id=1, source_target_pairs={{0,128},{4,36},{8,136},{12,44},{16,144},{20,52},{24,152},{28,60},{... | collective-permute-start | bytes 245768 | tf_op jit(solution)/shard_map/ppermute | solution.py:46
  117.6 3.6 %collective-permute-start.32 = (f32[160,128]{1,0:T(8,128)S(1)}, f32[160,128]{1,0:T(8,128)S(1)}, u32[]{:S(2)}, u32[]{:S(2)}) collective-permute-start(f32[160,128]{1,0:T(8,128)S(1)} %get-tuple-element.72), channel_id=1, source_target_pairs={{0,192},{4,52},{8,200},{12,60},{16,208},{20,4},{24,216},{28,12},{3... | collective-permute-start | bytes 245768 | tf_op jit(solution)/shard_map/ppermute | solution.py:46
  121.2 4.4 %collective-permute-start.33 = (f32[160,128]{1,0:T(8,128)S(1)}, f32[160,128]{1,0:T(8,128)S(1)}, u32[]{:S(2)}, u32[]{:S(2)}) collective-permute-start(f32[160,128]{1,0:T(8,128)S(1)} %fusion.7), channel_id=1, source_target_pairs={{0,1},{1,0},{2,3},{3,2},{4,5},{5,4},{6,7},{7,6},{8,9},{9,8},{10,11... | collective-permute-start | bytes 245768 | tf_op jit(solution)/shard_map/ppermute | solution.py:56
  125.9 5.6 %collective-permute-start.34 = (f32[24,176,128]{2,1,0:T(8,128)S(1)}, f32[24,176,128]{2,1,0:T(8,128)S(1)}, u32[]{:S(2)}, u32[]{:S(2)}) collective-permute-start(f32[24,176,128]{2,1,0:T(8,128)S(1)} %pad_maximum_fusion), channel_id=1, source_target_pairs={{0,4},{4,0},{8,12},{12,8},{16,20},{20,16},{24,28},{28,24},{32,36},... | collective-permute-start | bytes 6488072 | tf_op jit(solution)/shard_map/ppermute | solution.py:38
  126.7 4.9 %collective-permute-start.28 = (f32[8,176,128]{2,1,0:T(8,128)S(1)}, f32[8,176,128]{2,1,0:T(8,128)S(1)}, u32[]{:S(2)}, u32[]{:S(2)}) collective-permute-start(f32[8,176,128]{2,1,0:T(8,128)S(1)} %pad_maximum_fusion.2.rest_0_), channel_id=1, source_target_pairs={{0,4},{4,0},{8,12},{12,8},{16,20},{20,16},{24,28},{28,24},{32,36},... | collective-permute-start | bytes 2162696 | tf_op jit(solution)/shard_map/ppermute | solution.py:38
  126.8 4.5 %collective-permute-start.35 = (f32[160,128]{1,0:T(8,128)S(1)}, f32[160,128]{1,0:T(8,128)S(1)}, u32[]{:S(2)}, u32[]{:S(2)}) collective-permute-start(f32[160,128]{1,0:T(8,128)S(1)} %add.116), channel_id=1, source_target_pairs={{0,2},{1,3},{2,0},{3,1},{4,6},{5,7},{6,4},{7,5},{8,10},{9,11},{10,... | collective-permute-start | bytes 245768 | tf_op jit(solution)/shard_map/ppermute | solution.py:56
  131.3 7.3 %collective-permute-start.38 = (f32[160,128]{1,0:T(8,128)S(1)}, f32[160,128]{1,0:T(8,128)S(1)}, u32[]{:S(2)}, u32[]{:S(2)}) collective-permute-start(f32[160,128]{1,0:T(8,128)S(1)} %add.117), channel_id=1, source_target_pairs={{0,8},{4,12},{8,0},{12,4},{16,24},{20,28},{24,16},{28,20},{32,40},... | collective-permute-start | bytes 245768 | tf_op jit(solution)/shard_map/ppermute | solution.py:42
  138.6 6.3 %collective-permute-start.39 = (f32[160,128]{1,0:T(8,128)S(1)}, f32[160,128]{1,0:T(8,128)S(1)}, u32[]{:S(2)}, u32[]{:S(2)}) collective-permute-start(f32[160,128]{1,0:T(8,128)S(1)} %add.120), channel_id=1, source_target_pairs={{0,16},{4,68},{8,24},{12,76},{16,32},{20,84},{24,40},{28,92},{32,4... | collective-permute-start | bytes 245768 | tf_op jit(solution)/shard_map/ppermute | solution.py:46
  142.4 4.8 %collective-permute-start.40 = (f32[160,128]{1,0:T(8,128)S(1)}, f32[160,128]{1,0:T(8,128)S(1)}, u32[]{:S(2)}, u32[]{:S(2)}) collective-permute-start(f32[160,128]{1,0:T(8,128)S(1)} %add.120), channel_id=1, source_target_pairs={{0,32},{4,132},{8,40},{12,140},{16,48},{20,148},{24,56},{28,156},{... | collective-permute-start | bytes 245768 | tf_op jit(solution)/shard_map/ppermute | solution.py:46
  142.4 4.8 %collective-permute-start.41 = (f32[160,128]{1,0:T(8,128)S(1)}, f32[160,128]{1,0:T(8,128)S(1)}, u32[]{:S(2)}, u32[]{:S(2)}) collective-permute-start(f32[160,128]{1,0:T(8,128)S(1)} %add.120), channel_id=1, source_target_pairs={{0,48},{4,196},{8,56},{12,204},{16,0},{20,212},{24,8},{28,220},{32... | collective-permute-start | bytes 245768 | tf_op jit(solution)/shard_map/ppermute | solution.py:46
  144.9 4.8 %collective-permute-start.36 = (f32[2,176,128]{2,1,0:T(8,128)S(1)}, f32[2,176,128]{2,1,0:T(8,128)S(1)}, u32[]{:S(2)}, u32[]{:S(2)}) collective-permute-start(f32[2,176,128]{2,1,0:T(8,128)S(1)} %get-tuple-element.54), channel_id=1, source_target_pairs={{0,1},{1,0},{2,3},{3,2},{4,5},{5,4},{6,7},{7,6},{8,9},{9,8},{10,11... | collective-permute-start | bytes 540680 | tf_op jit(solution)/shard_map/ppermute | solution.py:56
  149.7 4.5 %collective-permute-start.42 = (f32[160,128]{1,0:T(8,128)S(1)}, f32[160,128]{1,0:T(8,128)S(1)}, u32[]{:S(2)}, u32[]{:S(2)}) collective-permute-start(f32[160,128]{1,0:T(8,128)S(1)} %add_add_fusion.1), channel_id=1, source_target_pairs={{0,192},{4,52},{8,200},{12,60},{16,208},{20,4},{24,216},{28,12},{3... | collective-permute-start | bytes 245768 | tf_op jit(solution)/shard_map/ppermute | solution.py:46
  151.5 4.9 %collective-permute-start.43 = (f32[160,128]{1,0:T(8,128)S(1)}, f32[160,128]{1,0:T(8,128)S(1)}, u32[]{:S(2)}, u32[]{:S(2)}) collective-permute-start(f32[160,128]{1,0:T(8,128)S(1)} %add_add_fusion.1), channel_id=1, source_target_pairs={{0,128},{4,36},{8,136},{12,44},{16,144},{20,52},{24,152},{28,60},{... | collective-permute-start | bytes 245768 | tf_op jit(solution)/shard_map/ppermute | solution.py:46
  151.5 5.4 %collective-permute-start.44 = (f32[160,128]{1,0:T(8,128)S(1)}, f32[160,128]{1,0:T(8,128)S(1)}, u32[]{:S(2)}, u32[]{:S(2)}) collective-permute-start(f32[160,128]{1,0:T(8,128)S(1)} %add_add_fusion.1), channel_id=1, source_target_pairs={{0,64},{4,20},{8,72},{12,28},{16,80},{20,36},{24,88},{28,44},{32,9... | collective-permute-start | bytes 245768 | tf_op jit(solution)/shard_map/ppermute | solution.py:46
  152.1 4.8 %collective-permute-start.37 = (f32[176,128]{1,0:T(8,128)S(1)}, f32[176,128]{1,0:T(8,128)S(1)}, u32[]{:S(2)}, u32[]{:S(2)}) collective-permute-start(f32[176,128]{1,0:T(8,128)S(1)} %fusion.1), channel_id=1, source_target_pairs={{0,2},{1,3},{2,0},{3,1},{4,6},{5,7},{6,4},{7,5},{8,10},{9,11},{10,... | collective-permute-start | bytes 270344 | tf_op jit(solution)/shard_map/ppermute | solution.py:56
  156.9 6.1 %collective-permute-start.45 = (f32[4,160,128]{2,1,0:T(8,128)S(1)}, f32[4,160,128]{2,1,0:T(8,128)S(1)}, u32[]{:S(2)}, u32[]{:S(2)}) collective-permute-start(f32[4,160,128]{2,1,0:T(8,128)S(1)} %pad_maximum_fusion.4.q), channel_id=1, source_target_pairs={{0,4},{4,0},{8,12},{12,8},{16,20},{20,16},{24,28},{28,24},{32,36},... | collective-permute-start | bytes 983048 | tf_op jit(solution)/shard_map/ppermute | solution.py:38

commit v2 on v1

--- a/solution.py
+++ b/solution.py
@@ -16,7 +16,6 @@
 VMEM = pl.BlockSpec(memory_space=pltpu.VMEM)
 SMEM = pl.BlockSpec(memory_space=pltpu.SMEM)
 ANY = pl.BlockSpec(memory_space=pl.ANY)
-HBM = pl.BlockSpec(memory_space=pltpu.HBM)
 MIB = 1024 * 1024
 COUNTS, ME, REP = 32, 36, 37
 
@@ -79,8 +78,8 @@
     return jnp.concatenate([w, w], axis=0)
 
 
-def twice_t(a):
-    h, l = split(a)
+def twice_t(w):
+    h, l = w[:, :SIDE], w[:, SIDE:]
     return jnp.concatenate(
         [jnp.concatenate([h, h], axis=1), jnp.concatenate([l, l], axis=1)], axis=0
     )
@@ -100,13 +99,15 @@
     return d1, d2, (diff >> 1) & 1, diff & 1
 
 
-def live_tile(tile_buf, meta, block, s):
-    t = tile_buf[block, 0, s]
-    return jnp.where(s < meta[COUNTS + block], t, jnp.zeros_like(t))
-
-
-def start_loads(refs, buf, tiles, tile_buf, sems):
-    copies = [pltpu.make_async_copy(tiles, tile_buf, sems.at[len(refs)])]
+def stage_kernel(meta, tiles, out):
+    for block in range(4):
+        for k in range(8):
+            t = tiles[block, 0, k]
+            out[block, k] = wide(jnp.where(k < meta[COUNTS + block], t, jnp.zeros_like(t)))
+
+
+def load_pieces(refs, buf, sems):
+    copies = []
     start = 0
     for k, ref in enumerate(refs):
         size = ref.shape[0]
@@ -119,9 +120,9 @@
 
 
 def agg_kernel(second, meta, tiles, *rest):
-    refs, outs, (buf, tile_buf, sems) = rest[:6], rest[6:8], rest[8:]
+    refs, outs, (buf, sems) = rest[:6], rest[6:8], rest[8:]
     me, rep = meta[ME], meta[REP]
-    start_loads(refs, buf, tiles, tile_buf, sems)
+    load_pieces(refs, buf, sems)
     rows = buf.shape[1]
     for d in range(NR):
         block = rep ^ d
@@ -131,27 +132,24 @@
                 s = 2 * i + u
                 d1, d2, dz, dc = relative(meta[block * 8 + s], me)
                 piece = buf[((dc * 4 + d2) * 4 + d1) * 2 + dz]
-                tile = live_tile(tile_buf, meta, block, s)
+                tile = tiles[block, s]
                 if second:
                     dn = (((1,), (1,)), ((), ()))
                     acc += lax.dot_general(
                         wide(piece), twice_t(tile), dn, preferred_element_type=F32
                     )
                 else:
-                    acc += jnp.dot(wide(tile), twice(piece), preferred_element_type=F32)
+                    acc += jnp.dot(tile, twice(piece), preferred_element_type=F32)
             return acc
 
         pairs = (meta[COUNTS + block] + 1) >> 1
         outs[d & 1][d >> 1] = fold(lax.fori_loop(0, pairs, step, jnp.zeros((rows, 256), F32)))
 
 
-def transposed_kernel(meta, tiles, near, far, own, oth, tile_buf, ct_buf, sem):
+def transposed_kernel(meta, tiles, near, far, own, oth, ct_buf):
     me, rep = meta[ME], meta[REP]
-    copy = pltpu.make_async_copy(tiles, tile_buf, sem)
-    copy.start()
     for o in (own, oth):
         o[...] = jnp.zeros(o.shape, F32)
-    copy.wait()
     for d in range(NR):
         block = rep ^ d
         ct_buf[...] = jnp.concatenate(
@@ -162,10 +160,8 @@
             done = []
             for u in range(2):
                 s = 2 * i + u
-                tile = live_tile(tile_buf, meta, block, s)
-                done.append(
-                    (s, fold(jnp.dot(ct_buf[...], twice(tile), preferred_element_type=F32)))
-                )
+                tile = jnp.concatenate([tiles[block, s]] * 2, axis=0)
+                done.append((s, fold(jnp.dot(ct_buf[...], tile, preferred_element_type=F32))))
             for s, r in done:
                 d1, d2, dz, dc = relative(meta[block * 8 + s], me)
                 at = (d1 * 4 + d2) * 2 + dz
@@ -257,15 +253,13 @@
     out[...] = base[...] + ((kept[0, part] + got[0, part]) + last[part])
 
 
-def call(kernel, outs, ins, scratch=(), smem=0, in_hbm=(), in_any=(), mib=8, cost=6):
+def call(kernel, outs, ins, scratch=(), smem=0, in_any=(), mib=8, cost=6, dtype=F32):
     specs = [SMEM] * smem + [VMEM] * (len(ins) - smem)
     for k in in_any:
         specs[k] = ANY
-    for k in in_hbm:
-        specs[k] = HBM
     return pl.pallas_call(
         kernel,
-        out_shape=[jax.ShapeDtypeStruct(s, F32) for s in outs],
+        out_shape=[jax.ShapeDtypeStruct(s, dtype) for s in outs],
         in_specs=specs,
         out_specs=[VMEM] * len(outs),
         scratch_shapes=list(scratch),
@@ -342,10 +336,9 @@
         functools.partial(agg_kernel, second), [(2,) + shape] * 2, head + tuple(pieces),
         scratch=(
             pltpu.VMEM((64, rows, SIDE), F32),
-            pltpu.VMEM((4, 1, 8, SIDE, SIDE), F32),
-            pltpu.SemaphoreType.DMA((7,)),
+            pltpu.SemaphoreType.DMA((6,)),
         ),
-        smem=1, in_hbm=(1,), in_any=range(2, 8), mib=16, cost=12,
+        smem=1, in_any=range(2, 8), mib=16, cost=12,
     )
 
 
@@ -364,7 +357,10 @@
 ):
     place = jnp.stack([lax.axis_index("row"), lax.axis_index("rep")]).astype(jnp.int32)
     meta = jnp.concatenate([columns.reshape(-1), counts.reshape(-1), place])
-    head = (meta, tiles)
+    (staged,) = call(
+        stage_kernel, [(4, 8, SIDE, 256)], (meta, tiles), smem=1, dtype=jnp.bfloat16
+    )
+    head = (meta, staged)
     block = (SIDE, SIDE)
     tall, padded = (CLS, SIDE), (CP, SIDE)
     ct, st, nt = cotangent.T, self_two.T, neigh_two.T
@@ -372,15 +368,10 @@
     swapped = send_z(features)
     pair = jnp.stack([ct, swap_rep(ct, 2)])
     far = swap_rep(pair, 1)
-    lane = gather_lane(features, swapped)
+    lane = gather_lane(features, swapped, staged)
     own, oth = call(
         transposed_kernel, [(32,) + padded] * 2, head + (after(pair, lane), far),
-        scratch=(
-            pltpu.VMEM((4, 1, 8, SIDE, SIDE), F32),
-            pltpu.VMEM((CP, 256), jnp.bfloat16),
-            pltpu.SemaphoreType.DMA(()),
-        ),
-        smem=1, in_hbm=(1,), mib=16, cost=12,
+        scratch=(pltpu.VMEM((CP, 256), jnp.bfloat16),), smem=1, mib=16, cost=12,
     )
     plane = gather_plane(lane)
     parts = scatter_core(own, oth)
@@ -403,7 +394,7 @@
         (meta, g, gz, after(pre, lane), sums, features, ct, st, nt, bias_two.reshape(1, -1)),
         scratch=(pltpu.VMEM((GROWS, SIDE), F32),), smem=1,
     )
-    plane = gather_plane(after(lane, same))
+    plane = gather_ring(after(lane, gz))
     kept = reduce_lane(same, other)
     kept = kept + swap_rep(kept, 1)
     pieces = gather_core(plane, kept)

time: 165 us -> 160 us (0.970)
  waiting for transfers between devices: 72.7 us -> 58.7 us
  starting transfers between devices: 71 us -> 79.9 us
  Pallas kernels: 12.4 us -> 14.2 us
  other arithmetic: 5.01 us -> 3.26 us
    ppermute x27 -> x28, waiting for transfers between devices: 49.9 us -> 34.1 us  [send_plane(): lax.ppermute(a, 'row', row_perm(lambda c: (d, 0, 0, 0) if c == stage else...]
    ppermute x8, starting transfers between devices: 6.52 us -> 12 us  [swap_rep(): return lax.ppermute(a, 'rep', [(j, j ^ bit) for j in range(NR)])]
    ppermute x7, starting transfers between devices: 16.1 us -> 21 us  [send_core(): return lax.ppermute(a, 'row', row_perm(lambda c: (0, 0, 0, 1)))]
    ppermute x7, waiting for transfers between devices: 1.74 us -> 5.31 us  [send_core(): return lax.ppermute(a, 'row', row_perm(lambda c: (0, 0, 0, 1)))]
    pallas_call x7 -> x8, Pallas kernels: 12.4 us -> 14.2 us  [call(): pl.pallas_call(kernel, out_shape=[jax.ShapeDtypeStruct(s, dtype) for s in...]
    ppermute x27 -> x28, starting transfers between devices: 32.8 us -> 31.4 us  [send_plane(): lax.ppermute(a, 'row', row_perm(lambda c: (d, 0, 0, 0) if c == stage else...]
  transfers between devices with their start and end apart: 46 -> 47, of which waited for: 27 -> 26; matrix products, arithmetic and copies ran while one was open for 3% -> 2% of each run, Pallas kernels for 4% -> 6%
where the time goes in v2:
time: 160 us; the launch traced here: 159 us
  starting transfers between devices  79.9 us (50%)
  waiting for transfers between devices  58.7 us (37%)
  Pallas kernels  14.2 us (9%)
  other arithmetic  3.26 us (2%)
  local copies, waits for them, and re-layouts  2.37 us (1%)
    ppermute x28, waiting for transfers between devices, send_plane(): lax.ppermute(a, 'row', row_perm(lambda c: (d, 0, 0, 0) if c == stage else...  34.1 us
    ppermute x28, starting transfers between devices, send_plane(): lax.ppermute(a, 'row', row_perm(lambda c: (d, 0, 0, 0) if c == stage else...  31.4 us
    ppermute x7, starting transfers between devices, send_core(): return lax.ppermute(a, 'row', row_perm(lambda c: (0, 0, 0, 1)))  21 us
    ppermute x4, starting transfers between devices, send_z(): return lax.ppermute(a, 'row', row_perm(lambda c: (0, 0, 1, 0)))  15.6 us
    ppermute x8, waiting for transfers between devices, swap_rep(): return lax.ppermute(a, 'rep', [(j, j ^ bit) for j in range(NR)])  14.2 us
    pallas_call x8, Pallas kernels, call(): pl.pallas_call(kernel, out_shape=[jax.ShapeDtypeStruct(s, dtype) for s in...  14.2 us
    ppermute x8, starting transfers between devices, swap_rep(): return lax.ppermute(a, 'rep', [(j, j ^ bit) for j in range(NR)])  12 us
    ppermute x7, waiting for transfers between devices, send_core(): return lax.ppermute(a, 'row', row_perm(lambda c: (0, 0, 0, 1)))  5.31 us
  transfers between devices with their start and end apart: 47, of which 26 were waited for; matrix products, arithmetic and copies ran while one was open for 2% of the time, Pallas kernels for 6%

profile of v2, /device:TPU:1, one launch (start us, length us, event | category | flops | bytes accessed | tf_op | source)
XLA Modules:
  0.0 159.4 jit_solution(9980520302574086006)
XLA Ops:
  0.6 7.8 %collective-permute-start = (f32[128,128]{1,0:T(8,128)}, f32[128,128]{1,0:T(8,128)S(1)}, u32[]{:S(2)}, u32[]{:S(2)}) collective-permute-start(f32[128,128]{1,0:T(8,128)} %feat.3), channel_id=1, source_target_pairs={{0,8},{4,12},{8,0},{12,4},{16,24},{20,28},{24,16},{28,20},{32,40},... | collective-permute-start | bytes 196616 | tf_op jit(solution)/shard_map/ppermute | solution.py:41
  8.5 1.2 collective-permute-start.8
  10.2 1.3 reduce.3
  11.6 0.7 pad_add_fusion.meta
  12.3 1.6 copy-done
  13.9 0.8 shard_map.162.tiles
  14.8 2.8 %collective-permute-start.1 = (f32[2,128,128]{2,1,0:T(8,128)S(1)}, f32[2,128,128]{2,1,0:T(8,128)S(1)}, u32[]{:S(2)}, u32[]{:S(2)}) collective-permute-start(f32[2,128,128]{2,1,0:T(8,128)S(1)} %pad_maximum_fusion.7), channel_id=1, source_target_pairs={{0,192},{4,52},{8,200},{12,60},{16,208},{20,4},{24,216},{28,12},{3... | collective-permute-start | bytes 393224 | tf_op jit(solution)/shard_map/ppermute | solution.py:45
  18.0 0.7 collective-permute-start.3
  18.8 0.8 collective-permute-start.9
  19.6 1.3 collective-permute-done.1
  20.9 2.2 %collective-permute-done.2 = f32[2,128,128]{2,1,0:T(8,128)S(1)} collective-permute-done((f32[2,128,128]{2,1,0:T(8,128)S(1)}, f32[2,128,128]{2,1,0:T(8,128)S(1)}, u32[]{:S(2)}, u32[]{:S(2)}) %collective-permute-start.2) | collective-permute-done | bytes 131104 | tf_op jit(solution)/shard_map/ppermute | solution.py:45
  23.1 1.6 collective-permute-done.3
  24.7 2.6 %shard_map.163 = (f32[32,176,128]{2,1,0:T(8,128)S(1)}, f32[32,176,128]{2,1,0:T(8,128)S(1)}) custom-call(s32[38]{0:T(128)S(1)} %pad_add_fusion.meta, bf16[4,8,128,256]{3,2,1,0:T(8,128)(2,1)S(1)} %shard_map.162.tiles, f32[2,172,128]{2,1,0:T(8,128)S(1)} %pad_maximum_fusion.5.near, f32[2,172,128]{2,1,0:T(8,128)S(1)} %collective-permute-done.9.far), custom_call_target="tpu_custom_call" | custom-call | bytes 12582912 | tf_op jit(solution)/shard_map/pallas_call | solution.py:260
  27.4 3.9 %collective-permute-start.10 = (f32[32,176,128]{2,1,0:T(8,128)S(1)}, f32[32,176,128]{2,1,0:T(8,128)S(1)}, u32[]{:S(2)}, u32[]{:S(2)}) collective-permute-start(f32[32,176,128]{2,1,0:T(8,128)S(1)} %get-tuple-element.40), channel_id=1, source_target_pairs={{0,4},{4,0},{8,12},{12,8},{16,20},{20,16},{24,28},{28,24},{32,36},... | collective-permute-start | bytes 8650760 | tf_op jit(solution)/shard_map/ppermute | solution.py:37
  31.8 0.9 collective-permute-start.6
  32.8 3.4 %collective-permute-done.10 = f32[32,176,128]{2,1,0:T(8,128)S(1)} collective-permute-done((f32[32,176,128]{2,1,0:T(8,128)S(1)}, f32[32,176,128]{2,1,0:T(8,128)S(1)}, u32[]{:S(2)}, u32[]{:S(2)}) %collective-permute-start.10) | collective-permute-done | bytes 2883616 | tf_op jit(solution)/shard_map/ppermute | solution.py:37
  36.6 3.0 %collective-permute-done.4.rest_1_ = f32[8,128,128]{2,1,0:T(8,128)S(1)} collective-permute-done((f32[8,128,128]{2,1,0:T(8,128)S(1)}, f32[8,128,128]{2,1,0:T(8,128)S(1)}, u32[]{:S(2)}, u32[]{:S(2)}) %collective-permute-start.4) | collective-permute-done | bytes 524320 | tf_op jit(solution)/shard_map/ppermute | solution.py:45
  39.6 1.6 collective-permute-done.5.rest_2_
  41.2 5.6 %collective-permute-done.6.rest_3_ = f32[8,128,128]{2,1,0:T(8,128)S(1)} collective-permute-done((f32[8,128,128]{2,1,0:T(8,128)S(1)}, f32[8,128,128]{2,1,0:T(8,128)S(1)}, u32[]{:S(2)}, u32[]{:S(2)}) %collective-permute-start.6) | collective-permute-done | bytes 524320 | tf_op jit(solution)/shard_map/ppermute | solution.py:45
  46.9 1.9 %collective-permute-start.11 = (f32[24,128,128]{2,1,0:T(8,128)S(1)}, f32[24,128,128]{2,1,0:T(8,128)S(1)}, u32[]{:S(2)}, u32[]{:S(2)}) collective-permute-start(f32[24,128,128]{2,1,0:T(8,128)S(1)} %pad_maximum_fusion.1), channel_id=1, source_target_pairs={{0,4},{4,0},{8,12},{12,8},{16,20},{20,16},{24,28},{28,24},{32,36},... | collective-permute-start | bytes 4718600 | tf_op jit(solution)/shard_map/ppermute | solution.py:37
  49.5 0.7 collective-permute-start.18
  50.2 2.4 %collective-permute-start.20 = (f32[8,176,128]{2,1,0:T(8,128)S(1)}, f32[8,176,128]{2,1,0:T(8,128)S(1)}, u32[]{:S(2)}, u32[]{:S(2)}) collective-permute-start(f32[8,176,128]{2,1,0:T(8,128)S(1)} %get-tuple-element.67), channel_id=1, source_target_pairs={{0,192},{4,52},{8,200},{12,60},{16,208},{20,4},{24,216},{28,12},{3... | collective-permute-start | bytes 2162696 | tf_op jit(solution)/shard_map/ppermute | solution.py:45
  52.6 2.4 %shard_map.164 = (f32[2,128,128]{2,1,0:T(8,128)S(1)}, f32[2,128,128]{2,1,0:T(8,128)S(1)}) custom-call(s32[38]{0:T(128)S(1)} %pad_add_fusion.meta, bf16[4,8,128,256]{3,2,1,0:T(8,128)(2,1)S(1)} %shard_map.162.tiles, f32[8,128,128]{2,1,0:T(8,128)S(1)} %constant_dynamic-update-slice_fusion.rest_0_, f32[8,128,128]{2,1,0:T(8,128)S(1)} %collective-permute-done.4.rest_1_, ...), custom_call_target="tpu_custom_call" | custom-call | bytes 12582912 | tf_op jit(solution)/shard_map/pallas_call | solution.py:260
  55.4 4.0 %collective-permute-done.12.got = f32[2,128,128]{2,1,0:T(8,128)S(1)} collective-permute-done((f32[2,128,128]{2,1,0:T(8,128)S(1)}, f32[2,128,128]{2,1,0:T(8,128)S(1)}, u32[]{:S(2)}, u32[]{:S(2)}) %collective-permute-start.12) | collective-permute-done | bytes 131104 | tf_op jit(solution)/shard_map/ppermute | solution.py:55
  60.1 0.8 collective-permute-done.19
  60.8 7.7 %collective-permute-done.18 = f32[8,176,128]{2,1,0:T(8,128)S(1)} collective-permute-done((f32[8,176,128]{2,1,0:T(8,128)S(1)}, f32[8,176,128]{2,1,0:T(8,128)S(1)}, u32[]{:S(2)}, u32[]{:S(2)}) %collective-permute-start.18) | collective-permute-done | bytes 720928 | tf_op jit(solution)/shard_map/ppermute | solution.py:45
  69.4 3.1 %collective-permute-start.14 = (f32[176,128]{1,0:T(8,128)S(1)}, f32[176,128]{1,0:T(8,128)S(1)}, u32[]{:S(2)}, u32[]{:S(2)}) collective-permute-start(f32[176,128]{1,0:T(8,128)S(1)} %get-tuple-element.44), channel_id=1, source_target_pairs={{0,8},{4,12},{8,0},{12,4},{16,24},{20,28},{24,16},{28,20},{32,40},... | collective-permute-start | bytes 270344 | tf_op jit(solution)/shard_map/ppermute | solution.py:41
  73.0 2.0 %collective-permute-start.22 = (f32[2,176,128]{2,1,0:T(8,128)S(1)}, f32[2,176,128]{2,1,0:T(8,128)S(1)}, u32[]{:S(2)}, u32[]{:S(2)}) collective-permute-start(f32[2,176,128]{2,1,0:T(8,128)S(1)} %get-tuple-element.72), channel_id=1, source_target_pairs={{0,32},{4,132},{8,40},{12,140},{16,48},{20,148},{24,56},{28,156},{... | collective-permute-start | bytes 540680 | tf_op jit(solution)/shard_map/ppermute | solution.py:45
  75.5 1.4 collective-permute-done.14
  76.9 0.8 collective-permute-start.15
  77.6 4.1 %collective-permute-start.16 = (f32[2,176,128]{2,1,0:T(8,128)S(1)}, f32[2,176,128]{2,1,0:T(8,128)S(1)}, u32[]{:S(2)}, u32[]{:S(2)}) collective-permute-start(f32[2,176,128]{2,1,0:T(8,128)S(1)} %pad_maximum_fusion.6), channel_id=1, source_target_pairs={{0,128},{4,36},{8,136},{12,44},{16,144},{20,52},{24,152},{28,60},{... | collective-permute-start | bytes 540680 | tf_op jit(solution)/shard_map/ppermute | solution.py:45
  81.8 1.7 %collective-permute-start.24 = (f32[176,128]{1,0:T(8,128)S(1)}, f32[176,128]{1,0:T(8,128)S(1)}, u32[]{:S(2)}, u32[]{:S(2)}) collective-permute-start(f32[176,128]{1,0:T(8,128)S(1)} %get-tuple-element.78), channel_id=1, source_target_pairs={{0,8},{4,12},{8,0},{12,4},{16,24},{20,28},{24,16},{28,20},{32,40},... | collective-permute-start | bytes 270344 | tf_op jit(solution)/shard_map/ppermute | solution.py:41
  83.5 1.6 collective-permute-done.15
  85.1 2.5 %collective-permute-done.17 = f32[2,176,128]{2,1,0:T(8,128)S(1)} collective-permute-done((f32[2,176,128]{2,1,0:T(8,128)S(1)}, f32[2,176,128]{2,1,0:T(8,128)S(1)}, u32[]{:S(2)}, u32[]{:S(2)}) %collective-permute-start.17) | collective-permute-done | bytes 180256 | tf_op jit(solution)/shard_map/ppermute | solution.py:45
  87.6 2.5 %collective-permute-done.24.gz = f32[176,128]{1,0:T(8,128)S(1)} collective-permute-done((f32[176,128]{1,0:T(8,128)S(1)}, f32[176,128]{1,0:T(8,128)S(1)}, u32[]{:S(2)}, u32[]{:S(2)}) %collective-permute-start.24) | collective-permute-done | bytes 90144 | tf_op jit(solution)/shard_map/ppermute | solution.py:41
  90.7 0.9 collective-permute-start.27
  91.6 1.5 shard_map.166
  93.1 5.4 %collective-permute-start.30 = (f32[4,160,128]{2,1,0:T(8,128)S(1)}, f32[4,160,128]{2,1,0:T(8,128)S(1)}, u32[]{:S(2)}, u32[]{:S(2)}) collective-permute-start(f32[4,160,128]{2,1,0:T(8,128)S(1)} %get-tuple-element.52), channel_id=1, source_target_pairs={{0,4},{4,0},{8,12},{12,8},{16,20},{20,16},{24,28},{28,24},{32,36},... | collective-permute-start | bytes 983048 | tf_op jit(solution)/shard_map/ppermute | solution.py:37
  98.6 1.3 collective-permute-done.30
  99.9 1.8 %collective-permute-start.31 = (f32[160,128]{1,0:T(8,128)S(1)}, f32[160,128]{1,0:T(8,128)S(1)}, u32[]{:S(2)}, u32[]{:S(2)}) collective-permute-start(f32[160,128]{1,0:T(8,128)S(1)} %get-tuple-element.76), channel_id=1, source_target_pairs={{0,64},{4,20},{8,72},{12,28},{16,80},{20,36},{24,88},{28,44},{32,9... | collective-permute-start | bytes 245768 | tf_op jit(solution)/shard_map/ppermute | solution.py:45
  101.7 2.1 %collective-permute-start.32 = (f32[160,128]{1,0:T(8,128)S(1)}, f32[160,128]{1,0:T(8,128)S(1)}, u32[]{:S(2)}, u32[]{:S(2)}) collective-permute-start(f32[160,128]{1,0:T(8,128)S(1)} %get-tuple-element.75), channel_id=1, source_target_pairs={{0,128},{4,36},{8,136},{12,44},{16,144},{20,52},{24,152},{28,60},{... | collective-permute-start | bytes 245768 | tf_op jit(solution)/shard_map/ppermute | solution.py:45
  103.8 1.4 collective-permute-start.33
  105.2 1.7 %collective-permute-start.26 = (f32[4,176,128]{2,1,0:T(8,128)S(1)}, f32[4,176,128]{2,1,0:T(8,128)S(1)}, u32[]{:S(2)}, u32[]{:S(2)}) collective-permute-start(f32[4,176,128]{2,1,0:T(8,128)S(1)} %slice.122), channel_id=1, source_target_pairs={{0,48},{4,196},{8,56},{12,204},{16,0},{20,212},{24,8},{28,220},{32... | collective-permute-start | bytes 1081352 | tf_op jit(solution)/shard_map/ppermute | solution.py:45
  107.1 1.2 collective-permute-done.32
  108.4 1.0 collective-permute-start.34
  109.3 2.7 %collective-permute-done.34 = f32[160,128]{1,0:T(8,128)S(1)} collective-permute-done((f32[160,128]{1,0:T(8,128)S(1)}, f32[160,128]{1,0:T(8,128)S(1)}, u32[]{:S(2)}, u32[]{:S(2)}) %collective-permute-start.34) | collective-permute-done | bytes 81952 | tf_op jit(solution)/shard_map/ppermute | solution.py:55
  112.5 2.0 %collective-permute-done.28 = f32[4,176,128]{2,1,0:T(8,128)S(1)} collective-permute-done((f32[4,176,128]{2,1,0:T(8,128)S(1)}, f32[4,176,128]{2,1,0:T(8,128)S(1)}, u32[]{:S(2)}, u32[]{:S(2)}) %collective-permute-start.28) | collective-permute-done | bytes 360480 | tf_op jit(solution)/shard_map/ppermute | solution.py:45
  114.6 5.3 %collective-permute-start.35 = (f32[24,176,128]{2,1,0:T(8,128)S(1)}, f32[24,176,128]{2,1,0:T(8,128)S(1)}, u32[]{:S(2)}, u32[]{:S(2)}) collective-permute-start(f32[24,176,128]{2,1,0:T(8,128)S(1)} %pad_maximum_fusion), channel_id=1, source_target_pairs={{0,4},{4,0},{8,12},{12,8},{16,20},{20,16},{24,28},{28,24},{32,36},... | collective-permute-start | bytes 6488072 | tf_op jit(solution)/shard_map/ppermute | solution.py:37
  120.0 3.3 %collective-permute-start.36 = (f32[160,128]{1,0:T(8,128)S(1)}, f32[160,128]{1,0:T(8,128)S(1)}, u32[]{:S(2)}, u32[]{:S(2)}) collective-permute-start(f32[160,128]{1,0:T(8,128)S(1)} %add.116), channel_id=1, source_target_pairs={{0,2},{1,3},{2,0},{3,1},{4,6},{5,7},{6,4},{7,5},{8,10},{9,11},{10,... | collective-permute-start | bytes 245768 | tf_op jit(solution)/shard_map/ppermute | solution.py:55
  123.3 4.2 %collective-permute-done.36 = f32[160,128]{1,0:T(8,128)S(1)} collective-permute-done((f32[160,128]{1,0:T(8,128)S(1)}, f32[160,128]{1,0:T(8,128)S(1)}, u32[]{:S(2)}, u32[]{:S(2)}) %collective-permute-start.36) | collective-permute-done | bytes 81952 | tf_op jit(solution)/shard_map/ppermute | solution.py:55
  127.5 2.9 %collective-permute-start.39 = (f32[160,128]{1,0:T(8,128)S(1)}, f32[160,128]{1,0:T(8,128)S(1)}, u32[]{:S(2)}, u32[]{:S(2)}) collective-permute-start(f32[160,128]{1,0:T(8,128)S(1)} %add.117), channel_id=1, source_target_pairs={{0,8},{4,12},{8,0},{12,4},{16,24},{20,28},{24,16},{28,20},{32,40},... | collective-permute-start | bytes 245768 | tf_op jit(solution)/shard_map/ppermute | solution.py:41
  130.5 4.1 %shard_map.167 = (f32[2,176,128]{2,1,0:T(8,128)S(1)}, f32[2,176,128]{2,1,0:T(8,128)S(1)}) custom-call(s32[38]{0:T(128)S(1)} %pad_add_fusion.meta, bf16[4,8,128,256]{3,2,1,0:T(8,128)(2,1)S(1)} %shard_map.162.tiles, f32[8,176,128]{2,1,0:T(8,128)S(1)} %pad_maximum_fusion.2.rest_0_, f32[8,176,128]{2,1,0:T(8,128)S(1)} %collective-permute-done.25.rest_1_, ...), custom_call_target="tpu_custom_call" | custom-call | bytes 12582912 | tf_op jit(solution)/shard_map/pallas_call | solution.py:260
  134.6 1.2 collective-permute-done.39
  135.9 2.3 %collective-permute-start.41 = (f32[160,128]{1,0:T(8,128)S(1)}, f32[160,128]{1,0:T(8,128)S(1)}, u32[]{:S(2)}, u32[]{:S(2)}) collective-permute-start(f32[160,128]{1,0:T(8,128)S(1)} %add.120), channel_id=1, source_target_pairs={{0,32},{4,132},{8,40},{12,140},{16,48},{20,148},{24,56},{28,156},{... | collective-permute-start | bytes 245768 | tf_op jit(solution)/shard_map/ppermute | solution.py:45
  138.6 0.7 collective-permute-start.37
  139.2 2.0 %collective-permute-done.40 = f32[160,128]{1,0:T(8,128)S(1)} collective-permute-done((f32[160,128]{1,0:T(8,128)S(1)}, f32[160,128]{1,0:T(8,128)S(1)}, u32[]{:S(2)}, u32[]{:S(2)}) %collective-permute-start.40) | collective-permute-done | bytes 81952 | tf_op jit(solution)/shard_map/ppermute | solution.py:45
  141.9 1.3 collective-permute-done.37.got
  143.4 2.0 %collective-permute-start.44 = (f32[160,128]{1,0:T(8,128)S(1)}, f32[160,128]{1,0:T(8,128)S(1)}, u32[]{:S(2)}, u32[]{:S(2)}) collective-permute-start(f32[160,128]{1,0:T(8,128)S(1)} %add_add_fusion.1), channel_id=1, source_target_pairs={{0,128},{4,36},{8,136},{12,44},{16,144},{20,52},{24,152},{28,60},{... | collective-permute-start | bytes 245768 | tf_op jit(solution)/shard_map/ppermute | solution.py:45
  145.4 0.9 collective-permute-start.45
  146.3 4.1 %collective-permute-start.38 = (f32[176,128]{1,0:T(8,128)S(1)}, f32[176,128]{1,0:T(8,128)S(1)}, u32[]{:S(2)}, u32[]{:S(2)}) collective-permute-start(f32[176,128]{1,0:T(8,128)S(1)} %fusion.1), channel_id=1, source_target_pairs={{0,2},{1,3},{2,0},{3,1},{4,6},{5,7},{6,4},{7,5},{8,10},{9,11},{10,... | collective-permute-start | bytes 270344 | tf_op jit(solution)/shard_map/ppermute | solution.py:55
  150.5 1.9 %collective-permute-done.38.last = f32[176,128]{1,0:T(8,128)S(1)} collective-permute-done((f32[176,128]{1,0:T(8,128)S(1)}, f32[176,128]{1,0:T(8,128)S(1)}, u32[]{:S(2)}, u32[]{:S(2)}) %collective-permute-start.38) | collective-permute-done | bytes 90144 | tf_op jit(solution)/shard_map/ppermute | solution.py:55
  152.3 4.4 %collective-permute-start.46 = (f32[4,160,128]{2,1,0:T(8,128)S(1)}, f32[4,160,128]{2,1,0:T(8,128)S(1)}, u32[]{:S(2)}, u32[]{:S(2)}) collective-permute-start(f32[4,160,128]{2,1,0:T(8,128)S(1)} %pad_maximum_fusion.4.q), channel_id=1, source_target_pairs={{0,4},{4,0},{8,12},{12,8},{16,20},{20,16},{24,28},{28,24},{32,36},... | collective-permute-start | bytes 983048 | tf_op jit(solution)/shard_map/ppermute | solution.py:37
  156.7 0.7 shard_map.168
  157.9 1.4 shard_map.169
  (87 shorter events, 9.1 us)
Async XLA Ops:
  0.6 14.1 %collective-permute-start = (f32[128,128]{1,0:T(8,128)}, f32[128,128]{1,0:T(8,128)S(1)}, u32[]{:S(2)}, u32[]{:S(2)}) collective-permute-start(f32[128,128]{1,0:T(8,128)} %feat.3), channel_id=1, source_target_pairs={{0,8},{4,12},{8,0},{12,4},{16,24},{20,28},{24,16},{28,20},{32,40},... | collective-permute-start | bytes 196616 | tf_op jit(solution)/shard_map/ppermute | solution.py:41
  8.5 10.3 %collective-permute-start.8 = (f32[172,128]{1,0:T(8,128)}, f32[172,128]{1,0:T(8,128)S(1)}, u32[]{:S(2)}, u32[]{:S(2)}) collective-permute-start(f32[172,128]{1,0:T(8,128)} %bitcast.47), channel_id=1, source_target_pairs={{0,2},{1,3},{2,0},{3,1},{4,6},{5,7},{6,4},{7,5},{8,10},{9,11},{10,... | collective-permute-start | bytes 264200 | tf_op jit(solution)/shard_map/ppermute | solution.py:55
  12.3 1.6 copy-start
  13.9 0.8 copy-start.2
  13.9 4.8 %copy-start.3 = (f32[128,172]{0,1:T(8,128)S(1)}, f32[128,172]{0,1:T(8,128)}, u32[]{:S(2)}) copy-start(f32[128,172]{0,1:T(8,128)} %param.21) | copy-start | bytes 264196
  14.8 6.1 %collective-permute-start.1 = (f32[2,128,128]{2,1,0:T(8,128)S(1)}, f32[2,128,128]{2,1,0:T(8,128)S(1)}, u32[]{:S(2)}, u32[]{:S(2)}) collective-permute-start(f32[2,128,128]{2,1,0:T(8,128)S(1)} %pad_maximum_fusion.7), channel_id=1, source_target_pairs={{0,192},{4,52},{8,200},{12,60},{16,208},{20,4},{24,216},{28,12},{3... | collective-permute-start | bytes 393224 | tf_op jit(solution)/shard_map/ppermute | solution.py:45
  17.6 5.5 %collective-permute-start.2 = (f32[2,128,128]{2,1,0:T(8,128)S(1)}, f32[2,128,128]{2,1,0:T(8,128)S(1)}, u32[]{:S(2)}, u32[]{:S(2)}) collective-permute-start(f32[2,128,128]{2,1,0:T(8,128)S(1)} %pad_maximum_fusion.7), channel_id=1, source_target_pairs={{0,128},{4,36},{8,136},{12,44},{16,144},{20,52},{24,152},{28,60},{... | collective-permute-start | bytes 393224 | tf_op jit(solution)/shard_map/ppermute | solution.py:45
  18.0 6.7 %collective-permute-start.3 = (f32[2,128,128]{2,1,0:T(8,128)S(1)}, f32[2,128,128]{2,1,0:T(8,128)S(1)}, u32[]{:S(2)}, u32[]{:S(2)}) collective-permute-start(f32[2,128,128]{2,1,0:T(8,128)S(1)} %pad_maximum_fusion.7), channel_id=1, source_target_pairs={{0,64},{4,20},{8,72},{12,28},{16,80},{20,36},{24,88},{28,44},{32,9... | collective-permute-start | bytes 393224 | tf_op jit(solution)/shard_map/ppermute | solution.py:45
  18.8 6.0 %collective-permute-start.9 = (f32[2,172,128]{2,1,0:T(8,128)S(1)}, f32[2,172,128]{2,1,0:T(8,128)S(1)}, u32[]{:S(2)}, u32[]{:S(2)}) collective-permute-start(f32[2,172,128]{2,1,0:T(8,128)S(1)} %pad_maximum_fusion.5.near), channel_id=1, source_target_pairs={{0,1},{1,0},{2,3},{3,2},{4,5},{5,4},{6,7},{7,6},{8,9},{9,8},{10,11... | collective-permute-start | bytes 528392 | tf_op jit(solution)/shard_map/ppermute | solution.py:55
  27.4 8.8 %collective-permute-start.10 = (f32[32,176,128]{2,1,0:T(8,128)S(1)}, f32[32,176,128]{2,1,0:T(8,128)S(1)}, u32[]{:S(2)}, u32[]{:S(2)}) collective-permute-start(f32[32,176,128]{2,1,0:T(8,128)S(1)} %get-tuple-element.40), channel_id=1, source_target_pairs={{0,4},{4,0},{8,12},{12,8},{16,20},{20,16},{24,28},{28,24},{32,36},... | collective-permute-start | bytes 8650760 | tf_op jit(solution)/shard_map/ppermute | solution.py:37
  31.3 8.3 %collective-permute-start.4 = (f32[8,128,128]{2,1,0:T(8,128)S(1)}, f32[8,128,128]{2,1,0:T(8,128)S(1)}, u32[]{:S(2)}, u32[]{:S(2)}) collective-permute-start(f32[8,128,128]{2,1,0:T(8,128)S(1)} %constant_dynamic-update-slice_fusion.rest_0_), channel_id=1, source_target_pairs={{0,48},{4,196},{8,56},{12,204},{16,0},{20,212},{24,8},{28,220},{32... | collective-permute-start | bytes 1572872 | tf_op jit(solution)/shard_map/ppermute | solution.py:45
  31.3 9.9 %collective-permute-start.5 = (f32[8,128,128]{2,1,0:T(8,128)S(1)}, f32[8,128,128]{2,1,0:T(8,128)S(1)}, u32[]{:S(2)}, u32[]{:S(2)}) collective-permute-start(f32[8,128,128]{2,1,0:T(8,128)S(1)} %constant_dynamic-update-slice_fusion.rest_0_), channel_id=1, source_target_pairs={{0,32},{4,132},{8,40},{12,140},{16,48},{20,148},{24,56},{28,156},{... | collective-permute-start | bytes 1572872 | tf_op jit(solution)/shard_map/ppermute | solution.py:45
  31.8 14.9 %collective-permute-start.6 = (f32[8,128,128]{2,1,0:T(8,128)S(1)}, f32[8,128,128]{2,1,0:T(8,128)S(1)}, u32[]{:S(2)}, u32[]{:S(2)}) collective-permute-start(f32[8,128,128]{2,1,0:T(8,128)S(1)} %constant_dynamic-update-slice_fusion.rest_0_), channel_id=1, source_target_pairs={{0,16},{4,68},{8,24},{12,76},{16,32},{20,84},{24,40},{28,92},{32,4... | collective-permute-start | bytes 1572872 | tf_op jit(solution)/shard_map/ppermute | solution.py:45
  46.9 5.7 %collective-permute-start.11 = (f32[24,128,128]{2,1,0:T(8,128)S(1)}, f32[24,128,128]{2,1,0:T(8,128)S(1)}, u32[]{:S(2)}, u32[]{:S(2)}) collective-permute-start(f32[24,128,128]{2,1,0:T(8,128)S(1)} %pad_maximum_fusion.1), channel_id=1, source_target_pairs={{0,4},{4,0},{8,12},{12,8},{16,20},{20,16},{24,28},{28,24},{32,36},... | collective-permute-start | bytes 4718600 | tf_op jit(solution)/shard_map/ppermute | solution.py:37
  48.8 3.8 %collective-permute-start.7 = (f32[8,128,128]{2,1,0:T(8,128)S(1)}, f32[8,128,128]{2,1,0:T(8,128)S(1)}, u32[]{:S(2)}, u32[]{:S(2)}) collective-permute-start(f32[8,128,128]{2,1,0:T(8,128)S(1)} %constant_dynamic-update-slice_fusion.rest_0_), channel_id=1, source_target_pairs={{0,4},{4,0},{8,12},{12,8},{16,20},{20,16},{24,28},{28,24},{32,36},... | collective-permute-start | bytes 1572872 | tf_op jit(solution)/shard_map/ppermute | solution.py:37
  48.9 12.0 %collective-permute-start.19 = (f32[8,176,128]{2,1,0:T(8,128)S(1)}, f32[8,176,128]{2,1,0:T(8,128)S(1)}, u32[]{:S(2)}, u32[]{:S(2)}) collective-permute-start(f32[8,176,128]{2,1,0:T(8,128)S(1)} %get-tuple-element.46), channel_id=1, source_target_pairs={{0,128},{4,36},{8,136},{12,44},{16,144},{20,52},{24,152},{28,60},{... | collective-permute-start | bytes 2162696 | tf_op jit(solution)/shard_map/ppermute | solution.py:45
  49.5 19.1 %collective-permute-start.18 = (f32[8,176,128]{2,1,0:T(8,128)S(1)}, f32[8,176,128]{2,1,0:T(8,128)S(1)}, u32[]{:S(2)}, u32[]{:S(2)}) collective-permute-start(f32[8,176,128]{2,1,0:T(8,128)S(1)} %get-tuple-element.69), channel_id=1, source_target_pairs={{0,64},{4,20},{8,72},{12,28},{16,80},{20,36},{24,88},{28,44},{32,9... | collective-permute-start | bytes 2162696 | tf_op jit(solution)/shard_map/ppermute | solution.py:45
  50.2 18.3 %collective-permute-start.20 = (f32[8,176,128]{2,1,0:T(8,128)S(1)}, f32[8,176,128]{2,1,0:T(8,128)S(1)}, u32[]{:S(2)}, u32[]{:S(2)}) collective-permute-start(f32[8,176,128]{2,1,0:T(8,128)S(1)} %get-tuple-element.67), channel_id=1, source_target_pairs={{0,192},{4,52},{8,200},{12,60},{16,208},{20,4},{24,216},{28,12},{3... | collective-permute-start | bytes 2162696 | tf_op jit(solution)/shard_map/ppermute | solution.py:45
  55.0 13.7 %copy-start.1 = (f32[256,172]{0,1:T(8,128)S(1)}, f32[256,172]{0,1:T(8,128)}, u32[]{:S(2)}) copy-start(f32[256,172]{0,1:T(8,128)} %param.19) | copy-start | bytes 528388
  55.0 13.7 %copy-start.5 = (f32[128,256]{1,0:T(8,128)S(1)}, f32[128,256]{1,0:T(8,128)}, u32[]{:S(2)}) copy-start(f32[128,256]{1,0:T(8,128)} %self_one.1) | copy-start | bytes 393220
  55.0 13.7 %copy-start.6 = (f32[128,256]{1,0:T(8,128)S(1)}, f32[128,256]{1,0:T(8,128)}, u32[]{:S(2)}) copy-start(f32[128,256]{1,0:T(8,128)} %neigh_one.1) | copy-start | bytes 393220
  55.0 13.7 %copy-start.7 = (f32[256]{0:T(256)S(1)}, f32[256]{0:T(256)}, u32[]{:S(2)}) copy-start(f32[256]{0:T(256)} %param.17) | copy-start | bytes 3076
  55.1 4.4 %collective-permute-start.12 = (f32[2,128,128]{2,1,0:T(8,128)S(1)}, f32[2,128,128]{2,1,0:T(8,128)S(1)}, u32[]{:S(2)}, u32[]{:S(2)}) collective-permute-start(f32[2,128,128]{2,1,0:T(8,128)S(1)} %get-tuple-element.43), channel_id=1, source_target_pairs={{0,1},{1,0},{2,3},{3,2},{4,5},{5,4},{6,7},{7,6},{8,9},{9,8},{10,11... | collective-permute-start | bytes 393224 | tf_op jit(solution)/shard_map/ppermute | solution.py:55
  59.4 9.3 %collective-permute-start.13 = (f32[128,128]{1,0:T(8,128)S(1)}, f32[128,128]{1,0:T(8,128)S(1)}, u32[]{:S(2)}, u32[]{:S(2)}) collective-permute-start(f32[128,128]{1,0:T(8,128)S(1)} %fusion.8), channel_id=1, source_target_pairs={{0,2},{1,3},{2,0},{3,1},{4,6},{5,7},{6,4},{7,5},{8,10},{9,11},{10,... | collective-permute-start | bytes 196616 | tf_op jit(solution)/shard_map/ppermute | solution.py:55
  69.3 22.3 %copy-start.4 = (f32[256,172]{0,1:T(8,128)S(1)}, f32[256,172]{0,1:T(8,128)}, u32[]{:S(2)}) copy-start(f32[256,172]{0,1:T(8,128)} %param.18) | copy-start | bytes 528388
  69.4 22.2 %copy-start.8 = (f32[172]{0:T(256)S(1)}, f32[172]{0:T(256)}, u32[]{:S(2)}) copy-start(f32[172]{0:T(256)} %param.20) | copy-start | bytes 2068
  69.4 7.5 %collective-permute-start.14 = (f32[176,128]{1,0:T(8,128)S(1)}, f32[176,128]{1,0:T(8,128)S(1)}, u32[]{:S(2)}, u32[]{:S(2)}) collective-permute-start(f32[176,128]{1,0:T(8,128)S(1)} %get-tuple-element.44), channel_id=1, source_target_pairs={{0,8},{4,12},{8,0},{12,4},{16,24},{20,28},{24,16},{28,20},{32,40},... | collective-permute-start | bytes 270344 | tf_op jit(solution)/shard_map/ppermute | solution.py:41
  72.5 9.2 %collective-permute-start.21 = (f32[2,176,128]{2,1,0:T(8,128)S(1)}, f32[2,176,128]{2,1,0:T(8,128)S(1)}, u32[]{:S(2)}, u32[]{:S(2)}) collective-permute-start(f32[2,176,128]{2,1,0:T(8,128)S(1)} %get-tuple-element.73), channel_id=1, source_target_pairs={{0,16},{4,68},{8,24},{12,76},{16,32},{20,84},{24,40},{28,92},{32,4... | collective-permute-start | bytes 540680 | tf_op jit(solution)/shard_map/ppermute | solution.py:45
  73.0 8.7 %collective-permute-start.22 = (f32[2,176,128]{2,1,0:T(8,128)S(1)}, f32[2,176,128]{2,1,0:T(8,128)S(1)}, u32[]{:S(2)}, u32[]{:S(2)}) collective-permute-start(f32[2,176,128]{2,1,0:T(8,128)S(1)} %get-tuple-element.72), channel_id=1, source_target_pairs={{0,32},{4,132},{8,40},{12,140},{16,48},{20,148},{24,56},{28,156},{... | collective-permute-start | bytes 540680 | tf_op jit(solution)/shard_map/ppermute | solution.py:45
  75.0 6.7 %collective-permute-start.23 = (f32[2,176,128]{2,1,0:T(8,128)S(1)}, f32[2,176,128]{2,1,0:T(8,128)S(1)}, u32[]{:S(2)}, u32[]{:S(2)}) collective-permute-start(f32[2,176,128]{2,1,0:T(8,128)S(1)} %get-tuple-element.71), channel_id=1, source_target_pairs={{0,48},{4,196},{8,56},{12,204},{16,0},{20,212},{24,8},{28,220},{32... | collective-permute-start | bytes 540680 | tf_op jit(solution)/shard_map/ppermute | solution.py:45
  76.9 8.2 %collective-permute-start.15 = (f32[2,176,128]{2,1,0:T(8,128)S(1)}, f32[2,176,128]{2,1,0:T(8,128)S(1)}, u32[]{:S(2)}, u32[]{:S(2)}) collective-permute-start(f32[2,176,128]{2,1,0:T(8,128)S(1)} %pad_maximum_fusion.6), channel_id=1, source_target_pairs={{0,192},{4,52},{8,200},{12,60},{16,208},{20,4},{24,216},{28,12},{3... | collective-permute-start | bytes 540680 | tf_op jit(solution)/shard_map/ppermute | solution.py:45
  77.6 7.5 %collective-permute-start.16 = (f32[2,176,128]{2,1,0:T(8,128)S(1)}, f32[2,176,128]{2,1,0:T(8,128)S(1)}, u32[]{:S(2)}, u32[]{:S(2)}) collective-permute-start(f32[2,176,128]{2,1,0:T(8,128)S(1)} %pad_maximum_fusion.6), channel_id=1, source_target_pairs={{0,128},{4,36},{8,136},{12,44},{16,144},{20,52},{24,152},{28,60},{... | collective-permute-start | bytes 540680 | tf_op jit(solution)/shard_map/ppermute | solution.py:45
  81.7 5.9 %collective-permute-start.17 = (f32[2,176,128]{2,1,0:T(8,128)S(1)}, f32[2,176,128]{2,1,0:T(8,128)S(1)}, u32[]{:S(2)}, u32[]{:S(2)}) collective-permute-start(f32[2,176,128]{2,1,0:T(8,128)S(1)} %pad_maximum_fusion.6), channel_id=1, source_target_pairs={{0,64},{4,20},{8,72},{12,28},{16,80},{20,36},{24,88},{28,44},{32,9... | collective-permute-start | bytes 540680 | tf_op jit(solution)/shard_map/ppermute | solution.py:45
  81.8 8.3 %collective-permute-start.24 = (f32[176,128]{1,0:T(8,128)S(1)}, f32[176,128]{1,0:T(8,128)S(1)}, u32[]{:S(2)}, u32[]{:S(2)}) collective-permute-start(f32[176,128]{1,0:T(8,128)S(1)} %get-tuple-element.78), channel_id=1, source_target_pairs={{0,8},{4,12},{8,0},{12,4},{16,24},{20,28},{24,16},{28,20},{32,40},... | collective-permute-start | bytes 270344 | tf_op jit(solution)/shard_map/ppermute | solution.py:41
  90.1 15.1 %collective-permute-start.25 = (f32[8,176,128]{2,1,0:T(8,128)S(1)}, f32[8,176,128]{2,1,0:T(8,128)S(1)}, u32[]{:S(2)}, u32[]{:S(2)}) collective-permute-start(f32[8,176,128]{2,1,0:T(8,128)S(1)} %pad_maximum_fusion.2.rest_0_), channel_id=1, source_target_pairs={{0,48},{4,196},{8,56},{12,204},{16,0},{20,212},{24,8},{28,220},{32... | collective-permute-start | bytes 2162696 | tf_op jit(solution)/shard_map/ppermute | solution.py:45
  90.7 16.2 %collective-permute-start.27 = (f32[8,176,128]{2,1,0:T(8,128)S(1)}, f32[8,176,128]{2,1,0:T(8,128)S(1)}, u32[]{:S(2)}, u32[]{:S(2)}) collective-permute-start(f32[8,176,128]{2,1,0:T(8,128)S(1)} %pad_maximum_fusion.2.rest_0_), channel_id=1, source_target_pairs={{0,16},{4,68},{8,24},{12,76},{16,32},{20,84},{24,40},{28,92},{32,4... | collective-permute-start | bytes 2162696 | tf_op jit(solution)/shard_map/ppermute | solution.py:45
  93.1 6.7 %collective-permute-start.30 = (f32[4,160,128]{2,1,0:T(8,128)S(1)}, f32[4,160,128]{2,1,0:T(8,128)S(1)}, u32[]{:S(2)}, u32[]{:S(2)}) collective-permute-start(f32[4,160,128]{2,1,0:T(8,128)S(1)} %get-tuple-element.52), channel_id=1, source_target_pairs={{0,4},{4,0},{8,12},{12,8},{16,20},{20,16},{24,28},{28,24},{32,36},... | collective-permute-start | bytes 983048 | tf_op jit(solution)/shard_map/ppermute | solution.py:37
  99.9 7.3 %collective-permute-start.31 = (f32[160,128]{1,0:T(8,128)S(1)}, f32[160,128]{1,0:T(8,128)S(1)}, u32[]{:S(2)}, u32[]{:S(2)}) collective-permute-start(f32[160,128]{1,0:T(8,128)S(1)} %get-tuple-element.76), channel_id=1, source_target_pairs={{0,64},{4,20},{8,72},{12,28},{16,80},{20,36},{24,88},{28,44},{32,9... | collective-permute-start | bytes 245768 | tf_op jit(solution)/shard_map/ppermute | solution.py:45
  101.7 6.7 %collective-permute-start.32 = (f32[160,128]{1,0:T(8,128)S(1)}, f32[160,128]{1,0:T(8,128)S(1)}, u32[]{:S(2)}, u32[]{:S(2)}) collective-permute-start(f32[160,128]{1,0:T(8,128)S(1)} %get-tuple-element.75), channel_id=1, source_target_pairs={{0,128},{4,36},{8,136},{12,44},{16,144},{20,52},{24,152},{28,60},{... | collective-permute-start | bytes 245768 | tf_op jit(solution)/shard_map/ppermute | solution.py:45
  103.8 4.5 %collective-permute-start.33 = (f32[160,128]{1,0:T(8,128)S(1)}, f32[160,128]{1,0:T(8,128)S(1)}, u32[]{:S(2)}, u32[]{:S(2)}) collective-permute-start(f32[160,128]{1,0:T(8,128)S(1)} %get-tuple-element.74), channel_id=1, source_target_pairs={{0,192},{4,52},{8,200},{12,60},{16,208},{20,4},{24,216},{28,12},{3... | collective-permute-start | bytes 245768 | tf_op jit(solution)/shard_map/ppermute | solution.py:45
  105.2 7.2 %collective-permute-start.26 = (f32[4,176,128]{2,1,0:T(8,128)S(1)}, f32[4,176,128]{2,1,0:T(8,128)S(1)}, u32[]{:S(2)}, u32[]{:S(2)}) collective-permute-start(f32[4,176,128]{2,1,0:T(8,128)S(1)} %slice.122), channel_id=1, source_target_pairs={{0,48},{4,196},{8,56},{12,204},{16,0},{20,212},{24,8},{28,220},{32... | collective-permute-start | bytes 1081352 | tf_op jit(solution)/shard_map/ppermute | solution.py:45
  106.9 7.6 %collective-permute-start.28 = (f32[4,176,128]{2,1,0:T(8,128)S(1)}, f32[4,176,128]{2,1,0:T(8,128)S(1)}, u32[]{:S(2)}, u32[]{:S(2)}) collective-permute-start(f32[4,176,128]{2,1,0:T(8,128)S(1)} %slice.123), channel_id=1, source_target_pairs={{0,16},{4,68},{8,24},{12,76},{16,32},{20,84},{24,40},{28,92},{32,4... | collective-permute-start | bytes 1081352 | tf_op jit(solution)/shard_map/ppermute | solution.py:45
  108.4 3.7 %collective-permute-start.34 = (f32[160,128]{1,0:T(8,128)S(1)}, f32[160,128]{1,0:T(8,128)S(1)}, u32[]{:S(2)}, u32[]{:S(2)}) collective-permute-start(f32[160,128]{1,0:T(8,128)S(1)} %fusion.7), channel_id=1, source_target_pairs={{0,1},{1,0},{2,3},{3,2},{4,5},{5,4},{6,7},{7,6},{8,9},{9,8},{10,11... | collective-permute-start | bytes 245768 | tf_op jit(solution)/shard_map/ppermute | solution.py:55
  114.6 15.9 %collective-permute-start.35 = (f32[24,176,128]{2,1,0:T(8,128)S(1)}, f32[24,176,128]{2,1,0:T(8,128)S(1)}, u32[]{:S(2)}, u32[]{:S(2)}) collective-permute-start(f32[24,176,128]{2,1,0:T(8,128)S(1)} %pad_maximum_fusion), channel_id=1, source_target_pairs={{0,4},{4,0},{8,12},{12,8},{16,20},{20,16},{24,28},{28,24},{32,36},... | collective-permute-start | bytes 6488072 | tf_op jit(solution)/shard_map/ppermute | solution.py:37
  119.9 10.6 %collective-permute-start.29 = (f32[8,176,128]{2,1,0:T(8,128)S(1)}, f32[8,176,128]{2,1,0:T(8,128)S(1)}, u32[]{:S(2)}, u32[]{:S(2)}) collective-permute-start(f32[8,176,128]{2,1,0:T(8,128)S(1)} %pad_maximum_fusion.2.rest_0_), channel_id=1, source_target_pairs={{0,4},{4,0},{8,12},{12,8},{16,20},{20,16},{24,28},{28,24},{32,36},... | collective-permute-start | bytes 2162696 | tf_op jit(solution)/shard_map/ppermute | solution.py:37
  120.0 7.5 %collective-permute-start.36 = (f32[160,128]{1,0:T(8,128)S(1)}, f32[160,128]{1,0:T(8,128)S(1)}, u32[]{:S(2)}, u32[]{:S(2)}) collective-permute-start(f32[160,128]{1,0:T(8,128)S(1)} %add.116), channel_id=1, source_target_pairs={{0,2},{1,3},{2,0},{3,1},{4,6},{5,7},{6,4},{7,5},{8,10},{9,11},{10,... | collective-permute-start | bytes 245768 | tf_op jit(solution)/shard_map/ppermute | solution.py:55
  127.5 8.3 %collective-permute-start.39 = (f32[160,128]{1,0:T(8,128)S(1)}, f32[160,128]{1,0:T(8,128)S(1)}, u32[]{:S(2)}, u32[]{:S(2)}) collective-permute-start(f32[160,128]{1,0:T(8,128)S(1)} %add.117), channel_id=1, source_target_pairs={{0,8},{4,12},{8,0},{12,4},{16,24},{20,28},{24,16},{28,20},{32,40},... | collective-permute-start | bytes 245768 | tf_op jit(solution)/shard_map/ppermute | solution.py:41
  135.8 5.5 %collective-permute-start.40 = (f32[160,128]{1,0:T(8,128)S(1)}, f32[160,128]{1,0:T(8,128)S(1)}, u32[]{:S(2)}, u32[]{:S(2)}) collective-permute-start(f32[160,128]{1,0:T(8,128)S(1)} %add.120), channel_id=1, source_target_pairs={{0,16},{4,68},{8,24},{12,76},{16,32},{20,84},{24,40},{28,92},{32,4... | collective-permute-start | bytes 245768 | tf_op jit(solution)/shard_map/ppermute | solution.py:45
  135.9 5.4 %collective-permute-start.41 = (f32[160,128]{1,0:T(8,128)S(1)}, f32[160,128]{1,0:T(8,128)S(1)}, u32[]{:S(2)}, u32[]{:S(2)}) collective-permute-start(f32[160,128]{1,0:T(8,128)S(1)} %add.120), channel_id=1, source_target_pairs={{0,32},{4,132},{8,40},{12,140},{16,48},{20,148},{24,56},{28,156},{... | collective-permute-start | bytes 245768 | tf_op jit(solution)/shard_map/ppermute | solution.py:45
  138.2 3.6 %collective-permute-start.42 = (f32[160,128]{1,0:T(8,128)S(1)}, f32[160,128]{1,0:T(8,128)S(1)}, u32[]{:S(2)}, u32[]{:S(2)}) collective-permute-start(f32[160,128]{1,0:T(8,128)S(1)} %add.120), channel_id=1, source_target_pairs={{0,48},{4,196},{8,56},{12,204},{16,0},{20,212},{24,8},{28,220},{32... | collective-permute-start | bytes 245768 | tf_op jit(solution)/shard_map/ppermute | solution.py:45
  138.6 4.6 %collective-permute-start.37 = (f32[2,176,128]{2,1,0:T(8,128)S(1)}, f32[2,176,128]{2,1,0:T(8,128)S(1)}, u32[]{:S(2)}, u32[]{:S(2)}) collective-permute-start(f32[2,176,128]{2,1,0:T(8,128)S(1)} %get-tuple-element.56), channel_id=1, source_target_pairs={{0,1},{1,0},{2,3},{3,2},{4,5},{5,4},{6,7},{7,6},{8,9},{9,8},{10,11... | collective-permute-start | bytes 540680 | tf_op jit(solution)/shard_map/ppermute | solution.py:55
  143.2 7.2 %collective-permute-start.43 = (f32[160,128]{1,0:T(8,128)S(1)}, f32[160,128]{1,0:T(8,128)S(1)}, u32[]{:S(2)}, u32[]{:S(2)}) collective-permute-start(f32[160,128]{1,0:T(8,128)S(1)} %add_add_fusion.1), channel_id=1, source_target_pairs={{0,192},{4,52},{8,200},{12,60},{16,208},{20,4},{24,216},{28,12},{3... | collective-permute-start | bytes 245768 | tf_op jit(solution)/shard_map/ppermute | solution.py:45
  143.4 7.1 %collective-permute-start.44 = (f32[160,128]{1,0:T(8,128)S(1)}, f32[160,128]{1,0:T(8,128)S(1)}, u32[]{:S(2)}, u32[]{:S(2)}) collective-permute-start(f32[160,128]{1,0:T(8,128)S(1)} %add_add_fusion.1), channel_id=1, source_target_pairs={{0,128},{4,36},{8,136},{12,44},{16,144},{20,52},{24,152},{28,60},{... | collective-permute-start | bytes 245768 | tf_op jit(solution)/shard_map/ppermute | solution.py:45
  145.4 5.0 %collective-permute-start.45 = (f32[160,128]{1,0:T(8,128)S(1)}, f32[160,128]{1,0:T(8,128)S(1)}, u32[]{:S(2)}, u32[]{:S(2)}) collective-permute-start(f32[160,128]{1,0:T(8,128)S(1)} %add_add_fusion.1), channel_id=1, source_target_pairs={{0,64},{4,20},{8,72},{12,28},{16,80},{20,36},{24,88},{28,44},{32,9... | collective-permute-start | bytes 245768 | tf_op jit(solution)/shard_map/ppermute | solution.py:45
  146.3 6.0 %collective-permute-start.38 = (f32[176,128]{1,0:T(8,128)S(1)}, f32[176,128]{1,0:T(8,128)S(1)}, u32[]{:S(2)}, u32[]{:S(2)}) collective-permute-start(f32[176,128]{1,0:T(8,128)S(1)} %fusion.1), channel_id=1, source_target_pairs={{0,2},{1,3},{2,0},{3,1},{4,6},{5,7},{6,4},{7,5},{8,10},{9,11},{10,... | collective-permute-start | bytes 270344 | tf_op jit(solution)/shard_map/ppermute | solution.py:55
  152.3 5.6 %collective-permute-start.46 = (f32[4,160,128]{2,1,0:T(8,128)S(1)}, f32[4,160,128]{2,1,0:T(8,128)S(1)}, u32[]{:S(2)}, u32[]{:S(2)}) collective-permute-start(f32[4,160,128]{2,1,0:T(8,128)S(1)} %pad_maximum_fusion.4.q), channel_id=1, source_target_pairs={{0,4},{4,0},{8,12},{12,8},{16,20},{20,16},{24,28},{28,24},{32,36},... | collective-permute-start | bytes 983048 | tf_op jit(solution)/shard_map/ppermute | solution.py:37

commit v3 on v2

--- a/solution.py
+++ b/solution.py
@@ -382,7 +382,7 @@
     kept, given = products
     got = swap_rep(given, 1)
     last = swap_rep(kept[1] + got[1], 2)
-    q = add4(after(laned[0], got), *laned[1:])
+    q = add4(after(laned[0], last), *laned[1:])
     sums, pre, yt = call(
         hidden_kernel, [block, (SIDE, 256), padded],
         (kept, got, last, features, self_one, neigh_one, bias_one.reshape(1, -1), nt),
@@ -397,9 +397,8 @@
     plane = gather_ring(after(lane, gz))
     kept = reduce_lane(same, other)
     kept = kept + swap_rep(kept, 1)
+    kept = kept + swap_rep(kept, 2)
     pieces = gather_core(plane, kept)
-    kept = kept + swap_rep(kept, 2)
-    pieces[-1] = after(pieces[-1], kept)
     products = agg(True, head, pieces)
     *parts, q, qo = last_sums(kept, products)
     (logits,) = call(logits_kernel, [tall], (*parts, base))

time: 160 us -> 156 us (0.975)
  starting transfers between devices: 79.9 us -> 72.3 us
  waiting for transfers between devices: 58.7 us -> 63.8 us
    ppermute x8, starting transfers between devices: 12 us -> 4.12 us  [swap_rep(): return lax.ppermute(a, 'rep', [(j, j ^ bit) for j in range(NR)])]
    ppermute x8, waiting for transfers between devices: 14.2 us -> 20.3 us  [swap_rep(): return lax.ppermute(a, 'rep', [(j, j ^ bit) for j in range(NR)])]
    ppermute x7, waiting for transfers between devices: 5.31 us -> 9.96 us  [send_core(): return lax.ppermute(a, 'row', row_perm(lambda c: (0, 0, 0, 1)))]
    ppermute x28, starting transfers between devices: 31.4 us -> 35.8 us  [send_plane(): lax.ppermute(a, 'row', row_perm(lambda c: (d, 0, 0, 0) if c == stage else...]
    ppermute x28, waiting for transfers between devices: 34.1 us -> 31.1 us  [send_plane(): lax.ppermute(a, 'row', row_perm(lambda c: (d, 0, 0, 0) if c == stage else...]
    ppermute x4, waiting for transfers between devices: 5.06 us -> 2.41 us  [send_z(): return lax.ppermute(a, 'row', row_perm(lambda c: (0, 0, 1, 0)))]
    ppermute x7, starting transfers between devices: 21 us -> 18.7 us  [send_core(): return lax.ppermute(a, 'row', row_perm(lambda c: (0, 0, 0, 1)))]
    ppermute x4, starting transfers between devices: 15.6 us -> 13.7 us  [send_z(): return lax.ppermute(a, 'row', row_perm(lambda c: (0, 0, 1, 0)))]
  transfers between devices with their start and end apart: 47 -> 47, of which waited for: 26 -> 29; matrix products, arithmetic and copies ran while one was open for 2% -> 2% of each run, Pallas kernels for 6% -> 6%
where the time goes in v3:
time: 156 us
  starting transfers between devices  72.3 us (46%)
  waiting for transfers between devices  63.8 us (41%)
  Pallas kernels  13.5 us (9%)
  other arithmetic  3.24 us (2%)
  local copies, waits for them, and re-layouts  2.37 us (2%)
    ppermute x28, starting transfers between devices, send_plane(): lax.ppermute(a, 'row', row_perm(lambda c: (d, 0, 0, 0) if c == stage else...  35.8 us
    ppermute x28, waiting for transfers between devices, send_plane(): lax.ppermute(a, 'row', row_perm(lambda c: (d, 0, 0, 0) if c == stage else...  31.1 us
    ppermute x8, waiting for transfers between devices, swap_rep(): return lax.ppermute(a, 'rep', [(j, j ^ bit) for j in range(NR)])  20.3 us
    ppermute x7, starting transfers between devices, send_core(): return lax.ppermute(a, 'row', row_perm(lambda c: (0, 0, 0, 1)))  18.7 us
    ppermute x4, starting transfers between devices, send_z(): return lax.ppermute(a, 'row', row_perm(lambda c: (0, 0, 1, 0)))  13.7 us
    pallas_call x8, Pallas kernels, call(): pl.pallas_call(kernel, out_shape=[jax.ShapeDtypeStruct(s, dtype) for s in...  13.5 us
    ppermute x7, waiting for transfers between devices, send_core(): return lax.ppermute(a, 'row', row_perm(lambda c: (0, 0, 0, 1)))  9.96 us
    ppermute x8, starting transfers between devices, swap_rep(): return lax.ppermute(a, 'rep', [(j, j ^ bit) for j in range(NR)])  4.12 us
  transfers between devices with their start and end apart: 47, of which 29 were waited for; matrix products, arithmetic and copies ran while one was open for 2% of the time, Pallas kernels for 6%

profile of v3, /device:TPU:1, one launch (start us, length us, event | category | flops | bytes accessed | tf_op | source)
XLA Modules:
  0.0 156.2 jit_solution(12981804143832105838)
XLA Ops:
  0.6 7.8 %collective-permute-start = (f32[128,128]{1,0:T(8,128)}, f32[128,128]{1,0:T(8,128)S(1)}, u32[]{:S(2)}, u32[]{:S(2)}) collective-permute-start(f32[128,128]{1,0:T(8,128)} %feat.3), channel_id=1, source_target_pairs={{0,8},{4,12},{8,0},{12,4},{16,24},{20,28},{24,16},{28,20},{32,40},... | collective-permute-start | bytes 196616 | tf_op jit(solution)/shard_map/ppermute | solution.py:41
  8.5 1.2 collective-permute-start.8
  10.2 1.3 reduce.3
  11.6 0.7 pad_add_fusion.meta
  12.3 1.6 %copy-done = f32[4,1,8,128,128]{4,3,2,1,0:T(8,128)S(1)} copy-done((f32[4,1,8,128,128]{4,3,2,1,0:T(8,128)S(1)}, f32[4,1,8,128,128]{4,3,2,1,0:T(8,128)}, u32[]{:S(2)}) %copy-start) | copy-done | bytes 2097176
  13.9 0.8 shard_map.162.tiles
  14.8 2.8 %collective-permute-start.1 = (f32[2,128,128]{2,1,0:T(8,128)S(1)}, f32[2,128,128]{2,1,0:T(8,128)S(1)}, u32[]{:S(2)}, u32[]{:S(2)}) collective-permute-start(f32[2,128,128]{2,1,0:T(8,128)S(1)} %pad_maximum_fusion.7), channel_id=1, source_target_pairs={{0,192},{4,52},{8,200},{12,60},{16,208},{20,4},{24,216},{28,12},{3... | collective-permute-start | bytes 393224 | tf_op jit(solution)/shard_map/ppermute | solution.py:45
  18.0 0.7 collective-permute-start.3
  18.8 0.8 collective-permute-start.9
  19.6 1.3 collective-permute-done.1
  20.9 2.2 %collective-permute-done.2 = f32[2,128,128]{2,1,0:T(8,128)S(1)} collective-permute-done((f32[2,128,128]{2,1,0:T(8,128)S(1)}, f32[2,128,128]{2,1,0:T(8,128)S(1)}, u32[]{:S(2)}, u32[]{:S(2)}) %collective-permute-start.2) | collective-permute-done | bytes 131104 | tf_op jit(solution)/shard_map/ppermute | solution.py:45
  23.1 1.6 %collective-permute-done.3 = f32[2,128,128]{2,1,0:T(8,128)S(1)} collective-permute-done((f32[2,128,128]{2,1,0:T(8,128)S(1)}, f32[2,128,128]{2,1,0:T(8,128)S(1)}, u32[]{:S(2)}, u32[]{:S(2)}) %collective-permute-start.3) | collective-permute-done | bytes 131104 | tf_op jit(solution)/shard_map/ppermute | solution.py:45
  24.7 2.4 %shard_map.163 = (f32[32,176,128]{2,1,0:T(8,128)S(1)}, f32[32,176,128]{2,1,0:T(8,128)S(1)}) custom-call(s32[38]{0:T(128)S(1)} %pad_add_fusion.meta, bf16[4,8,128,256]{3,2,1,0:T(8,128)(2,1)S(1)} %shard_map.162.tiles, f32[2,172,128]{2,1,0:T(8,128)S(1)} %pad_maximum_fusion.5.near, f32[2,172,128]{2,1,0:T(8,128)S(1)} %collective-permute-done.9.far), custom_call_target="tpu_custom_call" | custom-call | bytes 12582912 | tf_op jit(solution)/shard_map/pallas_call | solution.py:260
  27.2 3.9 %collective-permute-start.10 = (f32[32,176,128]{2,1,0:T(8,128)S(1)}, f32[32,176,128]{2,1,0:T(8,128)S(1)}, u32[]{:S(2)}, u32[]{:S(2)}) collective-permute-start(f32[32,176,128]{2,1,0:T(8,128)S(1)} %get-tuple-element.39), channel_id=1, source_target_pairs={{0,4},{4,0},{8,12},{12,8},{16,20},{20,16},{24,28},{28,24},{32,36},... | collective-permute-start | bytes 8650760 | tf_op jit(solution)/shard_map/ppermute | solution.py:37
  31.0 1.3 collective-permute-start.5
  32.5 3.4 %collective-permute-done.10 = f32[32,176,128]{2,1,0:T(8,128)S(1)} collective-permute-done((f32[32,176,128]{2,1,0:T(8,128)S(1)}, f32[32,176,128]{2,1,0:T(8,128)S(1)}, u32[]{:S(2)}, u32[]{:S(2)}) %collective-permute-start.10) | collective-permute-done | bytes 2883616 | tf_op jit(solution)/shard_map/ppermute | solution.py:37
  36.3 3.0 %collective-permute-done.4.rest_1_ = f32[8,128,128]{2,1,0:T(8,128)S(1)} collective-permute-done((f32[8,128,128]{2,1,0:T(8,128)S(1)}, f32[8,128,128]{2,1,0:T(8,128)S(1)}, u32[]{:S(2)}, u32[]{:S(2)}) %collective-permute-start.4) | collective-permute-done | bytes 524320 | tf_op jit(solution)/shard_map/ppermute | solution.py:45
  39.4 1.6 collective-permute-done.5.rest_2_
  40.9 5.6 %collective-permute-done.6.rest_3_ = f32[8,128,128]{2,1,0:T(8,128)S(1)} collective-permute-done((f32[8,128,128]{2,1,0:T(8,128)S(1)}, f32[8,128,128]{2,1,0:T(8,128)S(1)}, u32[]{:S(2)}, u32[]{:S(2)}) %collective-permute-start.6) | collective-permute-done | bytes 524320 | tf_op jit(solution)/shard_map/ppermute | solution.py:45
  46.7 2.1 %collective-permute-start.11 = (f32[24,128,128]{2,1,0:T(8,128)S(1)}, f32[24,128,128]{2,1,0:T(8,128)S(1)}, u32[]{:S(2)}, u32[]{:S(2)}) collective-permute-start(f32[24,128,128]{2,1,0:T(8,128)S(1)} %pad_maximum_fusion.1), channel_id=1, source_target_pairs={{0,4},{4,0},{8,12},{12,8},{16,20},{20,16},{24,28},{28,24},{32,36},... | collective-permute-start | bytes 4718600 | tf_op jit(solution)/shard_map/ppermute | solution.py:37
  49.5 0.6 collective-permute-start.18
  50.1 2.0 %collective-permute-start.20 = (f32[8,176,128]{2,1,0:T(8,128)S(1)}, f32[8,176,128]{2,1,0:T(8,128)S(1)}, u32[]{:S(2)}, u32[]{:S(2)}) collective-permute-start(f32[8,176,128]{2,1,0:T(8,128)S(1)} %get-tuple-element.65), channel_id=1, source_target_pairs={{0,192},{4,52},{8,200},{12,60},{16,208},{20,4},{24,216},{28,12},{3... | collective-permute-start | bytes 2162696 | tf_op jit(solution)/shard_map/ppermute | solution.py:45
  52.6 2.2 %shard_map.164 = (f32[2,128,128]{2,1,0:T(8,128)S(1)}, f32[2,128,128]{2,1,0:T(8,128)S(1)}) custom-call(s32[38]{0:T(128)S(1)} %pad_add_fusion.meta, bf16[4,8,128,256]{3,2,1,0:T(8,128)(2,1)S(1)} %shard_map.162.tiles, f32[8,128,128]{2,1,0:T(8,128)S(1)} %constant_dynamic-update-slice_fusion.rest_0_, f32[8,128,128]{2,1,0:T(8,128)S(1)} %collective-permute-done.4.rest_1_, ...), custom_call_target="tpu_custom_call" | custom-call | bytes 12582912 | tf_op jit(solution)/shard_map/pallas_call | solution.py:260
  54.8 1.0 collective-permute-start.12
  55.8 3.4 %collective-permute-done.12.got = f32[2,128,128]{2,1,0:T(8,128)S(1)} collective-permute-done((f32[2,128,128]{2,1,0:T(8,128)S(1)}, f32[2,128,128]{2,1,0:T(8,128)S(1)}, u32[]{:S(2)}, u32[]{:S(2)}) %collective-permute-start.12) | collective-permute-done | bytes 131104 | tf_op jit(solution)/shard_map/ppermute | solution.py:55
  59.2 0.8 collective-permute-start.13
  60.0 4.3 %collective-permute-done.13.last = f32[128,128]{1,0:T(8,128)S(1)} collective-permute-done((f32[128,128]{1,0:T(8,128)S(1)}, f32[128,128]{1,0:T(8,128)S(1)}, u32[]{:S(2)}, u32[]{:S(2)}) %collective-permute-start.13) | collective-permute-done | bytes 65568 | tf_op jit(solution)/shard_map/ppermute | solution.py:55
  64.3 0.6 shard_map.165
  64.9 3.8 %collective-permute-start.14 = (f32[176,128]{1,0:T(8,128)S(1)}, f32[176,128]{1,0:T(8,128)S(1)}, u32[]{:S(2)}, u32[]{:S(2)}) collective-permute-start(f32[176,128]{1,0:T(8,128)S(1)} %get-tuple-element.43), channel_id=1, source_target_pairs={{0,8},{4,12},{8,0},{12,4},{16,24},{20,28},{24,16},{28,20},{32,40},... | collective-permute-start | bytes 270344 | tf_op jit(solution)/shard_map/ppermute | solution.py:41
  69.3 5.6 %collective-permute-start.22 = (f32[2,176,128]{2,1,0:T(8,128)S(1)}, f32[2,176,128]{2,1,0:T(8,128)S(1)}, u32[]{:S(2)}, u32[]{:S(2)}) collective-permute-start(f32[2,176,128]{2,1,0:T(8,128)S(1)} %get-tuple-element.70), channel_id=1, source_target_pairs={{0,32},{4,132},{8,40},{12,140},{16,48},{20,148},{24,56},{28,156},{... | collective-permute-start | bytes 540680 | tf_op jit(solution)/shard_map/ppermute | solution.py:45
  74.9 2.0 %collective-permute-start.23 = (f32[2,176,128]{2,1,0:T(8,128)S(1)}, f32[2,176,128]{2,1,0:T(8,128)S(1)}, u32[]{:S(2)}, u32[]{:S(2)}) collective-permute-start(f32[2,176,128]{2,1,0:T(8,128)S(1)} %get-tuple-element.69), channel_id=1, source_target_pairs={{0,48},{4,196},{8,56},{12,204},{16,0},{20,212},{24,8},{28,220},{32... | collective-permute-start | bytes 540680 | tf_op jit(solution)/shard_map/ppermute | solution.py:45
  77.0 0.8 collective-permute-start.16
  77.8 0.7 collective-permute-start.17
  78.5 1.5 collective-permute-done.22
  80.1 1.5 collective-permute-start.24
  81.6 1.9 %collective-permute-done.15 = f32[2,176,128]{2,1,0:T(8,128)S(1)} collective-permute-done((f32[2,176,128]{2,1,0:T(8,128)S(1)}, f32[2,176,128]{2,1,0:T(8,128)S(1)}, u32[]{:S(2)}, u32[]{:S(2)}) %collective-permute-start.15) | collective-permute-done | bytes 180256 | tf_op jit(solution)/shard_map/ppermute | solution.py:45
  83.7 1.9 %collective-permute-done.17 = f32[2,176,128]{2,1,0:T(8,128)S(1)} collective-permute-done((f32[2,176,128]{2,1,0:T(8,128)S(1)}, f32[2,176,128]{2,1,0:T(8,128)S(1)}, u32[]{:S(2)}, u32[]{:S(2)}) %collective-permute-start.17) | collective-permute-done | bytes 180256 | tf_op jit(solution)/shard_map/ppermute | solution.py:45
  85.7 2.4 %collective-permute-done.24.gz = f32[176,128]{1,0:T(8,128)S(1)} collective-permute-done((f32[176,128]{1,0:T(8,128)S(1)}, f32[176,128]{1,0:T(8,128)S(1)}, u32[]{:S(2)}, u32[]{:S(2)}) %collective-permute-start.24) | collective-permute-done | bytes 90144 | tf_op jit(solution)/shard_map/ppermute | solution.py:41
  88.1 2.8 %collective-permute-start.25 = (f32[8,176,128]{2,1,0:T(8,128)S(1)}, f32[8,176,128]{2,1,0:T(8,128)S(1)}, u32[]{:S(2)}, u32[]{:S(2)}) collective-permute-start(f32[8,176,128]{2,1,0:T(8,128)S(1)} %pad_maximum_fusion.2.rest_0_), channel_id=1, source_target_pairs={{0,48},{4,196},{8,56},{12,204},{16,0},{20,212},{24,8},{28,220},{32... | collective-permute-start | bytes 2162696 | tf_op jit(solution)/shard_map/ppermute | solution.py:45
  90.9 1.5 shard_map.166
  92.4 6.9 %collective-permute-start.30 = (f32[4,160,128]{2,1,0:T(8,128)S(1)}, f32[4,160,128]{2,1,0:T(8,128)S(1)}, u32[]{:S(2)}, u32[]{:S(2)}) collective-permute-start(f32[4,160,128]{2,1,0:T(8,128)S(1)} %get-tuple-element.51), channel_id=1, source_target_pairs={{0,4},{4,0},{8,12},{12,8},{16,20},{20,16},{24,28},{28,24},{32,36},... | collective-permute-start | bytes 983048 | tf_op jit(solution)/shard_map/ppermute | solution.py:37
  99.3 1.3 collective-permute-done.30
  100.7 4.1 %collective-permute-start.32 = (f32[160,128]{1,0:T(8,128)S(1)}, f32[160,128]{1,0:T(8,128)S(1)}, u32[]{:S(2)}, u32[]{:S(2)}) collective-permute-start(f32[160,128]{1,0:T(8,128)S(1)} %get-tuple-element.73), channel_id=1, source_target_pairs={{0,128},{4,36},{8,136},{12,44},{16,144},{20,52},{24,152},{28,60},{... | collective-permute-start | bytes 245768 | tf_op jit(solution)/shard_map/ppermute | solution.py:45
  105.2 1.5 collective-permute-start.28
  106.7 2.6 %collective-permute-done.32 = f32[160,128]{1,0:T(8,128)S(1)} collective-permute-done((f32[160,128]{1,0:T(8,128)S(1)}, f32[160,128]{1,0:T(8,128)S(1)}, u32[]{:S(2)}, u32[]{:S(2)}) %collective-permute-start.32) | collective-permute-done | bytes 81952 | tf_op jit(solution)/shard_map/ppermute | solution.py:45
  109.5 3.6 %collective-permute-done.34 = f32[160,128]{1,0:T(8,128)S(1)} collective-permute-done((f32[160,128]{1,0:T(8,128)S(1)}, f32[160,128]{1,0:T(8,128)S(1)}, u32[]{:S(2)}, u32[]{:S(2)}) %collective-permute-start.34) | collective-permute-done | bytes 81952 | tf_op jit(solution)/shard_map/ppermute | solution.py:55
  113.2 5.1 %collective-permute-done.35 = f32[160,128]{1,0:T(8,128)S(1)} collective-permute-done((f32[160,128]{1,0:T(8,128)S(1)}, f32[160,128]{1,0:T(8,128)S(1)}, u32[]{:S(2)}, u32[]{:S(2)}) %collective-permute-start.35) | collective-permute-done | bytes 81952 | tf_op jit(solution)/shard_map/ppermute | solution.py:55
  118.4 5.1 %collective-permute-start.36 = (f32[24,176,128]{2,1,0:T(8,128)S(1)}, f32[24,176,128]{2,1,0:T(8,128)S(1)}, u32[]{:S(2)}, u32[]{:S(2)}) collective-permute-start(f32[24,176,128]{2,1,0:T(8,128)S(1)} %pad_maximum_fusion), channel_id=1, source_target_pairs={{0,4},{4,0},{8,12},{12,8},{16,20},{20,16},{24,28},{28,24},{32,36},... | collective-permute-start | bytes 6488072 | tf_op jit(solution)/shard_map/ppermute | solution.py:37
  123.6 0.6 collective-permute-start.39
  124.2 4.2 %collective-permute-done.29.rest_4_ = f32[8,176,128]{2,1,0:T(8,128)S(1)} collective-permute-done((f32[8,176,128]{2,1,0:T(8,128)S(1)}, f32[8,176,128]{2,1,0:T(8,128)S(1)}, u32[]{:S(2)}, u32[]{:S(2)}) %collective-permute-start.29) | collective-permute-done | bytes 720928 | tf_op jit(solution)/shard_map/ppermute | solution.py:37
  128.4 3.8 %shard_map.167 = (f32[2,176,128]{2,1,0:T(8,128)S(1)}, f32[2,176,128]{2,1,0:T(8,128)S(1)}) custom-call(s32[38]{0:T(128)S(1)} %pad_add_fusion.meta, bf16[4,8,128,256]{3,2,1,0:T(8,128)(2,1)S(1)} %shard_map.162.tiles, f32[8,176,128]{2,1,0:T(8,128)S(1)} %pad_maximum_fusion.2.rest_0_, f32[8,176,128]{2,1,0:T(8,128)S(1)} %collective-permute-done.25.rest_1_, ...), custom_call_target="tpu_custom_call" | custom-call | bytes 12582912 | tf_op jit(solution)/shard_map/pallas_call | solution.py:260
  132.4 2.1 %collective-permute-start.41 = (f32[160,128]{1,0:T(8,128)S(1)}, f32[160,128]{1,0:T(8,128)S(1)}, u32[]{:S(2)}, u32[]{:S(2)}) collective-permute-start(f32[160,128]{1,0:T(8,128)S(1)} %add.120), channel_id=1, source_target_pairs={{0,32},{4,132},{8,40},{12,140},{16,48},{20,148},{24,56},{28,156},{... | collective-permute-start | bytes 245768 | tf_op jit(solution)/shard_map/ppermute | solution.py:45
  134.6 0.9 collective-permute-start.42
  135.4 2.3 %collective-permute-done.40 = f32[160,128]{1,0:T(8,128)S(1)} collective-permute-done((f32[160,128]{1,0:T(8,128)S(1)}, f32[160,128]{1,0:T(8,128)S(1)}, u32[]{:S(2)}, u32[]{:S(2)}) %collective-permute-start.40) | collective-permute-done | bytes 81952 | tf_op jit(solution)/shard_map/ppermute | solution.py:45
  137.8 0.6 collective-permute-done.42
  138.4 1.7 %collective-permute-done.37.got = f32[2,176,128]{2,1,0:T(8,128)S(1)} collective-permute-done((f32[2,176,128]{2,1,0:T(8,128)S(1)}, f32[2,176,128]{2,1,0:T(8,128)S(1)}, u32[]{:S(2)}, u32[]{:S(2)}) %collective-permute-start.37) | collective-permute-done | bytes 180256 | tf_op jit(solution)/shard_map/ppermute | solution.py:55
  140.1 5.2 %collective-permute-start.43 = (f32[160,128]{1,0:T(8,128)S(1)}, f32[160,128]{1,0:T(8,128)S(1)}, u32[]{:S(2)}, u32[]{:S(2)}) collective-permute-start(f32[160,128]{1,0:T(8,128)S(1)} %add_add_fusion.1), channel_id=1, source_target_pairs={{0,192},{4,52},{8,200},{12,60},{16,208},{20,4},{24,216},{28,12},{3... | collective-permute-start | bytes 245768 | tf_op jit(solution)/shard_map/ppermute | solution.py:45
  145.2 0.6 collective-permute-start.45
  145.9 1.6 %collective-permute-done.43 = f32[160,128]{1,0:T(8,128)S(1)} collective-permute-done((f32[160,128]{1,0:T(8,128)S(1)}, f32[160,128]{1,0:T(8,128)S(1)}, u32[]{:S(2)}, u32[]{:S(2)}) %collective-permute-start.43) | collective-permute-done | bytes 81952 | tf_op jit(solution)/shard_map/ppermute | solution.py:45
  147.5 2.6 %collective-permute-done.44 = f32[160,128]{1,0:T(8,128)S(1)} collective-permute-done((f32[160,128]{1,0:T(8,128)S(1)}, f32[160,128]{1,0:T(8,128)S(1)}, u32[]{:S(2)}, u32[]{:S(2)}) %collective-permute-start.44) | collective-permute-done | bytes 81952 | tf_op jit(solution)/shard_map/ppermute | solution.py:45
  150.7 2.3 %collective-permute-done.38.last = f32[176,128]{1,0:T(8,128)S(1)} collective-permute-done((f32[176,128]{1,0:T(8,128)S(1)}, f32[176,128]{1,0:T(8,128)S(1)}, u32[]{:S(2)}, u32[]{:S(2)}) %collective-permute-start.38) | collective-permute-done | bytes 90144 | tf_op jit(solution)/shard_map/ppermute | solution.py:55
  153.5 0.7 shard_map.168
  154.1 0.6 collective-permute-done.46.qo
  154.7 1.4 shard_map.169
  (87 shorter events, 6.3 us)
Async XLA Ops:
  0.6 14.1 %collective-permute-start = (f32[128,128]{1,0:T(8,128)}, f32[128,128]{1,0:T(8,128)S(1)}, u32[]{:S(2)}, u32[]{:S(2)}) collective-permute-start(f32[128,128]{1,0:T(8,128)} %feat.3), channel_id=1, source_target_pairs={{0,8},{4,12},{8,0},{12,4},{16,24},{20,28},{24,16},{28,20},{32,40},... | collective-permute-start | bytes 196616 | tf_op jit(solution)/shard_map/ppermute | solution.py:41
  8.5 10.3 %collective-permute-start.8 = (f32[172,128]{1,0:T(8,128)}, f32[172,128]{1,0:T(8,128)S(1)}, u32[]{:S(2)}, u32[]{:S(2)}) collective-permute-start(f32[172,128]{1,0:T(8,128)} %bitcast.47), channel_id=1, source_target_pairs={{0,2},{1,3},{2,0},{3,1},{4,6},{5,7},{6,4},{7,5},{8,10},{9,11},{10,... | collective-permute-start | bytes 264200 | tf_op jit(solution)/shard_map/ppermute | solution.py:55
  12.3 1.6 %copy-start = (f32[4,1,8,128,128]{4,3,2,1,0:T(8,128)S(1)}, f32[4,1,8,128,128]{4,3,2,1,0:T(8,128)}, u32[]{:S(2)}) copy-start(f32[4,1,8,128,128]{4,3,2,1,0:T(8,128)} %tiles.1) | copy-start | bytes 6291460
  13.9 0.8 copy-start.2
  13.9 4.8 %copy-start.3 = (f32[128,172]{0,1:T(8,128)S(1)}, f32[128,172]{0,1:T(8,128)}, u32[]{:S(2)}) copy-start(f32[128,172]{0,1:T(8,128)} %param.21) | copy-start | bytes 264196
  14.8 6.1 %collective-permute-start.1 = (f32[2,128,128]{2,1,0:T(8,128)S(1)}, f32[2,128,128]{2,1,0:T(8,128)S(1)}, u32[]{:S(2)}, u32[]{:S(2)}) collective-permute-start(f32[2,128,128]{2,1,0:T(8,128)S(1)} %pad_maximum_fusion.7), channel_id=1, source_target_pairs={{0,192},{4,52},{8,200},{12,60},{16,208},{20,4},{24,216},{28,12},{3... | collective-permute-start | bytes 393224 | tf_op jit(solution)/shard_map/ppermute | solution.py:45
  17.6 5.5 %collective-permute-start.2 = (f32[2,128,128]{2,1,0:T(8,128)S(1)}, f32[2,128,128]{2,1,0:T(8,128)S(1)}, u32[]{:S(2)}, u32[]{:S(2)}) collective-permute-start(f32[2,128,128]{2,1,0:T(8,128)S(1)} %pad_maximum_fusion.7), channel_id=1, source_target_pairs={{0,128},{4,36},{8,136},{12,44},{16,144},{20,52},{24,152},{28,60},{... | collective-permute-start | bytes 393224 | tf_op jit(solution)/shard_map/ppermute | solution.py:45
  18.0 6.7 %collective-permute-start.3 = (f32[2,128,128]{2,1,0:T(8,128)S(1)}, f32[2,128,128]{2,1,0:T(8,128)S(1)}, u32[]{:S(2)}, u32[]{:S(2)}) collective-permute-start(f32[2,128,128]{2,1,0:T(8,128)S(1)} %pad_maximum_fusion.7), channel_id=1, source_target_pairs={{0,64},{4,20},{8,72},{12,28},{16,80},{20,36},{24,88},{28,44},{32,9... | collective-permute-start | bytes 393224 | tf_op jit(solution)/shard_map/ppermute | solution.py:45
  18.8 6.0 %collective-permute-start.9 = (f32[2,172,128]{2,1,0:T(8,128)S(1)}, f32[2,172,128]{2,1,0:T(8,128)S(1)}, u32[]{:S(2)}, u32[]{:S(2)}) collective-permute-start(f32[2,172,128]{2,1,0:T(8,128)S(1)} %pad_maximum_fusion.5.near), channel_id=1, source_target_pairs={{0,1},{1,0},{2,3},{3,2},{4,5},{5,4},{6,7},{7,6},{8,9},{9,8},{10,11... | collective-permute-start | bytes 528392 | tf_op jit(solution)/shard_map/ppermute | solution.py:55
  27.2 8.8 %collective-permute-start.10 = (f32[32,176,128]{2,1,0:T(8,128)S(1)}, f32[32,176,128]{2,1,0:T(8,128)S(1)}, u32[]{:S(2)}, u32[]{:S(2)}) collective-permute-start(f32[32,176,128]{2,1,0:T(8,128)S(1)} %get-tuple-element.39), channel_id=1, source_target_pairs={{0,4},{4,0},{8,12},{12,8},{16,20},{20,16},{24,28},{28,24},{32,36},... | collective-permute-start | bytes 8650760 | tf_op jit(solution)/shard_map/ppermute | solution.py:37
  31.0 8.3 %collective-permute-start.4 = (f32[8,128,128]{2,1,0:T(8,128)S(1)}, f32[8,128,128]{2,1,0:T(8,128)S(1)}, u32[]{:S(2)}, u32[]{:S(2)}) collective-permute-start(f32[8,128,128]{2,1,0:T(8,128)S(1)} %constant_dynamic-update-slice_fusion.rest_0_), channel_id=1, source_target_pairs={{0,48},{4,196},{8,56},{12,204},{16,0},{20,212},{24,8},{28,220},{32... | collective-permute-start | bytes 1572872 | tf_op jit(solution)/shard_map/ppermute | solution.py:45
  31.0 9.9 %collective-permute-start.5 = (f32[8,128,128]{2,1,0:T(8,128)S(1)}, f32[8,128,128]{2,1,0:T(8,128)S(1)}, u32[]{:S(2)}, u32[]{:S(2)}) collective-permute-start(f32[8,128,128]{2,1,0:T(8,128)S(1)} %constant_dynamic-update-slice_fusion.rest_0_), channel_id=1, source_target_pairs={{0,32},{4,132},{8,40},{12,140},{16,48},{20,148},{24,56},{28,156},{... | collective-permute-start | bytes 1572872 | tf_op jit(solution)/shard_map/ppermute | solution.py:45
  32.3 14.2 %collective-permute-start.6 = (f32[8,128,128]{2,1,0:T(8,128)S(1)}, f32[8,128,128]{2,1,0:T(8,128)S(1)}, u32[]{:S(2)}, u32[]{:S(2)}) collective-permute-start(f32[8,128,128]{2,1,0:T(8,128)S(1)} %constant_dynamic-update-slice_fusion.rest_0_), channel_id=1, source_target_pairs={{0,16},{4,68},{8,24},{12,76},{16,32},{20,84},{24,40},{28,92},{32,4... | collective-permute-start | bytes 1572872 | tf_op jit(solution)/shard_map/ppermute | solution.py:45
  46.6 17.7 %copy-start.1 = (f32[256,172]{0,1:T(8,128)S(1)}, f32[256,172]{0,1:T(8,128)}, u32[]{:S(2)}) copy-start(f32[256,172]{0,1:T(8,128)} %param.19) | copy-start | bytes 528388
  46.7 17.7 %copy-start.5 = (f32[128,256]{1,0:T(8,128)S(1)}, f32[128,256]{1,0:T(8,128)}, u32[]{:S(2)}) copy-start(f32[128,256]{1,0:T(8,128)} %self_one.1) | copy-start | bytes 393220
  46.7 17.6 %copy-start.6 = (f32[128,256]{1,0:T(8,128)S(1)}, f32[128,256]{1,0:T(8,128)}, u32[]{:S(2)}) copy-start(f32[128,256]{1,0:T(8,128)} %neigh_one.1) | copy-start | bytes 393220
  46.7 17.6 %copy-start.7 = (f32[256]{0:T(256)S(1)}, f32[256]{0:T(256)}, u32[]{:S(2)}) copy-start(f32[256]{0:T(256)} %param.17) | copy-start | bytes 3076
  46.7 5.9 %collective-permute-start.11 = (f32[24,128,128]{2,1,0:T(8,128)S(1)}, f32[24,128,128]{2,1,0:T(8,128)S(1)}, u32[]{:S(2)}, u32[]{:S(2)}) collective-permute-start(f32[24,128,128]{2,1,0:T(8,128)S(1)} %pad_maximum_fusion.1), channel_id=1, source_target_pairs={{0,4},{4,0},{8,12},{12,8},{16,20},{20,16},{24,28},{28,24},{32,36},... | collective-permute-start | bytes 4718600 | tf_op jit(solution)/shard_map/ppermute | solution.py:37
  48.8 3.8 %collective-permute-start.7 = (f32[8,128,128]{2,1,0:T(8,128)S(1)}, f32[8,128,128]{2,1,0:T(8,128)S(1)}, u32[]{:S(2)}, u32[]{:S(2)}) collective-permute-start(f32[8,128,128]{2,1,0:T(8,128)S(1)} %constant_dynamic-update-slice_fusion.rest_0_), channel_id=1, source_target_pairs={{0,4},{4,0},{8,12},{12,8},{16,20},{20,16},{24,28},{28,24},{32,36},... | collective-permute-start | bytes 1572872 | tf_op jit(solution)/shard_map/ppermute | solution.py:37
  48.9 19.8 %collective-permute-start.19 = (f32[8,176,128]{2,1,0:T(8,128)S(1)}, f32[8,176,128]{2,1,0:T(8,128)S(1)}, u32[]{:S(2)}, u32[]{:S(2)}) collective-permute-start(f32[8,176,128]{2,1,0:T(8,128)S(1)} %get-tuple-element.45), channel_id=1, source_target_pairs={{0,128},{4,36},{8,136},{12,44},{16,144},{20,52},{24,152},{28,60},{... | collective-permute-start | bytes 2162696 | tf_op jit(solution)/shard_map/ppermute | solution.py:45
  49.5 19.3 %collective-permute-start.18 = (f32[8,176,128]{2,1,0:T(8,128)S(1)}, f32[8,176,128]{2,1,0:T(8,128)S(1)}, u32[]{:S(2)}, u32[]{:S(2)}) collective-permute-start(f32[8,176,128]{2,1,0:T(8,128)S(1)} %get-tuple-element.67), channel_id=1, source_target_pairs={{0,64},{4,20},{8,72},{12,28},{16,80},{20,36},{24,88},{28,44},{32,9... | collective-permute-start | bytes 2162696 | tf_op jit(solution)/shard_map/ppermute | solution.py:45
  50.1 18.6 %collective-permute-start.20 = (f32[8,176,128]{2,1,0:T(8,128)S(1)}, f32[8,176,128]{2,1,0:T(8,128)S(1)}, u32[]{:S(2)}, u32[]{:S(2)}) collective-permute-start(f32[8,176,128]{2,1,0:T(8,128)S(1)} %get-tuple-element.65), channel_id=1, source_target_pairs={{0,192},{4,52},{8,200},{12,60},{16,208},{20,4},{24,216},{28,12},{3... | collective-permute-start | bytes 2162696 | tf_op jit(solution)/shard_map/ppermute | solution.py:45
  54.8 4.4 %collective-permute-start.12 = (f32[2,128,128]{2,1,0:T(8,128)S(1)}, f32[2,128,128]{2,1,0:T(8,128)S(1)}, u32[]{:S(2)}, u32[]{:S(2)}) collective-permute-start(f32[2,128,128]{2,1,0:T(8,128)S(1)} %get-tuple-element.42), channel_id=1, source_target_pairs={{0,1},{1,0},{2,3},{3,2},{4,5},{5,4},{6,7},{7,6},{8,9},{9,8},{10,11... | collective-permute-start | bytes 393224 | tf_op jit(solution)/shard_map/ppermute | solution.py:55
  59.2 5.1 %collective-permute-start.13 = (f32[128,128]{1,0:T(8,128)S(1)}, f32[128,128]{1,0:T(8,128)S(1)}, u32[]{:S(2)}, u32[]{:S(2)}) collective-permute-start(f32[128,128]{1,0:T(8,128)S(1)} %fusion.8), channel_id=1, source_target_pairs={{0,2},{1,3},{2,0},{3,1},{4,6},{5,7},{6,4},{7,5},{8,10},{9,11},{10,... | collective-permute-start | bytes 196616 | tf_op jit(solution)/shard_map/ppermute | solution.py:55
  64.9 12.0 %collective-permute-start.14 = (f32[176,128]{1,0:T(8,128)S(1)}, f32[176,128]{1,0:T(8,128)S(1)}, u32[]{:S(2)}, u32[]{:S(2)}) collective-permute-start(f32[176,128]{1,0:T(8,128)S(1)} %get-tuple-element.43), channel_id=1, source_target_pairs={{0,8},{4,12},{8,0},{12,4},{16,24},{20,28},{24,16},{28,20},{32,40},... | collective-permute-start | bytes 270344 | tf_op jit(solution)/shard_map/ppermute | solution.py:41
  68.9 22.0 %copy-start.4 = (f32[256,172]{0,1:T(8,128)S(1)}, f32[256,172]{0,1:T(8,128)}, u32[]{:S(2)}) copy-start(f32[256,172]{0,1:T(8,128)} %param.18) | copy-start | bytes 528388
  68.9 21.9 %copy-start.8 = (f32[172]{0:T(256)S(1)}, f32[172]{0:T(256)}, u32[]{:S(2)}) copy-start(f32[172]{0:T(256)} %param.20) | copy-start | bytes 2068
  69.0 8.8 %collective-permute-start.21 = (f32[2,176,128]{2,1,0:T(8,128)S(1)}, f32[2,176,128]{2,1,0:T(8,128)S(1)}, u32[]{:S(2)}, u32[]{:S(2)}) collective-permute-start(f32[2,176,128]{2,1,0:T(8,128)S(1)} %get-tuple-element.71), channel_id=1, source_target_pairs={{0,16},{4,68},{8,24},{12,76},{16,32},{20,84},{24,40},{28,92},{32,4... | collective-permute-start | bytes 540680 | tf_op jit(solution)/shard_map/ppermute | solution.py:45
  69.3 10.6 %collective-permute-start.22 = (f32[2,176,128]{2,1,0:T(8,128)S(1)}, f32[2,176,128]{2,1,0:T(8,128)S(1)}, u32[]{:S(2)}, u32[]{:S(2)}) collective-permute-start(f32[2,176,128]{2,1,0:T(8,128)S(1)} %get-tuple-element.70), channel_id=1, source_target_pairs={{0,32},{4,132},{8,40},{12,140},{16,48},{20,148},{24,56},{28,156},{... | collective-permute-start | bytes 540680 | tf_op jit(solution)/shard_map/ppermute | solution.py:45
  74.9 5.1 %collective-permute-start.23 = (f32[2,176,128]{2,1,0:T(8,128)S(1)}, f32[2,176,128]{2,1,0:T(8,128)S(1)}, u32[]{:S(2)}, u32[]{:S(2)}) collective-permute-start(f32[2,176,128]{2,1,0:T(8,128)S(1)} %get-tuple-element.69), channel_id=1, source_target_pairs={{0,48},{4,196},{8,56},{12,204},{16,0},{20,212},{24,8},{28,220},{32... | collective-permute-start | bytes 540680 | tf_op jit(solution)/shard_map/ppermute | solution.py:45
  76.9 6.6 %collective-permute-start.15 = (f32[2,176,128]{2,1,0:T(8,128)S(1)}, f32[2,176,128]{2,1,0:T(8,128)S(1)}, u32[]{:S(2)}, u32[]{:S(2)}) collective-permute-start(f32[2,176,128]{2,1,0:T(8,128)S(1)} %pad_maximum_fusion.6), channel_id=1, source_target_pairs={{0,192},{4,52},{8,200},{12,60},{16,208},{20,4},{24,216},{28,12},{3... | collective-permute-start | bytes 540680 | tf_op jit(solution)/shard_map/ppermute | solution.py:45
  77.0 6.7 %collective-permute-start.16 = (f32[2,176,128]{2,1,0:T(8,128)S(1)}, f32[2,176,128]{2,1,0:T(8,128)S(1)}, u32[]{:S(2)}, u32[]{:S(2)}) collective-permute-start(f32[2,176,128]{2,1,0:T(8,128)S(1)} %pad_maximum_fusion.6), channel_id=1, source_target_pairs={{0,128},{4,36},{8,136},{12,44},{16,144},{20,52},{24,152},{28,60},{... | collective-permute-start | bytes 540680 | tf_op jit(solution)/shard_map/ppermute | solution.py:45
  77.8 7.8 %collective-permute-start.17 = (f32[2,176,128]{2,1,0:T(8,128)S(1)}, f32[2,176,128]{2,1,0:T(8,128)S(1)}, u32[]{:S(2)}, u32[]{:S(2)}) collective-permute-start(f32[2,176,128]{2,1,0:T(8,128)S(1)} %pad_maximum_fusion.6), channel_id=1, source_target_pairs={{0,64},{4,20},{8,72},{12,28},{16,80},{20,36},{24,88},{28,44},{32,9... | collective-permute-start | bytes 540680 | tf_op jit(solution)/shard_map/ppermute | solution.py:45
  80.1 8.0 %collective-permute-start.24 = (f32[176,128]{1,0:T(8,128)S(1)}, f32[176,128]{1,0:T(8,128)S(1)}, u32[]{:S(2)}, u32[]{:S(2)}) collective-permute-start(f32[176,128]{1,0:T(8,128)S(1)} %get-tuple-element.76), channel_id=1, source_target_pairs={{0,8},{4,12},{8,0},{12,4},{16,24},{20,28},{24,16},{28,20},{32,40},... | collective-permute-start | bytes 270344 | tf_op jit(solution)/shard_map/ppermute | solution.py:41
  88.1 16.8 %collective-permute-start.25 = (f32[8,176,128]{2,1,0:T(8,128)S(1)}, f32[8,176,128]{2,1,0:T(8,128)S(1)}, u32[]{:S(2)}, u32[]{:S(2)}) collective-permute-start(f32[8,176,128]{2,1,0:T(8,128)S(1)} %pad_maximum_fusion.2.rest_0_), channel_id=1, source_target_pairs={{0,48},{4,196},{8,56},{12,204},{16,0},{20,212},{24,8},{28,220},{32... | collective-permute-start | bytes 2162696 | tf_op jit(solution)/shard_map/ppermute | solution.py:45
  90.9 14.3 %collective-permute-start.27 = (f32[8,176,128]{2,1,0:T(8,128)S(1)}, f32[8,176,128]{2,1,0:T(8,128)S(1)}, u32[]{:S(2)}, u32[]{:S(2)}) collective-permute-start(f32[8,176,128]{2,1,0:T(8,128)S(1)} %pad_maximum_fusion.2.rest_0_), channel_id=1, source_target_pairs={{0,16},{4,68},{8,24},{12,76},{16,32},{20,84},{24,40},{28,92},{32,4... | collective-permute-start | bytes 2162696 | tf_op jit(solution)/shard_map/ppermute | solution.py:45
  92.4 8.2 %collective-permute-start.30 = (f32[4,160,128]{2,1,0:T(8,128)S(1)}, f32[4,160,128]{2,1,0:T(8,128)S(1)}, u32[]{:S(2)}, u32[]{:S(2)}) collective-permute-start(f32[4,160,128]{2,1,0:T(8,128)S(1)} %get-tuple-element.51), channel_id=1, source_target_pairs={{0,4},{4,0},{8,12},{12,8},{16,20},{20,16},{24,28},{28,24},{32,36},... | collective-permute-start | bytes 983048 | tf_op jit(solution)/shard_map/ppermute | solution.py:37
  100.6 6.1 %collective-permute-start.31 = (f32[160,128]{1,0:T(8,128)S(1)}, f32[160,128]{1,0:T(8,128)S(1)}, u32[]{:S(2)}, u32[]{:S(2)}) collective-permute-start(f32[160,128]{1,0:T(8,128)S(1)} %get-tuple-element.74), channel_id=1, source_target_pairs={{0,64},{4,20},{8,72},{12,28},{16,80},{20,36},{24,88},{28,44},{32,9... | collective-permute-start | bytes 245768 | tf_op jit(solution)/shard_map/ppermute | solution.py:45
  100.7 8.6 %collective-permute-start.32 = (f32[160,128]{1,0:T(8,128)S(1)}, f32[160,128]{1,0:T(8,128)S(1)}, u32[]{:S(2)}, u32[]{:S(2)}) collective-permute-start(f32[160,128]{1,0:T(8,128)S(1)} %get-tuple-element.73), channel_id=1, source_target_pairs={{0,128},{4,36},{8,136},{12,44},{16,144},{20,52},{24,152},{28,60},{... | collective-permute-start | bytes 245768 | tf_op jit(solution)/shard_map/ppermute | solution.py:45
  104.8 4.5 %collective-permute-start.33 = (f32[160,128]{1,0:T(8,128)S(1)}, f32[160,128]{1,0:T(8,128)S(1)}, u32[]{:S(2)}, u32[]{:S(2)}) collective-permute-start(f32[160,128]{1,0:T(8,128)S(1)} %get-tuple-element.72), channel_id=1, source_target_pairs={{0,192},{4,52},{8,200},{12,60},{16,208},{20,4},{24,216},{28,12},{3... | collective-permute-start | bytes 245768 | tf_op jit(solution)/shard_map/ppermute | solution.py:45
  104.8 13.4 %collective-permute-start.26 = (f32[4,176,128]{2,1,0:T(8,128)S(1)}, f32[4,176,128]{2,1,0:T(8,128)S(1)}, u32[]{:S(2)}, u32[]{:S(2)}) collective-permute-start(f32[4,176,128]{2,1,0:T(8,128)S(1)} %slice.122), channel_id=1, source_target_pairs={{0,48},{4,196},{8,56},{12,204},{16,0},{20,212},{24,8},{28,220},{32... | collective-permute-start | bytes 1081352 | tf_op jit(solution)/shard_map/ppermute | solution.py:45
  105.2 13.1 %collective-permute-start.28 = (f32[4,176,128]{2,1,0:T(8,128)S(1)}, f32[4,176,128]{2,1,0:T(8,128)S(1)}, u32[]{:S(2)}, u32[]{:S(2)}) collective-permute-start(f32[4,176,128]{2,1,0:T(8,128)S(1)} %slice.123), channel_id=1, source_target_pairs={{0,16},{4,68},{8,24},{12,76},{16,32},{20,84},{24,40},{28,92},{32,4... | collective-permute-start | bytes 1081352 | tf_op jit(solution)/shard_map/ppermute | solution.py:45
  109.4 3.7 %collective-permute-start.34 = (f32[160,128]{1,0:T(8,128)S(1)}, f32[160,128]{1,0:T(8,128)S(1)}, u32[]{:S(2)}, u32[]{:S(2)}) collective-permute-start(f32[160,128]{1,0:T(8,128)S(1)} %fusion.7), channel_id=1, source_target_pairs={{0,1},{1,0},{2,3},{3,2},{4,5},{5,4},{6,7},{7,6},{8,9},{9,8},{10,11... | collective-permute-start | bytes 245768 | tf_op jit(solution)/shard_map/ppermute | solution.py:55
  113.1 5.2 %collective-permute-start.35 = (f32[160,128]{1,0:T(8,128)S(1)}, f32[160,128]{1,0:T(8,128)S(1)}, u32[]{:S(2)}, u32[]{:S(2)}) collective-permute-start(f32[160,128]{1,0:T(8,128)S(1)} %add.116), channel_id=1, source_target_pairs={{0,2},{1,3},{2,0},{3,1},{4,6},{5,7},{6,4},{7,5},{8,10},{9,11},{10,... | collective-permute-start | bytes 245768 | tf_op jit(solution)/shard_map/ppermute | solution.py:55
  118.4 10.0 %collective-permute-start.36 = (f32[24,176,128]{2,1,0:T(8,128)S(1)}, f32[24,176,128]{2,1,0:T(8,128)S(1)}, u32[]{:S(2)}, u32[]{:S(2)}) collective-permute-start(f32[24,176,128]{2,1,0:T(8,128)S(1)} %pad_maximum_fusion), channel_id=1, source_target_pairs={{0,4},{4,0},{8,12},{12,8},{16,20},{20,16},{24,28},{28,24},{32,36},... | collective-permute-start | bytes 6488072 | tf_op jit(solution)/shard_map/ppermute | solution.py:37
  123.5 4.9 %collective-permute-start.29 = (f32[8,176,128]{2,1,0:T(8,128)S(1)}, f32[8,176,128]{2,1,0:T(8,128)S(1)}, u32[]{:S(2)}, u32[]{:S(2)}) collective-permute-start(f32[8,176,128]{2,1,0:T(8,128)S(1)} %pad_maximum_fusion.2.rest_0_), channel_id=1, source_target_pairs={{0,4},{4,0},{8,12},{12,8},{16,20},{20,16},{24,28},{28,24},{32,36},... | collective-permute-start | bytes 2162696 | tf_op jit(solution)/shard_map/ppermute | solution.py:37
  123.6 8.7 %collective-permute-start.39 = (f32[160,128]{1,0:T(8,128)S(1)}, f32[160,128]{1,0:T(8,128)S(1)}, u32[]{:S(2)}, u32[]{:S(2)}) collective-permute-start(f32[160,128]{1,0:T(8,128)S(1)} %add.117), channel_id=1, source_target_pairs={{0,8},{4,12},{8,0},{12,4},{16,24},{20,28},{24,16},{28,20},{32,40},... | collective-permute-start | bytes 245768 | tf_op jit(solution)/shard_map/ppermute | solution.py:41
  132.3 5.5 %collective-permute-start.40 = (f32[160,128]{1,0:T(8,128)S(1)}, f32[160,128]{1,0:T(8,128)S(1)}, u32[]{:S(2)}, u32[]{:S(2)}) collective-permute-start(f32[160,128]{1,0:T(8,128)S(1)} %add.120), channel_id=1, source_target_pairs={{0,16},{4,68},{8,24},{12,76},{16,32},{20,84},{24,40},{28,92},{32,4... | collective-permute-start | bytes 245768 | tf_op jit(solution)/shard_map/ppermute | solution.py:45
  132.4 5.4 %collective-permute-start.41 = (f32[160,128]{1,0:T(8,128)S(1)}, f32[160,128]{1,0:T(8,128)S(1)}, u32[]{:S(2)}, u32[]{:S(2)}) collective-permute-start(f32[160,128]{1,0:T(8,128)S(1)} %add.120), channel_id=1, source_target_pairs={{0,32},{4,132},{8,40},{12,140},{16,48},{20,148},{24,56},{28,156},{... | collective-permute-start | bytes 245768 | tf_op jit(solution)/shard_map/ppermute | solution.py:45
  134.6 3.8 %collective-permute-start.42 = (f32[160,128]{1,0:T(8,128)S(1)}, f32[160,128]{1,0:T(8,128)S(1)}, u32[]{:S(2)}, u32[]{:S(2)}) collective-permute-start(f32[160,128]{1,0:T(8,128)S(1)} %add.120), channel_id=1, source_target_pairs={{0,48},{4,196},{8,56},{12,204},{16,0},{20,212},{24,8},{28,220},{32... | collective-permute-start | bytes 245768 | tf_op jit(solution)/shard_map/ppermute | solution.py:45
  135.4 4.6 %collective-permute-start.37 = (f32[2,176,128]{2,1,0:T(8,128)S(1)}, f32[2,176,128]{2,1,0:T(8,128)S(1)}, u32[]{:S(2)}, u32[]{:S(2)}) collective-permute-start(f32[2,176,128]{2,1,0:T(8,128)S(1)} %get-tuple-element.54), channel_id=1, source_target_pairs={{0,1},{1,0},{2,3},{3,2},{4,5},{5,4},{6,7},{7,6},{8,9},{9,8},{10,11... | collective-permute-start | bytes 540680 | tf_op jit(solution)/shard_map/ppermute | solution.py:55
  140.1 7.4 %collective-permute-start.43 = (f32[160,128]{1,0:T(8,128)S(1)}, f32[160,128]{1,0:T(8,128)S(1)}, u32[]{:S(2)}, u32[]{:S(2)}) collective-permute-start(f32[160,128]{1,0:T(8,128)S(1)} %add_add_fusion.1), channel_id=1, source_target_pairs={{0,192},{4,52},{8,200},{12,60},{16,208},{20,4},{24,216},{28,12},{3... | collective-permute-start | bytes 245768 | tf_op jit(solution)/shard_map/ppermute | solution.py:45
  145.2 4.9 %collective-permute-start.44 = (f32[160,128]{1,0:T(8,128)S(1)}, f32[160,128]{1,0:T(8,128)S(1)}, u32[]{:S(2)}, u32[]{:S(2)}) collective-permute-start(f32[160,128]{1,0:T(8,128)S(1)} %add_add_fusion.1), channel_id=1, source_target_pairs={{0,128},{4,36},{8,136},{12,44},{16,144},{20,52},{24,152},{28,60},{... | collective-permute-start | bytes 245768 | tf_op jit(solution)/shard_map/ppermute | solution.py:45
  145.2 5.4 %collective-permute-start.45 = (f32[160,128]{1,0:T(8,128)S(1)}, f32[160,128]{1,0:T(8,128)S(1)}, u32[]{:S(2)}, u32[]{:S(2)}) collective-permute-start(f32[160,128]{1,0:T(8,128)S(1)} %add_add_fusion.1), channel_id=1, source_target_pairs={{0,64},{4,20},{8,72},{12,28},{16,80},{20,36},{24,88},{28,44},{32,9... | collective-permute-start | bytes 245768 | tf_op jit(solution)/shard_map/ppermute | solution.py:45
  145.8 7.1 %collective-permute-start.38 = (f32[176,128]{1,0:T(8,128)S(1)}, f32[176,128]{1,0:T(8,128)S(1)}, u32[]{:S(2)}, u32[]{:S(2)}) collective-permute-start(f32[176,128]{1,0:T(8,128)S(1)} %fusion.1), channel_id=1, source_target_pairs={{0,2},{1,3},{2,0},{3,1},{4,6},{5,7},{6,4},{7,5},{8,10},{9,11},{10,... | collective-permute-start | bytes 270344 | tf_op jit(solution)/shard_map/ppermute | solution.py:55
  153.0 1.8 %collective-permute-start.46 = (f32[4,160,128]{2,1,0:T(8,128)S(1)}, f32[4,160,128]{2,1,0:T(8,128)S(1)}, u32[]{:S(2)}, u32[]{:S(2)}) collective-permute-start(f32[4,160,128]{2,1,0:T(8,128)S(1)} %pad_maximum_fusion.4.q), channel_id=1, source_target_pairs={{0,4},{4,0},{8,12},{12,8},{16,20},{20,16},{24,28},{28,24},{32,36},... | collective-permute-start | bytes 983048 | tf_op jit(solution)/shard_map/ppermute | solution.py:37

commit v4 on v3

--- a/solution.py
+++ b/solution.py
@@ -308,7 +308,7 @@
 
 def scatter_plane(q):
     q = add4(q[:2], *(send_plane(q[2 * d : 2 * d + 2], 1, d) for d in (1, 2, 3)))
-    return q[0], send_z(q[1])
+    return q
 
 
 def reduce_lane(same, other):
@@ -387,14 +387,15 @@
         hidden_kernel, [block, (SIDE, 256), padded],
         (kept, got, last, features, self_one, neigh_one, bias_one.reshape(1, -1), nt),
     )
-    g, gz = scatter_plane(q)
+    q_two = scatter_plane(q)
+    g, gz = q_two[0], send_z(q_two[1])
     lane = gather_lane(yt, send_z(yt))
     base, same, other = call(
         grad_kernel, [tall, (4, 160, SIDE), (4, 160, SIDE)],
         (meta, g, gz, after(pre, lane), sums, features, ct, st, nt, bias_two.reshape(1, -1)),
         scratch=(pltpu.VMEM((GROWS, SIDE), F32),), smem=1,
     )
-    plane = gather_ring(after(lane, gz))
+    plane = gather_ring(after(lane, q_two))
     kept = reduce_lane(same, other)
     kept = kept + swap_rep(kept, 1)
     kept = kept + swap_rep(kept, 2)

time: 156 us -> 152 us (0.974)
  starting transfers between devices: 72.3 us -> 63.5 us
  Pallas kernels: 13.5 us -> 19.8 us
    ppermute x28, starting transfers between devices: 35.8 us -> 28.9 us  [send_plane(): lax.ppermute(a, 'row', row_perm(lambda c: (d, 0, 0, 0) if c == stage else...]
    pallas_call x8, Pallas kernels: 13.5 us -> 19.8 us  [call(): pl.pallas_call(kernel, out_shape=[jax.ShapeDtypeStruct(s, dtype) for s in...]
    ppermute x28, waiting for transfers between devices: 31.1 us -> 34.5 us  [send_plane(): lax.ppermute(a, 'row', row_perm(lambda c: (d, 0, 0, 0) if c == stage else...]
    ppermute x4, starting transfers between devices: 13.7 us -> 11.8 us  [send_z(): return lax.ppermute(a, 'row', row_perm(lambda c: (0, 0, 1, 0)))]
    ppermute x8, waiting for transfers between devices: 20.3 us -> 18.7 us  [swap_rep(): return lax.ppermute(a, 'rep', [(j, j ^ bit) for j in range(NR)])]
    ppermute x4, waiting for transfers between devices: 2.41 us -> 0.81 us  [send_z(): return lax.ppermute(a, 'row', row_perm(lambda c: (0, 0, 1, 0)))]
  transfers between devices with their start and end apart: 47 -> 47, of which waited for: 29 -> 28; matrix products, arithmetic and copies ran while one was open for 2% -> 2% of each run, Pallas kernels for 6% -> 9%
where the time goes in v4:
time: 152 us; the launch traced here: 153 us
  starting transfers between devices  63.5 us (42%)
  waiting for transfers between devices  63.5 us (42%)
  Pallas kernels  19.8 us (13%)
  other arithmetic  3.24 us (2%)
  local copies, waits for them, and re-layouts  2.37 us (2%)
    ppermute x28, waiting for transfers between devices, send_plane(): lax.ppermute(a, 'row', row_perm(lambda c: (d, 0, 0, 0) if c == stage else...  34.5 us
    ppermute x28, starting transfers between devices, send_plane(): lax.ppermute(a, 'row', row_perm(lambda c: (d, 0, 0, 0) if c == stage else...  28.9 us
    pallas_call x8, Pallas kernels, call(): pl.pallas_call(kernel, out_shape=[jax.ShapeDtypeStruct(s, dtype) for s in...  19.8 us
    ppermute x8, waiting for transfers between devices, swap_rep(): return lax.ppermute(a, 'rep', [(j, j ^ bit) for j in range(NR)])  18.7 us
    ppermute x7, starting transfers between devices, send_core(): return lax.ppermute(a, 'row', row_perm(lambda c: (0, 0, 0, 1)))  17.8 us
    ppermute x4, starting transfers between devices, send_z(): return lax.ppermute(a, 'row', row_perm(lambda c: (0, 0, 1, 0)))  11.8 us
    ppermute x7, waiting for transfers between devices, send_core(): return lax.ppermute(a, 'row', row_perm(lambda c: (0, 0, 0, 1)))  9.51 us
    ppermute x8, starting transfers between devices, swap_rep(): return lax.ppermute(a, 'rep', [(j, j ^ bit) for j in range(NR)])  4.95 us
  transfers between devices with their start and end apart: 47, of which 28 were waited for; matrix products, arithmetic and copies ran while one was open for 2% of the time, Pallas kernels for 9%

profile of v4, /device:TPU:1, one launch (start us, length us, event | category | flops | bytes accessed | tf_op | source)
XLA Modules:
  0.0 153.4 jit_solution(7597040744235834082)
XLA Ops:
  0.6 7.8 %collective-permute-start = (f32[128,128]{1,0:T(8,128)}, f32[128,128]{1,0:T(8,128)S(1)}, u32[]{:S(2)}, u32[]{:S(2)}) collective-permute-start(f32[128,128]{1,0:T(8,128)} %feat.3), channel_id=1, source_target_pairs={{0,8},{4,12},{8,0},{12,4},{16,24},{20,28},{24,16},{28,20},{32,40},... | collective-permute-start | bytes 196616 | tf_op jit(solution)/shard_map/ppermute | solution.py:41
  8.5 1.2 collective-permute-start.8
  10.2 1.3 reduce.3
  11.6 0.7 pad_add_fusion.meta
  12.3 1.6 %copy-done = f32[4,1,8,128,128]{4,3,2,1,0:T(8,128)S(1)} copy-done((f32[4,1,8,128,128]{4,3,2,1,0:T(8,128)S(1)}, f32[4,1,8,128,128]{4,3,2,1,0:T(8,128)}, u32[]{:S(2)}) %copy-start) | copy-done | bytes 2097176
  13.9 0.8 shard_map.162.tiles
  14.8 2.8 %collective-permute-start.1 = (f32[2,128,128]{2,1,0:T(8,128)S(1)}, f32[2,128,128]{2,1,0:T(8,128)S(1)}, u32[]{:S(2)}, u32[]{:S(2)}) collective-permute-start(f32[2,128,128]{2,1,0:T(8,128)S(1)} %pad_maximum_fusion.7), channel_id=1, source_target_pairs={{0,192},{4,52},{8,200},{12,60},{16,208},{20,4},{24,216},{28,12},{3... | collective-permute-start | bytes 393224 | tf_op jit(solution)/shard_map/ppermute | solution.py:45
  18.0 0.7 collective-permute-start.3
  18.8 0.8 collective-permute-start.9
  19.6 1.3 collective-permute-done.1
  20.9 2.2 %collective-permute-done.2 = f32[2,128,128]{2,1,0:T(8,128)S(1)} collective-permute-done((f32[2,128,128]{2,1,0:T(8,128)S(1)}, f32[2,128,128]{2,1,0:T(8,128)S(1)}, u32[]{:S(2)}, u32[]{:S(2)}) %collective-permute-start.2) | collective-permute-done | bytes 131104 | tf_op jit(solution)/shard_map/ppermute | solution.py:45
  23.1 1.6 %collective-permute-done.3 = f32[2,128,128]{2,1,0:T(8,128)S(1)} collective-permute-done((f32[2,128,128]{2,1,0:T(8,128)S(1)}, f32[2,128,128]{2,1,0:T(8,128)S(1)}, u32[]{:S(2)}, u32[]{:S(2)}) %collective-permute-start.3) | collective-permute-done | bytes 131104 | tf_op jit(solution)/shard_map/ppermute | solution.py:45
  24.7 4.6 %shard_map.163 = (f32[32,176,128]{2,1,0:T(8,128)S(1)}, f32[32,176,128]{2,1,0:T(8,128)S(1)}) custom-call(s32[38]{0:T(128)S(1)} %pad_add_fusion.meta, bf16[4,8,128,256]{3,2,1,0:T(8,128)(2,1)S(1)} %shard_map.162.tiles, f32[2,172,128]{2,1,0:T(8,128)S(1)} %pad_maximum_fusion.5.near, f32[2,172,128]{2,1,0:T(8,128)S(1)} %collective-permute-done.9.far), custom_call_target="tpu_custom_call" | custom-call | bytes 12582912 | tf_op jit(solution)/shard_map/pallas_call | solution.py:260
  29.4 1.1 collective-permute-start.4
  30.6 1.2 collective-permute-start.5
  31.8 2.9 %collective-permute-done.10 = f32[32,176,128]{2,1,0:T(8,128)S(1)} collective-permute-done((f32[32,176,128]{2,1,0:T(8,128)S(1)}, f32[32,176,128]{2,1,0:T(8,128)S(1)}, u32[]{:S(2)}, u32[]{:S(2)}) %collective-permute-start.10) | collective-permute-done | bytes 2883616 | tf_op jit(solution)/shard_map/ppermute | solution.py:37
  35.1 2.8 %collective-permute-done.4.rest_1_ = f32[8,128,128]{2,1,0:T(8,128)S(1)} collective-permute-done((f32[8,128,128]{2,1,0:T(8,128)S(1)}, f32[8,128,128]{2,1,0:T(8,128)S(1)}, u32[]{:S(2)}, u32[]{:S(2)}) %collective-permute-start.4) | collective-permute-done | bytes 524320 | tf_op jit(solution)/shard_map/ppermute | solution.py:45
  37.8 2.6 %collective-permute-done.5.rest_2_ = f32[8,128,128]{2,1,0:T(8,128)S(1)} collective-permute-done((f32[8,128,128]{2,1,0:T(8,128)S(1)}, f32[8,128,128]{2,1,0:T(8,128)S(1)}, u32[]{:S(2)}, u32[]{:S(2)}) %collective-permute-start.5) | collective-permute-done | bytes 524320 | tf_op jit(solution)/shard_map/ppermute | solution.py:45
  40.4 5.6 %collective-permute-done.6.rest_3_ = f32[8,128,128]{2,1,0:T(8,128)S(1)} collective-permute-done((f32[8,128,128]{2,1,0:T(8,128)S(1)}, f32[8,128,128]{2,1,0:T(8,128)S(1)}, u32[]{:S(2)}, u32[]{:S(2)}) %collective-permute-start.6) | collective-permute-done | bytes 524320 | tf_op jit(solution)/shard_map/ppermute | solution.py:45
  46.2 2.4 %collective-permute-start.11 = (f32[24,128,128]{2,1,0:T(8,128)S(1)}, f32[24,128,128]{2,1,0:T(8,128)S(1)}, u32[]{:S(2)}, u32[]{:S(2)}) collective-permute-start(f32[24,128,128]{2,1,0:T(8,128)S(1)} %pad_maximum_fusion.1), channel_id=1, source_target_pairs={{0,4},{4,0},{8,12},{12,8},{16,20},{20,16},{24,28},{28,24},{32,36},... | collective-permute-start | bytes 4718600 | tf_op jit(solution)/shard_map/ppermute | solution.py:37
  48.7 2.4 %collective-permute-start.19 = (f32[8,176,128]{2,1,0:T(8,128)S(1)}, f32[8,176,128]{2,1,0:T(8,128)S(1)}, u32[]{:S(2)}, u32[]{:S(2)}) collective-permute-start(f32[8,176,128]{2,1,0:T(8,128)S(1)} %get-tuple-element.45), channel_id=1, source_target_pairs={{0,128},{4,36},{8,136},{12,44},{16,144},{20,52},{24,152},{28,60},{... | collective-permute-start | bytes 2162696 | tf_op jit(solution)/shard_map/ppermute | solution.py:45
  51.1 2.7 %collective-permute-start.20 = (f32[8,176,128]{2,1,0:T(8,128)S(1)}, f32[8,176,128]{2,1,0:T(8,128)S(1)}, u32[]{:S(2)}, u32[]{:S(2)}) collective-permute-start(f32[8,176,128]{2,1,0:T(8,128)S(1)} %get-tuple-element.65), channel_id=1, source_target_pairs={{0,192},{4,52},{8,200},{12,60},{16,208},{20,4},{24,216},{28,12},{3... | collective-permute-start | bytes 2162696 | tf_op jit(solution)/shard_map/ppermute | solution.py:45
  53.8 4.1 %shard_map.164 = (f32[2,128,128]{2,1,0:T(8,128)S(1)}, f32[2,128,128]{2,1,0:T(8,128)S(1)}) custom-call(s32[38]{0:T(128)S(1)} %pad_add_fusion.meta, bf16[4,8,128,256]{3,2,1,0:T(8,128)(2,1)S(1)} %shard_map.162.tiles, f32[8,128,128]{2,1,0:T(8,128)S(1)} %constant_dynamic-update-slice_fusion.rest_0_, f32[8,128,128]{2,1,0:T(8,128)S(1)} %collective-permute-done.4.rest_1_, ...), custom_call_target="tpu_custom_call" | custom-call | bytes 12582912 | tf_op jit(solution)/shard_map/pallas_call | solution.py:260
  57.9 1.3 collective-permute-start.12
  59.1 3.1 %collective-permute-done.12.got = f32[2,128,128]{2,1,0:T(8,128)S(1)} collective-permute-done((f32[2,128,128]{2,1,0:T(8,128)S(1)}, f32[2,128,128]{2,1,0:T(8,128)S(1)}, u32[]{:S(2)}, u32[]{:S(2)}) %collective-permute-start.12) | collective-permute-done | bytes 131104 | tf_op jit(solution)/shard_map/ppermute | solution.py:55
  62.2 1.4 collective-permute-start.13
  63.6 3.0 %collective-permute-done.13.last = f32[128,128]{1,0:T(8,128)S(1)} collective-permute-done((f32[128,128]{1,0:T(8,128)S(1)}, f32[128,128]{1,0:T(8,128)S(1)}, u32[]{:S(2)}, u32[]{:S(2)}) %collective-permute-start.13) | collective-permute-done | bytes 65568 | tf_op jit(solution)/shard_map/ppermute | solution.py:55
  67.4 1.0 collective-permute-done.18
  68.6 3.2 %collective-permute-start.21 = (f32[2,176,128]{2,1,0:T(8,128)S(1)}, f32[2,176,128]{2,1,0:T(8,128)S(1)}, u32[]{:S(2)}, u32[]{:S(2)}) collective-permute-start(f32[2,176,128]{2,1,0:T(8,128)S(1)} %get-tuple-element.71), channel_id=1, source_target_pairs={{0,16},{4,68},{8,24},{12,76},{16,32},{20,84},{24,40},{28,92},{32,4... | collective-permute-start | bytes 540680 | tf_op jit(solution)/shard_map/ppermute | solution.py:45
  71.8 2.5 %collective-permute-start.23 = (f32[2,176,128]{2,1,0:T(8,128)S(1)}, f32[2,176,128]{2,1,0:T(8,128)S(1)}, u32[]{:S(2)}, u32[]{:S(2)}) collective-permute-start(f32[2,176,128]{2,1,0:T(8,128)S(1)} %get-tuple-element.69), channel_id=1, source_target_pairs={{0,48},{4,196},{8,56},{12,204},{16,0},{20,212},{24,8},{28,220},{32... | collective-permute-start | bytes 540680 | tf_op jit(solution)/shard_map/ppermute | solution.py:45
  74.3 0.8 collective-permute-done.14
  75.2 0.7 collective-permute-start.16
  75.9 0.8 collective-permute-start.17
  76.6 1.0 collective-permute-done.22
  77.7 3.9 %collective-permute-start.29 = (f32[176,128]{1,0:T(8,128)S(1)}, f32[176,128]{1,0:T(8,128)S(1)}, u32[]{:S(2)}, u32[]{:S(2)}) collective-permute-start(f32[176,128]{1,0:T(8,128)S(1)} %get-tuple-element.75), channel_id=1, source_target_pairs={{0,8},{4,12},{8,0},{12,4},{16,24},{20,28},{24,16},{28,20},{32,40},... | collective-permute-start | bytes 270344 | tf_op jit(solution)/shard_map/ppermute | solution.py:41
  81.6 1.6 %collective-permute-done.16 = f32[2,176,128]{2,1,0:T(8,128)S(1)} collective-permute-done((f32[2,176,128]{2,1,0:T(8,128)S(1)}, f32[2,176,128]{2,1,0:T(8,128)S(1)}, u32[]{:S(2)}, u32[]{:S(2)}) %collective-permute-start.16) | collective-permute-done | bytes 180256 | tf_op jit(solution)/shard_map/ppermute | solution.py:45
  83.2 3.5 %collective-permute-done.17 = f32[2,176,128]{2,1,0:T(8,128)S(1)} collective-permute-done((f32[2,176,128]{2,1,0:T(8,128)S(1)}, f32[2,176,128]{2,1,0:T(8,128)S(1)}, u32[]{:S(2)}, u32[]{:S(2)}) %collective-permute-start.17) | collective-permute-done | bytes 180256 | tf_op jit(solution)/shard_map/ppermute | solution.py:45
  86.9 1.5 collective-permute-start.26
  88.3 1.5 %shard_map.166 = (f32[172,128]{1,0:T(8,128)S(1)}, f32[4,160,128]{2,1,0:T(8,128)S(1)}, f32[4,160,128]{2,1,0:T(8,128)S(1)}) custom-call(s32[38]{0:T(128)S(1)} %pad_add_fusion.meta, f32[176,128]{1,0:T(8,128)S(1)} %get-tuple-element.76.g, f32[176,128]{1,0:T(8,128)S(1)} %collective-permute-done.29.gz, f32[128,256]{1,0:T(8,128)S(1)} %get-tuple-element.48.pre, ...), custom_call_target="tpu_custom_call" | custom-call | bytes 6291456 | tf_op jit(solution)/shard_map/pallas_call | solution.py:260
  89.9 9.6 %collective-permute-start.30 = (f32[4,160,128]{2,1,0:T(8,128)S(1)}, f32[4,160,128]{2,1,0:T(8,128)S(1)}, u32[]{:S(2)}, u32[]{:S(2)}) collective-permute-start(f32[4,160,128]{2,1,0:T(8,128)S(1)} %get-tuple-element.51), channel_id=1, source_target_pairs={{0,4},{4,0},{8,12},{12,8},{16,20},{20,16},{24,28},{28,24},{32,36},... | collective-permute-start | bytes 983048 | tf_op jit(solution)/shard_map/ppermute | solution.py:37
  99.5 1.3 collective-permute-done.30
  100.9 2.2 %collective-permute-start.32 = (f32[160,128]{1,0:T(8,128)S(1)}, f32[160,128]{1,0:T(8,128)S(1)}, u32[]{:S(2)}, u32[]{:S(2)}) collective-permute-start(f32[160,128]{1,0:T(8,128)S(1)} %get-tuple-element.73), channel_id=1, source_target_pairs={{0,128},{4,36},{8,136},{12,44},{16,144},{20,52},{24,152},{28,60},{... | collective-permute-start | bytes 245768 | tf_op jit(solution)/shard_map/ppermute | solution.py:45
  103.6 1.1 collective-permute-start.25
  104.7 0.7 collective-permute-start.27
  105.4 2.0 %collective-permute-done.31 = f32[160,128]{1,0:T(8,128)S(1)} collective-permute-done((f32[160,128]{1,0:T(8,128)S(1)}, f32[160,128]{1,0:T(8,128)S(1)}, u32[]{:S(2)}, u32[]{:S(2)}) %collective-permute-start.31) | collective-permute-done | bytes 81952 | tf_op jit(solution)/shard_map/ppermute | solution.py:45
  107.5 1.0 collective-permute-done.33
  108.6 3.6 %collective-permute-done.34 = f32[160,128]{1,0:T(8,128)S(1)} collective-permute-done((f32[160,128]{1,0:T(8,128)S(1)}, f32[160,128]{1,0:T(8,128)S(1)}, u32[]{:S(2)}, u32[]{:S(2)}) %collective-permute-start.34) | collective-permute-done | bytes 81952 | tf_op jit(solution)/shard_map/ppermute | solution.py:55
  112.3 5.1 %collective-permute-done.35 = f32[160,128]{1,0:T(8,128)S(1)} collective-permute-done((f32[160,128]{1,0:T(8,128)S(1)}, f32[160,128]{1,0:T(8,128)S(1)}, u32[]{:S(2)}, u32[]{:S(2)}) %collective-permute-start.35) | collective-permute-done | bytes 81952 | tf_op jit(solution)/shard_map/ppermute | solution.py:55
  117.5 4.1 %collective-permute-start.36 = (f32[24,176,128]{2,1,0:T(8,128)S(1)}, f32[24,176,128]{2,1,0:T(8,128)S(1)}, u32[]{:S(2)}, u32[]{:S(2)}) collective-permute-start(f32[24,176,128]{2,1,0:T(8,128)S(1)} %pad_maximum_fusion), channel_id=1, source_target_pairs={{0,4},{4,0},{8,12},{12,8},{16,20},{20,16},{24,28},{28,24},{32,36},... | collective-permute-start | bytes 6488072 | tf_op jit(solution)/shard_map/ppermute | solution.py:37
  121.7 4.8 %collective-permute-done.28.rest_4_ = f32[8,176,128]{2,1,0:T(8,128)S(1)} collective-permute-done((f32[8,176,128]{2,1,0:T(8,128)S(1)}, f32[8,176,128]{2,1,0:T(8,128)S(1)}, u32[]{:S(2)}, u32[]{:S(2)}) %collective-permute-start.28) | collective-permute-done | bytes 720928 | tf_op jit(solution)/shard_map/ppermute | solution.py:37
  126.5 6.1 %shard_map.167 = (f32[2,176,128]{2,1,0:T(8,128)S(1)}, f32[2,176,128]{2,1,0:T(8,128)S(1)}) custom-call(s32[38]{0:T(128)S(1)} %pad_add_fusion.meta, bf16[4,8,128,256]{3,2,1,0:T(8,128)(2,1)S(1)} %shard_map.162.tiles, f32[8,176,128]{2,1,0:T(8,128)S(1)} %pad_maximum_fusion.2.rest_0_, f32[8,176,128]{2,1,0:T(8,128)S(1)} %collective-permute-done.24.rest_1_, ...), custom_call_target="tpu_custom_call" | custom-call | bytes 12582912 | tf_op jit(solution)/shard_map/pallas_call | solution.py:260
  132.8 2.6 %collective-permute-start.42 = (f32[160,128]{1,0:T(8,128)S(1)}, f32[160,128]{1,0:T(8,128)S(1)}, u32[]{:S(2)}, u32[]{:S(2)}) collective-permute-start(f32[160,128]{1,0:T(8,128)S(1)} %add.120), channel_id=1, source_target_pairs={{0,48},{4,196},{8,56},{12,204},{16,0},{20,212},{24,8},{28,220},{32... | collective-permute-start | bytes 245768 | tf_op jit(solution)/shard_map/ppermute | solution.py:45
  135.4 2.7 %collective-permute-done.40 = f32[160,128]{1,0:T(8,128)S(1)} collective-permute-done((f32[160,128]{1,0:T(8,128)S(1)}, f32[160,128]{1,0:T(8,128)S(1)}, u32[]{:S(2)}, u32[]{:S(2)}) %collective-permute-start.40) | collective-permute-done | bytes 81952 | tf_op jit(solution)/shard_map/ppermute | solution.py:45
  138.1 0.9 collective-permute-done.42
  139.0 2.8 %collective-permute-done.37.got = f32[2,176,128]{2,1,0:T(8,128)S(1)} collective-permute-done((f32[2,176,128]{2,1,0:T(8,128)S(1)}, f32[2,176,128]{2,1,0:T(8,128)S(1)}, u32[]{:S(2)}, u32[]{:S(2)}) %collective-permute-start.37) | collective-permute-done | bytes 180256 | tf_op jit(solution)/shard_map/ppermute | solution.py:55
  142.1 1.2 collective-permute-start.45
  143.4 1.7 %collective-permute-done.43 = f32[160,128]{1,0:T(8,128)S(1)} collective-permute-done((f32[160,128]{1,0:T(8,128)S(1)}, f32[160,128]{1,0:T(8,128)S(1)}, u32[]{:S(2)}, u32[]{:S(2)}) %collective-permute-start.43) | collective-permute-done | bytes 81952 | tf_op jit(solution)/shard_map/ppermute | solution.py:45
  145.1 1.8 %collective-permute-done.44 = f32[160,128]{1,0:T(8,128)S(1)} collective-permute-done((f32[160,128]{1,0:T(8,128)S(1)}, f32[160,128]{1,0:T(8,128)S(1)}, u32[]{:S(2)}, u32[]{:S(2)}) %collective-permute-start.44) | collective-permute-done | bytes 81952 | tf_op jit(solution)/shard_map/ppermute | solution.py:45
  146.9 1.1 collective-permute-done.45
  148.1 1.1 collective-permute-done.38.last
  149.2 1.5 collective-permute-start.46
  150.7 0.7 shard_map.168
  151.4 0.6 collective-permute-done.46.qo
  152.0 1.4 shard_map.169
  (87 shorter events, 4.8 us)
Async XLA Ops:
  0.6 14.1 %collective-permute-start = (f32[128,128]{1,0:T(8,128)}, f32[128,128]{1,0:T(8,128)S(1)}, u32[]{:S(2)}, u32[]{:S(2)}) collective-permute-start(f32[128,128]{1,0:T(8,128)} %feat.3), channel_id=1, source_target_pairs={{0,8},{4,12},{8,0},{12,4},{16,24},{20,28},{24,16},{28,20},{32,40},... | collective-permute-start | bytes 196616 | tf_op jit(solution)/shard_map/ppermute | solution.py:41
  8.5 10.3 %collective-permute-start.8 = (f32[172,128]{1,0:T(8,128)}, f32[172,128]{1,0:T(8,128)S(1)}, u32[]{:S(2)}, u32[]{:S(2)}) collective-permute-start(f32[172,128]{1,0:T(8,128)} %bitcast.47), channel_id=1, source_target_pairs={{0,2},{1,3},{2,0},{3,1},{4,6},{5,7},{6,4},{7,5},{8,10},{9,11},{10,... | collective-permute-start | bytes 264200 | tf_op jit(solution)/shard_map/ppermute | solution.py:55
  12.3 1.6 %copy-start = (f32[4,1,8,128,128]{4,3,2,1,0:T(8,128)S(1)}, f32[4,1,8,128,128]{4,3,2,1,0:T(8,128)}, u32[]{:S(2)}) copy-start(f32[4,1,8,128,128]{4,3,2,1,0:T(8,128)} %tiles.1) | copy-start | bytes 6291460
  13.9 0.8 copy-start.2
  13.9 4.8 %copy-start.3 = (f32[128,172]{0,1:T(8,128)S(1)}, f32[128,172]{0,1:T(8,128)}, u32[]{:S(2)}) copy-start(f32[128,172]{0,1:T(8,128)} %param.21) | copy-start | bytes 264196
  14.8 6.1 %collective-permute-start.1 = (f32[2,128,128]{2,1,0:T(8,128)S(1)}, f32[2,128,128]{2,1,0:T(8,128)S(1)}, u32[]{:S(2)}, u32[]{:S(2)}) collective-permute-start(f32[2,128,128]{2,1,0:T(8,128)S(1)} %pad_maximum_fusion.7), channel_id=1, source_target_pairs={{0,192},{4,52},{8,200},{12,60},{16,208},{20,4},{24,216},{28,12},{3... | collective-permute-start | bytes 393224 | tf_op jit(solution)/shard_map/ppermute | solution.py:45
  17.6 5.5 %collective-permute-start.2 = (f32[2,128,128]{2,1,0:T(8,128)S(1)}, f32[2,128,128]{2,1,0:T(8,128)S(1)}, u32[]{:S(2)}, u32[]{:S(2)}) collective-permute-start(f32[2,128,128]{2,1,0:T(8,128)S(1)} %pad_maximum_fusion.7), channel_id=1, source_target_pairs={{0,128},{4,36},{8,136},{12,44},{16,144},{20,52},{24,152},{28,60},{... | collective-permute-start | bytes 393224 | tf_op jit(solution)/shard_map/ppermute | solution.py:45
  18.0 6.7 %collective-permute-start.3 = (f32[2,128,128]{2,1,0:T(8,128)S(1)}, f32[2,128,128]{2,1,0:T(8,128)S(1)}, u32[]{:S(2)}, u32[]{:S(2)}) collective-permute-start(f32[2,128,128]{2,1,0:T(8,128)S(1)} %pad_maximum_fusion.7), channel_id=1, source_target_pairs={{0,64},{4,20},{8,72},{12,28},{16,80},{20,36},{24,88},{28,44},{32,9... | collective-permute-start | bytes 393224 | tf_op jit(solution)/shard_map/ppermute | solution.py:45
  18.8 6.0 %collective-permute-start.9 = (f32[2,172,128]{2,1,0:T(8,128)S(1)}, f32[2,172,128]{2,1,0:T(8,128)S(1)}, u32[]{:S(2)}, u32[]{:S(2)}) collective-permute-start(f32[2,172,128]{2,1,0:T(8,128)S(1)} %pad_maximum_fusion.5.near), channel_id=1, source_target_pairs={{0,1},{1,0},{2,3},{3,2},{4,5},{5,4},{6,7},{7,6},{8,9},{9,8},{10,11... | collective-permute-start | bytes 528392 | tf_op jit(solution)/shard_map/ppermute | solution.py:55
  29.3 5.4 %collective-permute-start.10 = (f32[32,176,128]{2,1,0:T(8,128)S(1)}, f32[32,176,128]{2,1,0:T(8,128)S(1)}, u32[]{:S(2)}, u32[]{:S(2)}) collective-permute-start(f32[32,176,128]{2,1,0:T(8,128)S(1)} %get-tuple-element.39), channel_id=1, source_target_pairs={{0,4},{4,0},{8,12},{12,8},{16,20},{20,16},{24,28},{28,24},{32,36},... | collective-permute-start | bytes 8650760 | tf_op jit(solution)/shard_map/ppermute | solution.py:37
  29.4 8.4 %collective-permute-start.4 = (f32[8,128,128]{2,1,0:T(8,128)S(1)}, f32[8,128,128]{2,1,0:T(8,128)S(1)}, u32[]{:S(2)}, u32[]{:S(2)}) collective-permute-start(f32[8,128,128]{2,1,0:T(8,128)S(1)} %constant_dynamic-update-slice_fusion.rest_0_), channel_id=1, source_target_pairs={{0,48},{4,196},{8,56},{12,204},{16,0},{20,212},{24,8},{28,220},{32... | collective-permute-start | bytes 1572872 | tf_op jit(solution)/shard_map/ppermute | solution.py:45
  30.6 9.9 %collective-permute-start.5 = (f32[8,128,128]{2,1,0:T(8,128)S(1)}, f32[8,128,128]{2,1,0:T(8,128)S(1)}, u32[]{:S(2)}, u32[]{:S(2)}) collective-permute-start(f32[8,128,128]{2,1,0:T(8,128)S(1)} %constant_dynamic-update-slice_fusion.rest_0_), channel_id=1, source_target_pairs={{0,32},{4,132},{8,40},{12,140},{16,48},{20,148},{24,56},{28,156},{... | collective-permute-start | bytes 1572872 | tf_op jit(solution)/shard_map/ppermute | solution.py:45
  31.8 14.2 %collective-permute-start.6 = (f32[8,128,128]{2,1,0:T(8,128)S(1)}, f32[8,128,128]{2,1,0:T(8,128)S(1)}, u32[]{:S(2)}, u32[]{:S(2)}) collective-permute-start(f32[8,128,128]{2,1,0:T(8,128)S(1)} %constant_dynamic-update-slice_fusion.rest_0_), channel_id=1, source_target_pairs={{0,16},{4,68},{8,24},{12,76},{16,32},{20,84},{24,40},{28,92},{32,4... | collective-permute-start | bytes 1572872 | tf_op jit(solution)/shard_map/ppermute | solution.py:45
  46.2 20.5 %copy-start.1 = (f32[256,172]{0,1:T(8,128)S(1)}, f32[256,172]{0,1:T(8,128)}, u32[]{:S(2)}) copy-start(f32[256,172]{0,1:T(8,128)} %param.19) | copy-start | bytes 528388
  46.2 20.5 %copy-start.5 = (f32[128,256]{1,0:T(8,128)S(1)}, f32[128,256]{1,0:T(8,128)}, u32[]{:S(2)}) copy-start(f32[128,256]{1,0:T(8,128)} %self_one.1) | copy-start | bytes 393220
  46.2 20.5 %copy-start.6 = (f32[128,256]{1,0:T(8,128)S(1)}, f32[128,256]{1,0:T(8,128)}, u32[]{:S(2)}) copy-start(f32[128,256]{1,0:T(8,128)} %neigh_one.1) | copy-start | bytes 393220
  46.2 20.4 %copy-start.7 = (f32[256]{0:T(256)S(1)}, f32[256]{0:T(256)}, u32[]{:S(2)}) copy-start(f32[256]{0:T(256)} %param.17) | copy-start | bytes 3076
  46.2 7.5 %collective-permute-start.11 = (f32[24,128,128]{2,1,0:T(8,128)S(1)}, f32[24,128,128]{2,1,0:T(8,128)S(1)}, u32[]{:S(2)}, u32[]{:S(2)}) collective-permute-start(f32[24,128,128]{2,1,0:T(8,128)S(1)} %pad_maximum_fusion.1), channel_id=1, source_target_pairs={{0,4},{4,0},{8,12},{12,8},{16,20},{20,16},{24,28},{28,24},{32,36},... | collective-permute-start | bytes 4718600 | tf_op jit(solution)/shard_map/ppermute | solution.py:37
  48.6 5.2 %collective-permute-start.7 = (f32[8,128,128]{2,1,0:T(8,128)S(1)}, f32[8,128,128]{2,1,0:T(8,128)S(1)}, u32[]{:S(2)}, u32[]{:S(2)}) collective-permute-start(f32[8,128,128]{2,1,0:T(8,128)S(1)} %constant_dynamic-update-slice_fusion.rest_0_), channel_id=1, source_target_pairs={{0,4},{4,0},{8,12},{12,8},{16,20},{20,16},{24,28},{28,24},{32,36},... | collective-permute-start | bytes 1572872 | tf_op jit(solution)/shard_map/ppermute | solution.py:37
  48.7 18.7 %collective-permute-start.19 = (f32[8,176,128]{2,1,0:T(8,128)S(1)}, f32[8,176,128]{2,1,0:T(8,128)S(1)}, u32[]{:S(2)}, u32[]{:S(2)}) collective-permute-start(f32[8,176,128]{2,1,0:T(8,128)S(1)} %get-tuple-element.45), channel_id=1, source_target_pairs={{0,128},{4,36},{8,136},{12,44},{16,144},{20,52},{24,152},{28,60},{... | collective-permute-start | bytes 2162696 | tf_op jit(solution)/shard_map/ppermute | solution.py:45
  51.1 17.3 %collective-permute-start.18 = (f32[8,176,128]{2,1,0:T(8,128)S(1)}, f32[8,176,128]{2,1,0:T(8,128)S(1)}, u32[]{:S(2)}, u32[]{:S(2)}) collective-permute-start(f32[8,176,128]{2,1,0:T(8,128)S(1)} %get-tuple-element.67), channel_id=1, source_target_pairs={{0,64},{4,20},{8,72},{12,28},{16,80},{20,36},{24,88},{28,44},{32,9... | collective-permute-start | bytes 2162696 | tf_op jit(solution)/shard_map/ppermute | solution.py:45
  51.1 17.3 %collective-permute-start.20 = (f32[8,176,128]{2,1,0:T(8,128)S(1)}, f32[8,176,128]{2,1,0:T(8,128)S(1)}, u32[]{:S(2)}, u32[]{:S(2)}) collective-permute-start(f32[8,176,128]{2,1,0:T(8,128)S(1)} %get-tuple-element.65), channel_id=1, source_target_pairs={{0,192},{4,52},{8,200},{12,60},{16,208},{20,4},{24,216},{28,12},{3... | collective-permute-start | bytes 2162696 | tf_op jit(solution)/shard_map/ppermute | solution.py:45
  57.9 4.4 %collective-permute-start.12 = (f32[2,128,128]{2,1,0:T(8,128)S(1)}, f32[2,128,128]{2,1,0:T(8,128)S(1)}, u32[]{:S(2)}, u32[]{:S(2)}) collective-permute-start(f32[2,128,128]{2,1,0:T(8,128)S(1)} %get-tuple-element.42), channel_id=1, source_target_pairs={{0,1},{1,0},{2,3},{3,2},{4,5},{5,4},{6,7},{7,6},{8,9},{9,8},{10,11... | collective-permute-start | bytes 393224 | tf_op jit(solution)/shard_map/ppermute | solution.py:55
  62.2 4.4 %collective-permute-start.13 = (f32[128,128]{1,0:T(8,128)S(1)}, f32[128,128]{1,0:T(8,128)S(1)}, u32[]{:S(2)}, u32[]{:S(2)}) collective-permute-start(f32[128,128]{1,0:T(8,128)S(1)} %fusion.8), channel_id=1, source_target_pairs={{0,2},{1,3},{2,0},{3,1},{4,6},{5,7},{6,4},{7,5},{8,10},{9,11},{10,... | collective-permute-start | bytes 196616 | tf_op jit(solution)/shard_map/ppermute | solution.py:55
  67.2 7.8 %collective-permute-start.14 = (f32[176,128]{1,0:T(8,128)S(1)}, f32[176,128]{1,0:T(8,128)S(1)}, u32[]{:S(2)}, u32[]{:S(2)}) collective-permute-start(f32[176,128]{1,0:T(8,128)S(1)} %get-tuple-element.43), channel_id=1, source_target_pairs={{0,8},{4,12},{8,0},{12,4},{16,24},{20,28},{24,16},{28,20},{32,40},... | collective-permute-start | bytes 270344 | tf_op jit(solution)/shard_map/ppermute | solution.py:41
  68.5 19.8 %copy-start.4 = (f32[256,172]{0,1:T(8,128)S(1)}, f32[256,172]{0,1:T(8,128)}, u32[]{:S(2)}) copy-start(f32[256,172]{0,1:T(8,128)} %param.18) | copy-start | bytes 528388
  68.5 19.8 %copy-start.8 = (f32[172]{0:T(256)S(1)}, f32[172]{0:T(256)}, u32[]{:S(2)}) copy-start(f32[172]{0:T(256)} %param.20) | copy-start | bytes 2068
  68.6 7.3 %collective-permute-start.21 = (f32[2,176,128]{2,1,0:T(8,128)S(1)}, f32[2,176,128]{2,1,0:T(8,128)S(1)}, u32[]{:S(2)}, u32[]{:S(2)}) collective-permute-start(f32[2,176,128]{2,1,0:T(8,128)S(1)} %get-tuple-element.71), channel_id=1, source_target_pairs={{0,16},{4,68},{8,24},{12,76},{16,32},{20,84},{24,40},{28,92},{32,4... | collective-permute-start | bytes 540680 | tf_op jit(solution)/shard_map/ppermute | solution.py:45
  71.8 5.8 %collective-permute-start.22 = (f32[2,176,128]{2,1,0:T(8,128)S(1)}, f32[2,176,128]{2,1,0:T(8,128)S(1)}, u32[]{:S(2)}, u32[]{:S(2)}) collective-permute-start(f32[2,176,128]{2,1,0:T(8,128)S(1)} %get-tuple-element.70), channel_id=1, source_target_pairs={{0,32},{4,132},{8,40},{12,140},{16,48},{20,148},{24,56},{28,156},{... | collective-permute-start | bytes 540680 | tf_op jit(solution)/shard_map/ppermute | solution.py:45
  71.8 5.8 %collective-permute-start.23 = (f32[2,176,128]{2,1,0:T(8,128)S(1)}, f32[2,176,128]{2,1,0:T(8,128)S(1)}, u32[]{:S(2)}, u32[]{:S(2)}) collective-permute-start(f32[2,176,128]{2,1,0:T(8,128)S(1)} %get-tuple-element.69), channel_id=1, source_target_pairs={{0,48},{4,196},{8,56},{12,204},{16,0},{20,212},{24,8},{28,220},{32... | collective-permute-start | bytes 540680 | tf_op jit(solution)/shard_map/ppermute | solution.py:45
  75.1 6.5 %collective-permute-start.15 = (f32[2,176,128]{2,1,0:T(8,128)S(1)}, f32[2,176,128]{2,1,0:T(8,128)S(1)}, u32[]{:S(2)}, u32[]{:S(2)}) collective-permute-start(f32[2,176,128]{2,1,0:T(8,128)S(1)} %pad_maximum_fusion.6), channel_id=1, source_target_pairs={{0,192},{4,52},{8,200},{12,60},{16,208},{20,4},{24,216},{28,12},{3... | collective-permute-start | bytes 540680 | tf_op jit(solution)/shard_map/ppermute | solution.py:45
  75.2 8.0 %collective-permute-start.16 = (f32[2,176,128]{2,1,0:T(8,128)S(1)}, f32[2,176,128]{2,1,0:T(8,128)S(1)}, u32[]{:S(2)}, u32[]{:S(2)}) collective-permute-start(f32[2,176,128]{2,1,0:T(8,128)S(1)} %pad_maximum_fusion.6), channel_id=1, source_target_pairs={{0,128},{4,36},{8,136},{12,44},{16,144},{20,52},{24,152},{28,60},{... | collective-permute-start | bytes 540680 | tf_op jit(solution)/shard_map/ppermute | solution.py:45
  75.9 10.8 %collective-permute-start.17 = (f32[2,176,128]{2,1,0:T(8,128)S(1)}, f32[2,176,128]{2,1,0:T(8,128)S(1)}, u32[]{:S(2)}, u32[]{:S(2)}) collective-permute-start(f32[2,176,128]{2,1,0:T(8,128)S(1)} %pad_maximum_fusion.6), channel_id=1, source_target_pairs={{0,64},{4,20},{8,72},{12,28},{16,80},{20,36},{24,88},{28,44},{32,9... | collective-permute-start | bytes 540680 | tf_op jit(solution)/shard_map/ppermute | solution.py:45
  77.7 10.6 %collective-permute-start.29 = (f32[176,128]{1,0:T(8,128)S(1)}, f32[176,128]{1,0:T(8,128)S(1)}, u32[]{:S(2)}, u32[]{:S(2)}) collective-permute-start(f32[176,128]{1,0:T(8,128)S(1)} %get-tuple-element.75), channel_id=1, source_target_pairs={{0,8},{4,12},{8,0},{12,4},{16,24},{20,28},{24,16},{28,20},{32,40},... | collective-permute-start | bytes 270344 | tf_op jit(solution)/shard_map/ppermute | solution.py:41
  86.8 16.8 %collective-permute-start.24 = (f32[8,176,128]{2,1,0:T(8,128)S(1)}, f32[8,176,128]{2,1,0:T(8,128)S(1)}, u32[]{:S(2)}, u32[]{:S(2)}) collective-permute-start(f32[8,176,128]{2,1,0:T(8,128)S(1)} %pad_maximum_fusion.2.rest_0_), channel_id=1, source_target_pairs={{0,48},{4,196},{8,56},{12,204},{16,0},{20,212},{24,8},{28,220},{32... | collective-permute-start | bytes 2162696 | tf_op jit(solution)/shard_map/ppermute | solution.py:45
  86.9 17.8 %collective-permute-start.26 = (f32[8,176,128]{2,1,0:T(8,128)S(1)}, f32[8,176,128]{2,1,0:T(8,128)S(1)}, u32[]{:S(2)}, u32[]{:S(2)}) collective-permute-start(f32[8,176,128]{2,1,0:T(8,128)S(1)} %pad_maximum_fusion.2.rest_0_), channel_id=1, source_target_pairs={{0,16},{4,68},{8,24},{12,76},{16,32},{20,84},{24,40},{28,92},{32,4... | collective-permute-start | bytes 2162696 | tf_op jit(solution)/shard_map/ppermute | solution.py:45
  89.9 10.9 %collective-permute-start.30 = (f32[4,160,128]{2,1,0:T(8,128)S(1)}, f32[4,160,128]{2,1,0:T(8,128)S(1)}, u32[]{:S(2)}, u32[]{:S(2)}) collective-permute-start(f32[4,160,128]{2,1,0:T(8,128)S(1)} %get-tuple-element.51), channel_id=1, source_target_pairs={{0,4},{4,0},{8,12},{12,8},{16,20},{20,16},{24,28},{28,24},{32,36},... | collective-permute-start | bytes 983048 | tf_op jit(solution)/shard_map/ppermute | solution.py:37
  100.8 6.7 %collective-permute-start.31 = (f32[160,128]{1,0:T(8,128)S(1)}, f32[160,128]{1,0:T(8,128)S(1)}, u32[]{:S(2)}, u32[]{:S(2)}) collective-permute-start(f32[160,128]{1,0:T(8,128)S(1)} %get-tuple-element.74), channel_id=1, source_target_pairs={{0,64},{4,20},{8,72},{12,28},{16,80},{20,36},{24,88},{28,44},{32,9... | collective-permute-start | bytes 245768 | tf_op jit(solution)/shard_map/ppermute | solution.py:45
  100.9 6.6 %collective-permute-start.32 = (f32[160,128]{1,0:T(8,128)S(1)}, f32[160,128]{1,0:T(8,128)S(1)}, u32[]{:S(2)}, u32[]{:S(2)}) collective-permute-start(f32[160,128]{1,0:T(8,128)S(1)} %get-tuple-element.73), channel_id=1, source_target_pairs={{0,128},{4,36},{8,136},{12,44},{16,144},{20,52},{24,152},{28,60},{... | collective-permute-start | bytes 245768 | tf_op jit(solution)/shard_map/ppermute | solution.py:45
  103.1 5.4 %collective-permute-start.33 = (f32[160,128]{1,0:T(8,128)S(1)}, f32[160,128]{1,0:T(8,128)S(1)}, u32[]{:S(2)}, u32[]{:S(2)}) collective-permute-start(f32[160,128]{1,0:T(8,128)S(1)} %get-tuple-element.72), channel_id=1, source_target_pairs={{0,192},{4,52},{8,200},{12,60},{16,208},{20,4},{24,216},{28,12},{3... | collective-permute-start | bytes 245768 | tf_op jit(solution)/shard_map/ppermute | solution.py:45
  103.6 13.8 %collective-permute-start.25 = (f32[4,176,128]{2,1,0:T(8,128)S(1)}, f32[4,176,128]{2,1,0:T(8,128)S(1)}, u32[]{:S(2)}, u32[]{:S(2)}) collective-permute-start(f32[4,176,128]{2,1,0:T(8,128)S(1)} %slice.121), channel_id=1, source_target_pairs={{0,48},{4,196},{8,56},{12,204},{16,0},{20,212},{24,8},{28,220},{32... | collective-permute-start | bytes 1081352 | tf_op jit(solution)/shard_map/ppermute | solution.py:45
  104.7 12.7 %collective-permute-start.27 = (f32[4,176,128]{2,1,0:T(8,128)S(1)}, f32[4,176,128]{2,1,0:T(8,128)S(1)}, u32[]{:S(2)}, u32[]{:S(2)}) collective-permute-start(f32[4,176,128]{2,1,0:T(8,128)S(1)} %slice.122), channel_id=1, source_target_pairs={{0,16},{4,68},{8,24},{12,76},{16,32},{20,84},{24,40},{28,92},{32,4... | collective-permute-start | bytes 1081352 | tf_op jit(solution)/shard_map/ppermute | solution.py:45
  108.5 3.7 %collective-permute-start.34 = (f32[160,128]{1,0:T(8,128)S(1)}, f32[160,128]{1,0:T(8,128)S(1)}, u32[]{:S(2)}, u32[]{:S(2)}) collective-permute-start(f32[160,128]{1,0:T(8,128)S(1)} %fusion.7), channel_id=1, source_target_pairs={{0,1},{1,0},{2,3},{3,2},{4,5},{5,4},{6,7},{7,6},{8,9},{9,8},{10,11... | collective-permute-start | bytes 245768 | tf_op jit(solution)/shard_map/ppermute | solution.py:55
  112.2 5.2 %collective-permute-start.35 = (f32[160,128]{1,0:T(8,128)S(1)}, f32[160,128]{1,0:T(8,128)S(1)}, u32[]{:S(2)}, u32[]{:S(2)}) collective-permute-start(f32[160,128]{1,0:T(8,128)S(1)} %add.116), channel_id=1, source_target_pairs={{0,2},{1,3},{2,0},{3,1},{4,6},{5,7},{6,4},{7,5},{8,10},{9,11},{10,... | collective-permute-start | bytes 245768 | tf_op jit(solution)/shard_map/ppermute | solution.py:55
  117.5 9.0 %collective-permute-start.36 = (f32[24,176,128]{2,1,0:T(8,128)S(1)}, f32[24,176,128]{2,1,0:T(8,128)S(1)}, u32[]{:S(2)}, u32[]{:S(2)}) collective-permute-start(f32[24,176,128]{2,1,0:T(8,128)S(1)} %pad_maximum_fusion), channel_id=1, source_target_pairs={{0,4},{4,0},{8,12},{12,8},{16,20},{20,16},{24,28},{28,24},{32,36},... | collective-permute-start | bytes 6488072 | tf_op jit(solution)/shard_map/ppermute | solution.py:37
  121.6 4.9 %collective-permute-start.28 = (f32[8,176,128]{2,1,0:T(8,128)S(1)}, f32[8,176,128]{2,1,0:T(8,128)S(1)}, u32[]{:S(2)}, u32[]{:S(2)}) collective-permute-start(f32[8,176,128]{2,1,0:T(8,128)S(1)} %pad_maximum_fusion.2.rest_0_), channel_id=1, source_target_pairs={{0,4},{4,0},{8,12},{12,8},{16,20},{20,16},{24,28},{28,24},{32,36},... | collective-permute-start | bytes 2162696 | tf_op jit(solution)/shard_map/ppermute | solution.py:37
  121.7 10.9 %collective-permute-start.39 = (f32[160,128]{1,0:T(8,128)S(1)}, f32[160,128]{1,0:T(8,128)S(1)}, u32[]{:S(2)}, u32[]{:S(2)}) collective-permute-start(f32[160,128]{1,0:T(8,128)S(1)} %add.117), channel_id=1, source_target_pairs={{0,8},{4,12},{8,0},{12,4},{16,24},{20,28},{24,16},{28,20},{32,40},... | collective-permute-start | bytes 245768 | tf_op jit(solution)/shard_map/ppermute | solution.py:41
  132.6 5.5 %collective-permute-start.40 = (f32[160,128]{1,0:T(8,128)S(1)}, f32[160,128]{1,0:T(8,128)S(1)}, u32[]{:S(2)}, u32[]{:S(2)}) collective-permute-start(f32[160,128]{1,0:T(8,128)S(1)} %add.120), channel_id=1, source_target_pairs={{0,16},{4,68},{8,24},{12,76},{16,32},{20,84},{24,40},{28,92},{32,4... | collective-permute-start | bytes 245768 | tf_op jit(solution)/shard_map/ppermute | solution.py:45
  132.7 5.4 %collective-permute-start.41 = (f32[160,128]{1,0:T(8,128)S(1)}, f32[160,128]{1,0:T(8,128)S(1)}, u32[]{:S(2)}, u32[]{:S(2)}) collective-permute-start(f32[160,128]{1,0:T(8,128)S(1)} %add.120), channel_id=1, source_target_pairs={{0,32},{4,132},{8,40},{12,140},{16,48},{20,148},{24,56},{28,156},{... | collective-permute-start | bytes 245768 | tf_op jit(solution)/shard_map/ppermute | solution.py:45
  132.8 6.1 %collective-permute-start.42 = (f32[160,128]{1,0:T(8,128)S(1)}, f32[160,128]{1,0:T(8,128)S(1)}, u32[]{:S(2)}, u32[]{:S(2)}) collective-permute-start(f32[160,128]{1,0:T(8,128)S(1)} %add.120), channel_id=1, source_target_pairs={{0,48},{4,196},{8,56},{12,204},{16,0},{20,212},{24,8},{28,220},{32... | collective-permute-start | bytes 245768 | tf_op jit(solution)/shard_map/ppermute | solution.py:45
  135.4 6.4 %collective-permute-start.37 = (f32[2,176,128]{2,1,0:T(8,128)S(1)}, f32[2,176,128]{2,1,0:T(8,128)S(1)}, u32[]{:S(2)}, u32[]{:S(2)}) collective-permute-start(f32[2,176,128]{2,1,0:T(8,128)S(1)} %get-tuple-element.54), channel_id=1, source_target_pairs={{0,1},{1,0},{2,3},{3,2},{4,5},{5,4},{6,7},{7,6},{8,9},{9,8},{10,11... | collective-permute-start | bytes 540680 | tf_op jit(solution)/shard_map/ppermute | solution.py:55
  141.8 3.3 %collective-permute-start.43 = (f32[160,128]{1,0:T(8,128)S(1)}, f32[160,128]{1,0:T(8,128)S(1)}, u32[]{:S(2)}, u32[]{:S(2)}) collective-permute-start(f32[160,128]{1,0:T(8,128)S(1)} %add_add_fusion.1), channel_id=1, source_target_pairs={{0,192},{4,52},{8,200},{12,60},{16,208},{20,4},{24,216},{28,12},{3... | collective-permute-start | bytes 245768 | tf_op jit(solution)/shard_map/ppermute | solution.py:45
  142.1 4.8 %collective-permute-start.44 = (f32[160,128]{1,0:T(8,128)S(1)}, f32[160,128]{1,0:T(8,128)S(1)}, u32[]{:S(2)}, u32[]{:S(2)}) collective-permute-start(f32[160,128]{1,0:T(8,128)S(1)} %add_add_fusion.1), channel_id=1, source_target_pairs={{0,128},{4,36},{8,136},{12,44},{16,144},{20,52},{24,152},{28,60},{... | collective-permute-start | bytes 245768 | tf_op jit(solution)/shard_map/ppermute | solution.py:45
  142.1 6.0 %collective-permute-start.45 = (f32[160,128]{1,0:T(8,128)S(1)}, f32[160,128]{1,0:T(8,128)S(1)}, u32[]{:S(2)}, u32[]{:S(2)}) collective-permute-start(f32[160,128]{1,0:T(8,128)S(1)} %add_add_fusion.1), channel_id=1, source_target_pairs={{0,64},{4,20},{8,72},{12,28},{16,80},{20,36},{24,88},{28,44},{32,9... | collective-permute-start | bytes 245768 | tf_op jit(solution)/shard_map/ppermute | solution.py:45
  143.3 5.9 %collective-permute-start.38 = (f32[176,128]{1,0:T(8,128)S(1)}, f32[176,128]{1,0:T(8,128)S(1)}, u32[]{:S(2)}, u32[]{:S(2)}) collective-permute-start(f32[176,128]{1,0:T(8,128)S(1)} %fusion.1), channel_id=1, source_target_pairs={{0,2},{1,3},{2,0},{3,1},{4,6},{5,7},{6,4},{7,5},{8,10},{9,11},{10,... | collective-permute-start | bytes 270344 | tf_op jit(solution)/shard_map/ppermute | solution.py:55
  149.2 2.8 %collective-permute-start.46 = (f32[4,160,128]{2,1,0:T(8,128)S(1)}, f32[4,160,128]{2,1,0:T(8,128)S(1)}, u32[]{:S(2)}, u32[]{:S(2)}) collective-permute-start(f32[4,160,128]{2,1,0:T(8,128)S(1)} %pad_maximum_fusion.4.q), channel_id=1, source_target_pairs={{0,4},{4,0},{8,12},{12,8},{16,20},{20,16},{24,28},{28,24},{32,36},... | collective-permute-start | bytes 983048 | tf_op jit(solution)/shard_map/ppermute | solution.py:37
